TPU v7x, 256 devices: a whole 4x4x8 slice. The times are simulated.
256 devices in a mesh: slab: 32 (over z, y_lo, core), sub: 8 (over x, y_hi).
Axes of the slice: x: 4, y: 4 (y_hi: 2, y_lo: 2; y = y_hi * 2 + y_lo), z: 8, core: 2. Of those that a mesh axis runs over, the one named last changes fastest.
Arguments:
- features: bfloat16 [262144, 128], P(('slab', 'sub')), may hold values from -6 to 6
- positions: float32 [3, 262144], P(None, ('slab', 'sub')), may hold values from 0 to 1, as said below
- atom_count: int32 [256], P(('slab', 'sub')), may hold values from 512 to 1024, as said below
- kgrid: int32 [3, 2048], replicated, may hold values from -6 to 6
- k_filter: float32 [2048, 128], replicated, may hold values from 0.1 to 1
- w_mix: float32 [128, 128], replicated, may hold values from -0.5 to 0.5
- w_recv: bfloat16 [128, 128], replicated, may hold values from -0.5 to 0.5
- w_send: bfloat16 [128, 128], replicated, may hold values from -0.5 to 0.5
- w_basis: bfloat16 [8, 128], replicated, may hold values from -2 to 2
- w_out: bfloat16 [128, 128], replicated, may hold values from -0.5 to 0.5
- edge_basis: bfloat16 [8, 8388608], P(None, ('slab', 'sub')), may hold values from -1 to 1
- senders: int32 [8388608], P(('slab', 'sub')), may hold values from 0 to 9215, as said below
Outputs:
- updated: float32 [262144, 128], P(('slab', 'sub'))
Inputs may be any that keep to these rules, and one draw needn't show every extreme that they name: `atom_count`: one block has exactly 1024 live atoms; live atoms of a block are its first rows. senders[e] = (3 a + c) * 1024 + j with a, c in 0..2 and j below the atom_count of the block it names. Each atom of block (s, b) has positions[0] in [b / 8, (b + 1) / 8), positions[2] in [s / 32, (s + 1) / 32), positions[1] in [0, 1).
All inputs are finite; a program needn't handle non-finite values.
Results may differ from a plain program's by a relative error of at most 0.0021.
Values may be sent and summed in bfloat16 or wider, within the bound.
No kernel may reach another device: no remote copies, remote signals or barrier semaphores. Data moves between devices by JAX's collectives and lax.ppermute only.
A program may use at most 128 MiB of HBM per device.

v0:
```python
import math

import jax
import jax.numpy as jnp
from jax import lax
from jax.sharding import PartitionSpec as P


def extended(cells, sides, width):
    for axis, dim in sides:
        count = lax.axis_size(axis)
        head = lax.slice_in_dim(cells, 0, width, axis=dim)
        tail = lax.slice_in_dim(cells, cells.shape[dim] - width, cells.shape[dim], axis=dim)
        cells = jnp.concatenate(
            [
                lax.ppermute(tail, axis, [(i, (i + 1) % count) for i in range(count)]),
                cells,
                lax.ppermute(head, axis, [((i + 1) % count, i) for i in range(count)]),
            ],
            axis=dim,
        )
    return cells


def phase_tables(k_rows, coords):
    wave = k_rows.astype(jnp.float32)
    phase = (
        wave[0][:, None] * coords[0][None, :]
        + wave[1][:, None] * coords[1][None, :]
        + wave[2][:, None] * coords[2][None, :]
    ) * (2.0 * math.pi)
    return (jnp.cos(phase).astype(jnp.bfloat16), jnp.sin(phase).astype(jnp.bfloat16))


def whole_tables(kgrid, coords):
    k_count = kgrid.shape[1]
    k_step = 512
    blocks = kgrid.reshape(3, k_count // k_step, k_step).transpose(1, 0, 2)
    cos_parts, sin_parts = lax.map(lambda wave: phase_tables(wave, coords), blocks)
    atom_rows = coords.shape[1]
    return (cos_parts.reshape(k_count, atom_rows), sin_parts.reshape(k_count, atom_rows))


def filter_rows(factor_sums, k_filter, w_mix, norm_factor):
    channels = k_filter.shape[1]
    real_part = jnp.dot(
        factor_sums[:, :channels] * norm_factor * k_filter,
        w_mix,
        precision=lax.Precision.HIGHEST,
        preferred_element_type=jnp.float32,
    )
    imag_part = jnp.dot(
        factor_sums[:, channels:] * norm_factor * k_filter,
        w_mix,
        precision=lax.Precision.HIGHEST,
        preferred_element_type=jnp.float32,
    )
    return jnp.concatenate([real_part, imag_part], axis=1).astype(jnp.bfloat16)


def edge_messages(recv_proj, sender_pool, senders, edge_basis, w_basis, w_out, degree):
    atom_rows = recv_proj.shape[0]
    channels = recv_proj.shape[1]
    gathered = (
        jnp.take(sender_pool, senders, axis=0)
        .astype(jnp.float32)
        .reshape(atom_rows, degree, channels)
    )
    radial = lax.dot_general(
        edge_basis, w_basis, (((0,), (0,)), ((), ())), preferred_element_type=jnp.float32
    ).reshape(atom_rows, degree, channels)
    hidden = jax.nn.silu(recv_proj[:, None, :] + gathered + radial).astype(jnp.bfloat16)
    message = jnp.dot(
        hidden.reshape(atom_rows * degree, channels), w_out, preferred_element_type=jnp.float32
    )
    return jnp.sum(message.reshape(atom_rows, degree, channels), axis=1) * (1.0 / math.sqrt(degree))


def per_device(
    features,
    positions,
    atom_count,
    kgrid,
    k_filter,
    w_mix,
    w_recv,
    w_send,
    w_basis,
    w_out,
    edge_basis,
    senders,
):
    atom_rows, channels = features.shape
    degree = senders.shape[0] // atom_rows
    total_k = kgrid.shape[1]
    devices = lax.axis_size(("slab", "sub"))
    norm_factor = 1.0 / math.sqrt(atom_rows * devices)
    live_mask = (jnp.arange(atom_rows, dtype=jnp.int32) < atom_count[0]).astype(jnp.float32)
    masked = (features.astype(jnp.float32) * live_mask[:, None]).astype(jnp.bfloat16)
    ghost_grid = extended(
        features.reshape(1, 1, atom_rows * channels), (("slab", 0), ("sub", 1)), 1
    )
    sender_pool = jnp.dot(
        ghost_grid.reshape(9 * atom_rows, channels), w_send, preferred_element_type=jnp.float32
    ).astype(jnp.bfloat16)
    cos_table, sin_table = whole_tables(kgrid, positions)
    k_share = total_k // devices
    cos_rows = cos_table
    sin_rows = sin_table
    owned = lax.psum_scatter(
        jnp.concatenate(
            [
                jnp.dot(cos_rows, masked, preferred_element_type=jnp.float32),
                jnp.dot(sin_rows, masked, preferred_element_type=jnp.float32),
            ],
            axis=1,
        ),
        ("slab", "sub"),
        scatter_dimension=0,
        tiled=True,
    )
    k_first = lax.axis_index(("slab", "sub")) * k_share
    filtered = filter_rows(
        owned, lax.dynamic_slice_in_dim(k_filter, k_first, k_share, 0), w_mix, norm_factor
    )
    block_rows = lax.all_gather(filtered, ("slab", "sub"), axis=0, tiled=True)
    cos_rows = cos_table
    sin_rows = sin_table
    contract = (((0,), (0,)), ((), ()))
    first_term = lax.dot_general(
        cos_rows, block_rows[:, :channels], contract, preferred_element_type=jnp.float32
    )
    second_term = lax.dot_general(
        sin_rows, block_rows[:, channels:], contract, preferred_element_type=jnp.float32
    )
    long_range = first_term + second_term
    recv_proj = jnp.dot(features, w_recv, preferred_element_type=jnp.float32)
    aggregate = edge_messages(recv_proj, sender_pool, senders, edge_basis, w_basis, w_out, degree)
    return live_mask[:, None] * (aggregate + long_range * (4.0 / math.sqrt(total_k)))


def solution(mesh):
    placed = (
        P(("slab", "sub"), None),
        P(None, ("slab", "sub")),
        P(("slab", "sub")),
        P(),
        P(),
        P(),
        P(),
        P(),
        P(),
        P(),
        P(None, ("slab", "sub")),
        P(("slab", "sub")),
    )
    return jax.shard_map(
        per_device, mesh=mesh, in_specs=placed, out_specs=P(("slab", "sub"), None), check_vma=False
    )
```

profile of v0, /device:TPU:1, one launch (start us, length us, event | category | flops | bytes accessed | tf_op | source)
XLA Modules:
  0.0 1897.7 jit_solution(1368881749157710960)
XLA Ops:
  6.5 1.9 reshape.367
  8.5 3.2 collective-permute-start.1
  12.4 44.7 %while.12 = (s32[]{:T(128)}, bf16[4,512,1024]{2,1,0:T(8,128)(2,1)}, bf16[4,512,1024]{2,1,0:T(8,128)(2,1)}, s32[4,3,512]{2,1,0:T(4,128)}, f32[3,1024]{1,0:T(4,128)}, /*index=5*/s32[]{:T(128)}) while((s32[]{:T(128)}, bf16[4,512,1024]{2,1,0:T(8,128)(2,1)}, bf16[4,512,1024]{2,1,0:T(8,128)(2,1)}, s32[4,3,512]{2,1,0:T(4,128)}, f32[3,1024]{1,0:T(4,128)}, ...), condition=%wide.region_2.3_spmd, body=%wide.region_1.2_spmd.sunk | while | flops 4195842 | bytes 2164821 | solution.py:39
  14.0 9.6 fusion.47
  25.2 9.6 fusion.47
  36.3 9.6 fusion.47
  47.5 9.6 fusion.47
  57.1 3.9 fusion.15
  66.7 3.2 pad_maximum_fusion.2
  69.9 4.5 collective-permute-start.3
  74.5 40.2 %collective-permute-done.3 = bf16[3,1,131072]{2,0,1:T(4,128)(2,1)S(1)} collective-permute-done((bf16[3,1,131072]{2,0,1:T(4,128)(2,1)S(1)}, bf16[3,1,131072]{2,0,1:T(4,128)(2,1)S(1)}, u32[]{:S(2)}, u32[]{:S(2)}) %collective-permute-start.3) | collective-permute-done | bytes 786464 | tf_op jit(solution)/shard_map/ppermute | solution.py:18
  114.6 4.5 collective-permute-done.2
  119.1 4.1 pad_maximum_fusion
  123.3 4.1 copy.17
  127.3 5.8 reshape.368
  133.1 2.4 convolution_convert_fusion
  135.5 114.2 %gather_fusion = bf16[32768,128]{1,0:T(8,128)(2,1)} fusion(bf16[9216,128]{1,0:T(8,128)(2,1)S(1)} %convolution_convert_fusion, s32[32768]{0:T(1024)S(1)} %fusion.13), kind=kCustom, calls=%fused_computation | custom fusion | bytes 16908288 | tf_op jit(solution)/shard_map/jit(_take)/gather | solution.py:65
  249.7 9.1 bitcast_add_fusion
  258.8 1086.7 %reduce-scatter.4.cloned.1.call-done = f32[8,256]{1,0:T(8,128)} async-done(((f32[2048,256]{1,0:T(8,128)}), f32[8,256]{1,0:T(8,128)}) %reduce-scatter.4.cloned.1.call-update) | async-done | bytes 8208
  1347.5 8.7 multiply_convert_fusion
  1356.3 5.1 fusion.4
  1361.5 523.3 %all-gather.2.cloned.1.call-done = bf16[2048,256]{1,0:T(8,128)(2,1)} async-done(((bf16[8,256]{1,0:T(8,128)(2,1)}), bf16[2048,256]{1,0:T(8,128)(2,1)}) %all-gather.2.cloned.1.call-update) | async-done | bytes 1048592 | tf_op jit(solution)/shard_map/all_gather | solution.py:126
  1884.8 3.7 fusion.11
  1888.7 2.2 fusion.9
  (61 shorter events, 14.1 us)
Async XLA Ops:
  6.5 59.1 %copy-start = (f32[2048,128]{1,0:T(8,128)S(1)}, f32[2048,128]{1,0:T(8,128)}, u32[]{:S(2)}) copy-start(f32[2048,128]{1,0:T(8,128)} %param.18) | copy-start | bytes 3145732
  6.5 1338.9 %reduce-scatter.4.cloned.1.call-start = ((), (), s32[]{:S(2)}) async-start(), calls=%async_computation.2 | async-start | bytes 2105344
  8.5 58.2 %collective-permute-start.1 = (bf16[1,1,131072]{2,0,1:T(2,128)(2,1)}, bf16[1,1,131072]{2,0,1:T(2,128)(2,1)}, u32[]{:S(2)}, u32[]{:S(2)}) collective-permute-start(bf16[1,1,131072]{2,0,1:T(2,128)(2,1)} %reshape.367), channel_id=1, source_target_pairs={{8,0},{16,8},{24,16},{32,24},{40,32},{48,40},{56,48},{64,56},{72,6... | collective-permute-start | bytes 786440 | tf_op jit(solution)/shard_map/ppermute | solution.py:18
  11.7 55.0 %collective-permute-start = (bf16[1,1,131072]{2,0,1:T(2,128)(2,1)}, bf16[1,1,131072]{2,0,1:T(2,128)(2,1)}, u32[]{:S(2)}, u32[]{:S(2)}) collective-permute-start(bf16[1,1,131072]{2,0,1:T(2,128)(2,1)} %reshape.367), channel_id=1, source_target_pairs={{0,8},{8,16},{16,24},{24,32},{32,40},{40,48},{48,56},{56,64},{64,7... | collective-permute-start | bytes 786440 | tf_op jit(solution)/shard_map/ppermute | solution.py:16
  12.4 44.7 %copy-start.4 = (bf16[1024,128]{1,0:T(8,128)(2,1)S(1)}, bf16[1024,128]{1,0:T(8,128)(2,1)}, u32[]{:S(2)}) copy-start(bf16[1024,128]{1,0:T(8,128)(2,1)} %param.14) | copy-start | bytes 786436
  57.1 3.9 copy-start.2
  64.6 9.8 copy-start.5
  64.6 1820.2 %all-gather.2.cloned.1.call-start = ((), (), s32[]{:S(2)}) async-start(), calls=%async_computation.1 | async-start | bytes 1052672 | tf_op jit(solution)/shard_map/all_gather | solution.py:126
  69.9 44.7 %collective-permute-start.3 = (bf16[3,1,131072]{2,0,1:T(4,128)(2,1)S(1)}, bf16[3,1,131072]{2,0,1:T(4,128)(2,1)S(1)}, u32[]{:S(2)}, u32[]{:S(2)}) collective-permute-start(bf16[3,1,131072]{2,0,1:T(4,128)(2,1)S(1)} %pad_maximum_fusion.2), channel_id=1, source_target_pairs={{1,0},{2,1},{3,2},{4,3},{5,4},{6,5},{7,6},{0,7},{9,8},{10,9},{11,1... | collective-permute-start | bytes 2359304 | tf_op jit(solution)/shard_map/ppermute | solution.py:18
  74.4 44.7 %collective-permute-start.2 = (bf16[3,1,131072]{2,0,1:T(4,128)(2,1)S(1)}, bf16[3,1,131072]{2,0,1:T(4,128)(2,1)S(1)}, u32[]{:S(2)}, u32[]{:S(2)}) collective-permute-start(bf16[3,1,131072]{2,0,1:T(4,128)(2,1)S(1)} %pad_maximum_fusion.2), channel_id=1, source_target_pairs={{0,1},{1,2},{2,3},{3,4},{4,5},{5,6},{6,7},{7,0},{8,9},{9,10},{10,1... | collective-permute-start | bytes 2359304 | tf_op jit(solution)/shard_map/ppermute | solution.py:16
  127.3 5.8 copy-start.8
  249.7 1096.7 %copy-start.7 = (f32[128,128]{1,0:T(8,128)S(1)}, f32[128,128]{1,0:T(8,128)}, u32[]{:S(2)}) copy-start(f32[128,128]{1,0:T(8,128)} %param.19) | copy-start | bytes 196612
  249.7 1097.8 %copy-start.9 = (bf16[8,32768]{1,0:T(8,128)(2,1)S(1)}, bf16[8,32768]{1,0:T(8,128)(2,1)}, u32[]{:S(2)}) copy-start(bf16[8,32768]{1,0:T(8,128)(2,1)} %param.24) | copy-start | bytes 1572868
  249.7 1097.8 %copy-start.11 = (bf16[8,128]{1,0:T(8,128)(2,1)S(1)}, bf16[8,128]{1,0:T(8,128)(2,1)}, u32[]{:S(2)}) copy-start(bf16[8,128]{1,0:T(8,128)(2,1)} %param.22) | copy-start | bytes 6148
  1347.5 8.8 copy-start.10
  1884.8 3.7 copy-start.3
  1884.8 3.9 copy-start.6
  1884.8 6.1 copy-start.1
Sparse Core Ops, SparseCore 0:
  64.7 1280.6 reduce-scatter.3
  1347.6 537.1 all-gather.1
where the time goes:
time: 1900 us
  waiting for transfers between devices  1650 us (87%)
  local copies, waits for them, and re-layouts  132 us (7%)
  other arithmetic  59.4 us (3%)
  matrix products  29.1 us (2%)
    unnamed x3, waiting for transfers between devices  1090 us
    all_gather x1, waiting for transfers between devices, per_device(): block_rows = lax.all_gather(filtered, ('slab', 'sub'), axis=0, tiled=True)  523 us
    gather x1, local copies, waits for them, and re-layouts, edge_messages(): jnp.take(sender_pool, senders, axis=0).astype(jnp.float32)  114 us
    ppermute x2, waiting for transfers between devices, extended(): lax.ppermute(head, axis, [((i + 1) % count, i) for i in range(count)])  40.2 us
    dynamic_update_slice x4, other arithmetic, whole_tables(): lax.map(lambda wave: phase_tables(wave, coords), blocks)  38.4 us
  transfers between devices with their start and end apart: 6, of which 4 were waited for; matrix products, arithmetic and copies ran while one was open for 11% of the time, Pallas kernels for 0%

commit v1 on v0

v1 whole, which is shorter than its diff:
```python
import functools
import math

import jax
import jax.numpy as jnp
import numpy as np
from jax import lax
from jax.experimental import pallas as pl
from jax.experimental.pallas import tpu as pltpu
from jax.sharding import PartitionSpec as P

TOP = 6
SIDE = 2 * TOP + 1
XY_ROWS = 88
WAVE_ROWS = 2304
DEVICES = 256
ROWS_EACH = WAVE_ROWS // DEVICES
PARTS = 4
COS_TERMS = (
    0.999999989059022, -19.7392044994538, 64.93911745989, -85.4501395308031,
    60.1676309503793, -25.9675992464965, 6.52865815867317,
)
VMEM_LIMIT = 48 * 2**20


def wave_layout():
    flat = [(0, 0)] + [(kx, 0) for kx in range(1, TOP + 1)]
    flat += [(kx, ky) for ky in range(1, TOP + 1) for kx in range(-TOP, TOP + 1)]
    codes = np.full((WAVE_ROWS,), -1, np.int32)
    xy = np.zeros((2, XY_ROWS), np.float32)

    def code(kx, ky, kz):
        return ((kz + TOP) * SIDE + ky + TOP) * SIDE + kx + TOP

    for row, (kx, ky) in enumerate(flat):
        xy[0, row], xy[1, row] = kx, ky
        for kz in range(1, TOP + 1):
            base = (kz - 1) * 4 * XY_ROWS + row
            codes[base] = code(kx, ky, kz)
            codes[base + 2 * XY_ROWS] = code(kx, ky, kz)
            if row > 0:
                codes[base + XY_ROWS] = code(-kx, -ky, kz)
                codes[base + 3 * XY_ROWS] = code(-kx, -ky, kz)
        base = TOP * 4 * XY_ROWS + row
        codes[base] = code(kx, ky, 0)
        if row > 0:
            codes[base + XY_ROWS] = code(kx, ky, 0)
    return xy, codes.reshape(ROWS_EACH, DEVICES)


XY, CODES = wave_layout()


def turn_waves(turns):
    rest = turns - jnp.floor(turns + 0.5)
    quarter = rest - 0.25
    quarter = jnp.where(quarter < -0.5, quarter + 1.0, quarter)

    def cosine(part):
        square = part * part
        total = jnp.full_like(square, COS_TERMS[-1])
        for term in COS_TERMS[-2::-1]:
            total = total * square + term
        return total

    return cosine(rest), cosine(quarter)


def table_tile(xy_ref, pos_ref, first, width):
    wide = (XY_ROWS, width)
    coords = [jnp.broadcast_to(pos_ref[d : d + 1, first : first + width], wide) for d in range(2)]
    flat_turns = (
        jnp.broadcast_to(xy_ref[0][:, :1], wide) * coords[0]
        + jnp.broadcast_to(xy_ref[1][:, :1], wide) * coords[1]
    )
    cos_xy, sin_xy = turn_waves(flat_turns)
    steps = lax.broadcasted_iota(jnp.int32, (8, width), 0).astype(jnp.float32)
    cos_z, sin_z = turn_waves(
        steps * jnp.broadcast_to(pos_ref[2:3, first : first + width], (8, width))
    )
    rows = []
    for kz in range(1, TOP + 1):
        cos_k = jnp.broadcast_to(cos_z[kz : kz + 1], wide)
        sin_k = jnp.broadcast_to(sin_z[kz : kz + 1], wide)
        both_cos, both_sin = cos_xy * cos_k, sin_xy * sin_k
        sin_cos, cos_sin = sin_xy * cos_k, cos_xy * sin_k
        rows += [both_cos - both_sin, both_cos + both_sin, cos_sin + sin_cos, cos_sin - sin_cos]
    rows += [cos_xy, sin_xy, jnp.zeros((WAVE_ROWS - 26 * XY_ROWS, width), jnp.float32)]
    return jnp.concatenate(rows, axis=0).astype(jnp.bfloat16)


def factor_kernel(count_ref, xy_ref, pos_ref, features_ref, sums_ref, table_ref):
    atoms, channels = features_ref.shape
    features = features_ref[...]
    live = lax.broadcasted_iota(jnp.int32, (atoms, channels), 0) < count_ref[0]
    masked = jnp.where(live, features.astype(jnp.float32), 0.0).astype(jnp.bfloat16)
    for first in range(0, atoms, 128):
        table_ref[:, first : first + 128] = table_tile(xy_ref, pos_ref, first, 128)
    for r in range(ROWS_EACH):
        sums_ref[:, r * channels : (r + 1) * channels] = jnp.dot(
            table_ref[r * DEVICES : (r + 1) * DEVICES, :],
            masked,
            preferred_element_type=jnp.float32,
        )


def factor_call(atom_count, positions, features):
    atoms, channels = features.shape
    vmem = pl.BlockSpec(memory_space=pltpu.VMEM)
    return pl.pallas_call(
        factor_kernel,
        in_specs=[pl.BlockSpec(memory_space=pltpu.SMEM), vmem, vmem, vmem],
        out_specs=vmem,
        out_shape=jax.ShapeDtypeStruct((DEVICES, ROWS_EACH * channels), jnp.float32),
        scratch_shapes=[pltpu.VMEM((WAVE_ROWS, atoms), jnp.bfloat16)],
        compiler_params=pltpu.CompilerParams(vmem_limit_bytes=VMEM_LIMIT),
        name="factor_sums",
    )(atom_count, jnp.asarray(np.broadcast_to(XY[:, :, None], (2, XY_ROWS, 128))), positions, features)


def filter_kernel(norm_factor, sums_ref, weight_ref, mix_ref, out_ref):
    channels = mix_ref.shape[0]
    total = jnp.sum(sums_ref[...], axis=0, keepdims=True)
    rows = [total[:, r * channels : (r + 1) * channels] for r in range(ROWS_EACH)]
    rows.append(jnp.zeros((16 - ROWS_EACH, channels), jnp.float32))
    scaled = jnp.concatenate(rows, axis=0) * norm_factor * weight_ref[...]
    mixed = jnp.dot(
        scaled, mix_ref[...], precision=lax.Precision.HIGHEST, preferred_element_type=jnp.float32
    )
    for r in range(ROWS_EACH):
        out_ref[:, r * channels : (r + 1) * channels] = jnp.broadcast_to(
            mixed[r : r + 1], (out_ref.shape[0], channels)
        ).astype(jnp.bfloat16)


def filter_call(sums, weights, w_mix, norm_factor):
    return pl.pallas_call(
        functools.partial(filter_kernel, norm_factor),
        out_shape=jax.ShapeDtypeStruct(sums.shape, jnp.bfloat16),
        name="filter_rows",
    )(sums, weights, w_mix)


def wave_weights(kgrid, k_filter, first):
    kx, ky, kz = kgrid[0], kgrid[1], kgrid[2]
    low = (kz < 0) | ((kz == 0) & ((ky < 0) | ((ky == 0) & (kx < 0))))
    sign = jnp.where(low, -1, 1)
    code = ((kz * sign + TOP) * SIDE + ky * sign + TOP) * SIDE + kx * sign + TOP
    mine = lax.dynamic_slice_in_dim(jnp.asarray(CODES), first, 1, 1)
    mine = jnp.pad(mine, ((0, 16 - ROWS_EACH), (0, 0)), constant_values=-1)
    same = (mine == code[None, :]).astype(jnp.float32)
    return jnp.dot(same, k_filter, precision=lax.Precision.HIGHEST)


def edge_kernel(
    degree, unroll, ids_ref, basis_ref, features_ref, recv_ref, wb_ref, wo_ref, *refs
):
    blocks, (after_ref, out_ref, pool_ref, radial_ref, part_ref, own_ref) = refs[:9], refs[9:]
    atoms, channels = features_ref.shape
    del after_ref

    @pl.when(pl.program_id(0) == 0)
    def _():
        for at, block in enumerate(blocks):
            rows = block.shape[0]
            pool_ref[at * rows : (at + 1) * rows, :] = block[...].astype(jnp.float32)

    own_ref[...] = jnp.dot(
        features_ref[...], recv_ref[...], preferred_element_type=jnp.float32
    )
    radial_ref[...] = lax.dot_general(
        basis_ref[...], wb_ref[...], (((0,), (0,)), ((), ())), preferred_element_type=jnp.float32
    )
    sublane = lax.broadcasted_iota(jnp.int32, (8, channels), 0)

    def one_atom(atom):
        own = jnp.broadcast_to(own_ref[pl.ds(atom, 1), :], (8, channels))
        total = None
        for at in range(0, degree, 8):
            edge = atom * degree + at
            rows = [
                jnp.broadcast_to(pool_ref[pl.ds(ids_ref[edge + r], 1), :], (8, channels))
                for r in range(8)
            ]
            sent = rows[0]
            for r in range(1, 8):
                sent = jnp.where(sublane == r, rows[r], sent)
            half = (sent + radial_ref[pl.ds(pl.multiple_of(edge, 8), 8), :] + own) * 0.5
            hidden = (half + half * jnp.tanh(half)).astype(jnp.bfloat16).astype(jnp.float32)
            total = hidden if total is None else total + hidden
        part_ref[pl.ds(pl.multiple_of(atom * 8, 8), 8), :] = total

    def some_atoms(step, carry):
        for u in range(unroll):
            one_atom(step * unroll + u)
        return carry

    lax.fori_loop(0, atoms // unroll, some_atoms, 0)
    summed = part_ref[pl.ds(0, atoms, stride=8), :]
    for r in range(1, 8):
        summed = summed + part_ref[pl.ds(r, atoms, stride=8), :]
    high = summed.astype(jnp.bfloat16)
    low = (summed - high.astype(jnp.float32)).astype(jnp.bfloat16)
    message = jnp.dot(high, wo_ref[...], preferred_element_type=jnp.float32) + jnp.dot(
        low, wo_ref[...], preferred_element_type=jnp.float32
    )
    out_ref[...] = message * (1.0 / math.sqrt(degree))


def edge_call(part, after, senders, edge_basis, features, w_recv, w_basis, w_out, blocks):
    atoms, channels = features.shape
    degree = senders.shape[0] // atoms
    step = 128
    steps = atoms // PARTS // step
    first = part * steps
    whole = lambda array: pl.BlockSpec(array.shape, lambda i: (0, 0), pipeline_mode=pl.Buffered(1))
    rows = sum(block.shape[0] for block in blocks)
    return pl.pallas_call(
        functools.partial(edge_kernel, degree, 8),
        grid=(steps,),
        in_specs=[
            pl.BlockSpec((step * degree,), lambda i: (first + i,), memory_space=pltpu.SMEM),
            pl.BlockSpec((edge_basis.shape[0], step * degree), lambda i: (0, first + i)),
            pl.BlockSpec((step, channels), lambda i: (first + i, 0)),
            whole(w_recv),
            whole(w_basis),
            whole(w_out),
        ]
        + [whole(block) for block in blocks]
        + [pl.BlockSpec(memory_space=pl.ANY)],
        out_specs=pl.BlockSpec((step, channels), lambda i: (i, 0)),
        out_shape=jax.ShapeDtypeStruct((atoms // PARTS, channels), jnp.float32),
        scratch_shapes=[
            pltpu.VMEM((rows, channels), jnp.float32),
            pltpu.VMEM((step * degree, channels), jnp.float32),
            pltpu.VMEM((step * 8, channels), jnp.float32),
            pltpu.VMEM((step, channels), jnp.float32),
        ],
        compiler_params=pltpu.CompilerParams(vmem_limit_bytes=VMEM_LIMIT),
        cost_estimate=pl.CostEstimate(
            flops=8 * 10**9, bytes_accessed=4 * 10**6, transcendentals=10**6
        ),
        name="edge_part_%d" % part,
    )(senders, edge_basis, features, w_recv, w_basis, w_out, *blocks, after)


def final_kernel(scale, count_ref, xy_ref, pos_ref, factors_ref, *refs):
    parts, out_ref = refs[:-1], refs[-1]
    channels = out_ref.shape[1]
    factors = jnp.concatenate(
        [factors_ref[:, r * channels : (r + 1) * channels] for r in range(ROWS_EACH)], axis=0
    )
    for at, part in enumerate(parts):
        atoms = part.shape[0]
        first = at * atoms
        table = table_tile(xy_ref, pos_ref, first, atoms)
        field = lax.dot_general(
            factors, table, (((0,), (0,)), ((), ())), preferred_element_type=jnp.float32
        )
        live = first + lax.broadcasted_iota(jnp.int32, (atoms, channels), 0) < count_ref[0]
        out_ref[first : first + atoms, :] = jnp.where(live, part[...] + field.T * scale, 0.0)


def final_call(atom_count, positions, factors, parts, scale):
    atoms = sum(part.shape[0] for part in parts)
    channels = parts[0].shape[1]
    vmem = pl.BlockSpec(memory_space=pltpu.VMEM)
    return pl.pallas_call(
        functools.partial(final_kernel, scale),
        in_specs=[pl.BlockSpec(memory_space=pltpu.SMEM)] + [vmem] * (3 + len(parts)),
        out_specs=vmem,
        out_shape=jax.ShapeDtypeStruct((atoms, channels), jnp.float32),
        compiler_params=pltpu.CompilerParams(vmem_limit_bytes=VMEM_LIMIT),
        name="updated_rows",
    )(
        atom_count,
        jnp.asarray(np.broadcast_to(XY[:, :, None], (2, XY_ROWS, 128))),
        positions,
        factors,
        *parts,
    )


def shifted(array, axis, step):
    count = lax.axis_size(axis)
    return lax.ppermute(array, axis, [(i, (i + step) % count) for i in range(count)])


def per_device(
    features, positions, atom_count, kgrid, k_filter, w_mix, w_recv, w_send, w_basis, w_out,
    edge_basis, senders,
):
    atoms, channels = features.shape
    total_k = kgrid.shape[1]
    subs, slabs = lax.axis_size("sub"), lax.axis_size("slab")
    send_proj = jnp.dot(features, w_send, preferred_element_type=jnp.float32).astype(jnp.bfloat16)
    column = [shifted(send_proj, "slab", 1), send_proj, shifted(send_proj, "slab", -1)]
    before = [shifted(block, "sub", 1) for block in column]
    behind = [shifted(block, "sub", -1) for block in column]
    blocks = [block for a in range(3) for block in (before[a], column[a], behind[a])]

    sums = factor_call(atom_count, positions, features)
    sums = lax.all_to_all(sums, "sub", 0, 0, tiled=True)
    sums = jnp.sum(sums.reshape(subs, slabs, -1), axis=0)
    stage_one = sums
    sums = lax.all_to_all(sums, "slab", 0, 0, tiled=True)
    first = lax.axis_index("sub") * slabs + lax.axis_index("slab")
    weights = wave_weights(kgrid, k_filter, first)
    filtered = filter_call(sums, weights, w_mix, 1.0 / math.sqrt(atoms * DEVICES))
    spread = lax.all_to_all(filtered, "slab", 0, 0, tiled=True)
    factors = jnp.broadcast_to(spread[None], (subs,) + spread.shape).reshape(DEVICES, -1)
    factors = lax.all_to_all(factors, "sub", 0, 0, tiled=True)

    after = [stage_one, stage_one, filtered, spread]
    parts = [
        edge_call(p, after[p], senders, edge_basis, features, w_recv, w_basis, w_out, blocks)
        for p in range(PARTS)
    ]
    return final_call(atom_count, positions, factors, parts, 4.0 / math.sqrt(total_k))


def solution(mesh):
    placed = (
        P(("slab", "sub"), None),
        P(None, ("slab", "sub")),
        P(("slab", "sub")),
        P(), P(), P(), P(), P(), P(), P(),
        P(None, ("slab", "sub")),
        P(("slab", "sub")),
    )
    return jax.shard_map(
        per_device, mesh=mesh, in_specs=placed, out_specs=P(("slab", "sub"), None), check_vma=False
    )
```

time: 1900 us -> 146 us (0.08)
  waiting for transfers between devices: 1650 us -> 20.8 us
  local copies, waits for them, and re-layouts: 132 us -> 15 us
  other arithmetic: 59.4 us -> 2.96 us
  Pallas kernels: 0 us -> 49 us
  starting transfers between devices: 7.8 us -> 54.5 us
  matrix products: 29.1 us -> 1.27 us
    unnamed x3 -> x0, waiting for transfers between devices: 1090 us -> none
    all_gather x1 -> x0, waiting for transfers between devices: 523 us -> none  [per_device(): block_rows = lax.all_gather(filtered, ('slab', 'sub'), axis=0, tiled=True)]
    gather x1 -> x0, local copies, waits for them, and re-layouts: 114 us -> none  [edge_messages(): jnp.take(sender_pool, senders, axis=0).astype(jnp.float32)]
    pallas_call x0 -> x7, Pallas kernels: none -> 49 us  [the longest x4 40.4 us: edge_call(): pl.pallas_call(functools.partial(edge_kernel, degree, 8), grid=(steps,),...]
    dynamic_update_slice x4 -> x0, other arithmetic: 38.4 us -> none  [whole_tables(): lax.map(lambda wave: phase_tables(wave, coords), blocks)]
    all_to_all x0 -> x4, starting transfers between devices: none -> 34.2 us  [the longest x1 11.2 us: per_device(): sums = lax.all_to_all(sums, 'slab', 0, 0, tiled=True)]
    dot_general x10 -> x2, matrix products: 29.1 us -> 1.27 us  [the longest x1 1.07 us: wave_weights(): return jnp.dot(same, k_filter, precision=lax.Precision.HIGHEST)]
    ppermute x4 -> x8, waiting for transfers between devices: 44.7 us -> 20.8 us  [shifted(): lax.ppermute(array, axis, [(i, (i + step) % count) for i in range(count)])]
  transfers between devices with their start and end apart: 6 -> 12, of which waited for: 4 -> 1; matrix products, arithmetic and copies ran while one was open for 11% -> 3% of each run, Pallas kernels for 0% -> 28%
where the time goes in v1:
time: 146 us; the launch traced here: 145 us
  starting transfers between devices  54.5 us (37%)
  Pallas kernels  49 us (34%)
  waiting for transfers between devices  20.8 us (14%)
  local copies, waits for them, and re-layouts  15 us (10%)
  other arithmetic  2.96 us (2%)
    pallas_call x4, Pallas kernels, edge_call(): pl.pallas_call(functools.partial(edge_kernel, degree, 8), grid=(steps,),...  40.4 us
    ppermute x8, waiting for transfers between devices, shifted(): lax.ppermute(array, axis, [(i, (i + step) % count) for i in range(count)])  20.8 us
    ppermute x8, starting transfers between devices, shifted(): lax.ppermute(array, axis, [(i, (i + step) % count) for i in range(count)])  20.3 us
    unnamed x52, local copies, waits for them, and re-layouts  11.3 us
    all_to_all x1, starting transfers between devices, per_device(): sums = lax.all_to_all(sums, 'slab', 0, 0, tiled=True)  11.2 us
    all_to_all x1, starting transfers between devices, per_device(): spread = lax.all_to_all(filtered, 'slab', 0, 0, tiled=True)  8.9 us
    all_to_all x1, starting transfers between devices, per_device(): sums = lax.all_to_all(sums, 'sub', 0, 0, tiled=True)  7.61 us
    all_to_all x1, starting transfers between devices, per_device(): factors = lax.all_to_all(factors, 'sub', 0, 0, tiled=True)  6.47 us
  transfers between devices with their start and end apart: 12, of which 1 were waited for; matrix products, arithmetic and copies ran while one was open for 3% of the time, Pallas kernels for 28%

profile of v1, /device:TPU:1, one launch (start us, length us, event | category | flops | bytes accessed | tf_op | source)
XLA Modules:
  0.0 144.6 jit_solution(1111217837066305380)
XLA Ops:
  3.2 4.1 %factor_sums.1 = f32[256,1152]{1,0:T(8,128)} custom-call(s32[1]{0:T(128)S(6)} %copy.27.count_ref, f32[2,88,128]{2,1,0:T(8,128)S(1)} %jit_solution_.6.xy_ref, f32[3,1024]{1,0:T(4,128)S(1)} %copy-done.4, bf16[1024,128]{1,0:T(8,128)(2,1)S(1)} %copy-done.1), custom_call_target="tpu_custom_call" | custom-call | tf_op jit(solution)/shard_map/factor_sums/pallas_call | solution.py:110
  7.3 7.6 %all-to-all-start = ((f32[8,32,1152]{2,1,0:T(8,128)}), f32[8,32,1152]{2,1,0:T(8,128)}, u32[]{:S(2)}, u32[]{:S(2)}) async-start(f32[8,32,1152]{2,1,0:T(8,128)} %bitcast), calls=%async_computation | async-start | bytes 2359296 | tf_op jit(solution)/shard_map/all_to_all | solution.py:303
  15.1 1.3 collective-permute-start
  16.4 3.8 %collective-permute-start.3 = (bf16[1024,128]{1,0:T(8,128)(2,1)S(1)}, bf16[1024,128]{1,0:T(8,128)(2,1)S(1)}, u32[]{:S(2)}, u32[]{:S(2)}) collective-permute-start(bf16[1024,128]{1,0:T(8,128)(2,1)S(1)} %convolution_convert_fusion.refs_4_), channel_id=1, source_target_pairs={{0,1},{1,2},{2,3},{3,4},{4,5},{5,6},{6,7},{7,0},{8,9},{9,10},{10,1... | collective-permute-start | bytes 786440 | tf_op jit(solution)/shard_map/ppermute | solution.py:286
  20.3 2.1 %collective-permute-start.4 = (bf16[1024,128]{1,0:T(8,128)(2,1)S(1)}, bf16[1024,128]{1,0:T(8,128)(2,1)}, u32[]{:S(2)}, u32[]{:S(2)}) collective-permute-start(bf16[1024,128]{1,0:T(8,128)(2,1)S(1)} %convolution_convert_fusion.refs_4_), channel_id=1, source_target_pairs={{0,7},{1,0},{2,1},{3,2},{4,3},{5,4},{6,5},{7,6},{8,15},{9,8},{10,9... | collective-permute-start | bytes 786440 | tf_op jit(solution)/shard_map/ppermute | solution.py:286
  23.1 20.8 %collective-permute-done.refs_1_ = bf16[1024,128]{1,0:T(8,128)(2,1)S(1)} collective-permute-done((bf16[1024,128]{1,0:T(8,128)(2,1)S(1)}, bf16[1024,128]{1,0:T(8,128)(2,1)S(1)}, u32[]{:S(2)}, u32[]{:S(2)}) %collective-permute-start) | collective-permute-done | bytes 262176 | tf_op jit(solution)/shard_map/ppermute | solution.py:286
  43.9 6.0 %collective-permute-start.1 = (bf16[1024,128]{1,0:T(8,128)(2,1)S(1)}, bf16[1024,128]{1,0:T(8,128)(2,1)}, u32[]{:S(2)}, u32[]{:S(2)}) collective-permute-start(bf16[1024,128]{1,0:T(8,128)(2,1)S(1)} %collective-permute-done.refs_1_), channel_id=1, source_target_pairs={{0,1},{1,2},{2,3},{3,4},{4,5},{5,6},{6,7},{7,0},{8,9},{9,10},{10,1... | collective-permute-start | bytes 786440 | tf_op jit(solution)/shard_map/ppermute | solution.py:286
  49.9 2.0 %collective-permute-start.2 = (bf16[1024,128]{1,0:T(8,128)(2,1)S(1)}, bf16[1024,128]{1,0:T(8,128)(2,1)}, u32[]{:S(2)}, u32[]{:S(2)}) collective-permute-start(bf16[1024,128]{1,0:T(8,128)(2,1)S(1)} %collective-permute-done.refs_1_), channel_id=1, source_target_pairs={{0,7},{1,0},{2,1},{3,2},{4,3},{5,4},{6,5},{7,6},{8,15},{9,8},{10,9... | collective-permute-start | bytes 786440 | tf_op jit(solution)/shard_map/ppermute | solution.py:286
  52.9 4.1 %collective-permute-start.7 = (bf16[1024,128]{1,0:T(8,128)(2,1)S(1)}, bf16[1024,128]{1,0:T(8,128)(2,1)}, u32[]{:S(2)}, u32[]{:S(2)}) collective-permute-start(bf16[1024,128]{1,0:T(8,128)(2,1)S(1)} %collective-permute-done.5.refs_7_), channel_id=1, source_target_pairs={{0,7},{1,0},{2,1},{3,2},{4,3},{5,4},{6,5},{7,6},{8,15},{9,8},{10,9... | collective-permute-start | bytes 786440 | tf_op jit(solution)/shard_map/ppermute | solution.py:286
  57.0 1.1 fusion.weight_ref
  58.1 1.4 reduce_sum.9.refs_9_
  60.3 11.2 %all-to-all-start.1 = ((f32[32,1,1152]{2,1,0:T(1,128)}), f32[32,1,1152]{2,1,0:T(1,128)S(1)}, u32[]{:S(2)}, u32[]{:S(2)}) async-start(f32[32,1,1152]{2,1,0:T(1,128)} %copy.18), calls=%async_computation.1 | async-start | bytes 294912 | tf_op jit(solution)/shard_map/all_to_all | solution.py:306
  72.6 10.1 %edge_part_1.1.refs_1_ = f32[256,128]{1,0:T(8,128)S(1)} custom-call(s32[32768]{0:T(1024)S(1)} %copy-done.16, bf16[8,32768]{1,0:T(8,128)(2,1)S(1)} %copy-done.6, bf16[1024,128]{1,0:T(8,128)(2,1)S(1)} %copy-done.2, bf16[128,128]{1,0:T(8,128)(2,1)S(1)} %copy-done.17, bf16[8,128]{1,0:T(8,128)(2,1)S(1)} %copy-done.20, bf16[128,128]{1,0:T(8,128)(2,1)S(1)} %copy-done.18, ...), custom_call_target="tpu_custom_call" | custom-call | flops 8000000000 | bytes 4000000 | tf_op jit(solution)/shard_map/edge_part_1/pallas_call | solution.py:218
  82.7 10.1 %edge_part_0.1.refs_0_ = f32[256,128]{1,0:T(8,128)S(1)} custom-call(s32[32768]{0:T(1024)S(1)} %copy-done.16, bf16[8,32768]{1,0:T(8,128)(2,1)S(1)} %copy-done.6, bf16[1024,128]{1,0:T(8,128)(2,1)S(1)} %copy-done.2, bf16[128,128]{1,0:T(8,128)(2,1)S(1)} %copy-done.17, bf16[8,128]{1,0:T(8,128)(2,1)S(1)} %copy-done.20, bf16[128,128]{1,0:T(8,128)(2,1)S(1)} %copy-done.18, ...), custom_call_target="tpu_custom_call" | custom-call | flops 8000000000 | bytes 4000000 | tf_op jit(solution)/shard_map/edge_part_0/pallas_call | solution.py:218
  93.5 1.7 %filter_rows.1.refs_9_ = bf16[32,1152]{1,0:T(8,128)(2,1)} custom-call(f32[32,1152]{1,0:T(8,128)} %bitcast.21, f32[16,128]{1,0:T(8,128)} %fusion.weight_ref, f32[128,128]{1,0:T(8,128)} %mix_ref.1), custom_call_target="tpu_custom_call" | custom-call | tf_op jit(solution)/shard_map/filter_rows/pallas_call | solution.py:137
  95.8 1.5 %reduce.1 = bf16[32,1152]{1,0:T(8,128)(2,1)S(1)} reduce(bf16[32,1,1152]{2,0,1:T(8,128)(2,1)} %bitcast.20, bf16[]{:T(256)} %broadcast.29), dimensions={1}, to_apply=%copy.19.reduce_sub_computation | reduce | bytes 147458 | tf_op jit(solution)/shard_map/all_to_all | solution.py:310
  98.0 8.9 %all-to-all-start.2 = ((bf16[32,2,576]{2,1,0:T(2,128)(2,1)}), bf16[32,2,576]{2,1,0:T(2,128)(2,1)S(1)}, u32[]{:S(2)}, u32[]{:S(2)}) async-start(bf16[32,2,576]{2,1,0:T(2,128)(2,1)} %reshape.14), calls=%async_computation.2 | async-start | bytes 163840 | tf_op jit(solution)/shard_map/all_to_all | solution.py:310
  107.9 0.9 copy-done.10
  108.8 0.9 copy-done.14
  109.7 10.1 %edge_part_2.1.refs_2_ = f32[256,128]{1,0:T(8,128)S(1)} custom-call(s32[32768]{0:T(1024)S(1)} %copy-done.16, bf16[8,32768]{1,0:T(8,128)(2,1)S(1)} %copy-done.6, bf16[1024,128]{1,0:T(8,128)(2,1)S(1)} %copy-done.2, bf16[128,128]{1,0:T(8,128)(2,1)S(1)} %copy-done.17, bf16[8,128]{1,0:T(8,128)(2,1)S(1)} %copy-done.20, bf16[128,128]{1,0:T(8,128)(2,1)S(1)} %copy-done.18, ...), custom_call_target="tpu_custom_call" | custom-call | flops 8000000000 | bytes 4000000 | tf_op jit(solution)/shard_map/edge_part_2/pallas_call | solution.py:218
  120.9 6.5 %all-to-all-start.3 = ((bf16[8,32,1152]{2,1,0:T(8,128)(2,1)}), bf16[8,32,1152]{2,1,0:T(8,128)(2,1)S(1)}, u32[]{:S(2)}, u32[]{:S(2)}) async-start(bf16[8,32,1152]{2,1,0:T(8,128)(2,1)} %broadcast_in_dim.20), calls=%async_computation.3 | async-start | bytes 1179648 | tf_op jit(solution)/shard_map/all_to_all | solution.py:312
  128.3 0.9 copy-done.11
  131.7 10.1 %edge_part_3.1.refs_3_ = f32[256,128]{1,0:T(8,128)S(1)} custom-call(s32[32768]{0:T(1024)S(1)} %copy-done.16, bf16[8,32768]{1,0:T(8,128)(2,1)S(1)} %copy-done.6, bf16[1024,128]{1,0:T(8,128)(2,1)S(1)} %copy-done.2, bf16[128,128]{1,0:T(8,128)(2,1)S(1)} %copy-done.17, bf16[8,128]{1,0:T(8,128)(2,1)S(1)} %copy-done.21, bf16[128,128]{1,0:T(8,128)(2,1)S(1)} %copy-done.19, ...), custom_call_target="tpu_custom_call" | custom-call | flops 8000000000 | bytes 4000000 | tf_op jit(solution)/shard_map/edge_part_3/pallas_call | solution.py:218
  141.8 2.8 %updated_rows.1 = f32[1024,128]{1,0:T(8,128)} custom-call(s32[1]{0:T(128)S(6)} %copy.27.count_ref, f32[2,88,128]{2,1,0:T(8,128)S(1)} %jit_solution_.6.xy_ref, f32[3,1024]{1,0:T(4,128)S(1)} %copy-done.5, bf16[256,1152]{1,0:T(8,128)(2,1)S(1)} %bitcast.16, f32[256,128]{1,0:T(8,128)S(1)} %edge_part_0.1.refs_0_, f32[256,128]{1,0:T(8,128)S(1)} %edge_part_1.1.refs_1_, ...), custom_call_target="tpu_custom_call" | custom-call | tf_op jit(solution)/shard_map/updated_rows/pallas_call | solution.py:268
  (70 shorter events, 13.4 us)
Async XLA Ops:
  0.0 57.0 %copy-start = (f32[2048,128]{1,0:T(8,128)S(1)}, f32[2048,128]{1,0:T(8,128)}, u32[]{:S(2)}) copy-start(f32[2048,128]{1,0:T(8,128)} %param.19) | copy-start | bytes 3145732
  7.2 7.6 %copy-start.2 = (bf16[1024,128]{1,0:T(8,128)(2,1)S(1)}, bf16[1024,128]{1,0:T(8,128)(2,1)}, u32[]{:S(2)}) copy-start(bf16[1024,128]{1,0:T(8,128)(2,1)} %features_ref.9) | copy-start | bytes 786436
  7.2 7.6 %copy-start.22 = (bf16[128,128]{1,0:T(8,128)(2,1)S(1)}, bf16[128,128]{1,0:T(8,128)(2,1)}, u32[]{:S(2)}) copy-start(bf16[128,128]{1,0:T(8,128)(2,1)} %param.22) | copy-start | bytes 98308
  7.2 15.1 %copy-start.23 = (s32[3,2048]{1,0:T(4,128)S(1)}, s32[3,2048]{1,0:T(4,128)}, u32[]{:S(2)}) copy-start(s32[3,2048]{1,0:T(4,128)} %param.18) | copy-start | bytes 73732
  7.3 50.9 %all-to-all-start = ((f32[8,32,1152]{2,1,0:T(8,128)}), f32[8,32,1152]{2,1,0:T(8,128)}, u32[]{:S(2)}, u32[]{:S(2)}) async-start(f32[8,32,1152]{2,1,0:T(8,128)} %bitcast), calls=%async_computation | async-start | bytes 2359296 | tf_op jit(solution)/shard_map/all_to_all | solution.py:303
  15.1 28.8 %collective-permute-start = (bf16[1024,128]{1,0:T(8,128)(2,1)S(1)}, bf16[1024,128]{1,0:T(8,128)(2,1)S(1)}, u32[]{:S(2)}, u32[]{:S(2)}) collective-permute-start(bf16[1024,128]{1,0:T(8,128)(2,1)S(1)} %convolution_convert_fusion.refs_4_), channel_id=1, source_target_pairs={{0,8},{8,16},{16,24},{24,32},{32,40},{40,48},{48,56},{56,64},{64,7... | collective-permute-start | bytes 786440 | tf_op jit(solution)/shard_map/ppermute | solution.py:286
  16.4 35.5 %collective-permute-start.5 = (bf16[1024,128]{1,0:T(8,128)(2,1)S(1)}, bf16[1024,128]{1,0:T(8,128)(2,1)S(1)}, u32[]{:S(2)}, u32[]{:S(2)}) collective-permute-start(bf16[1024,128]{1,0:T(8,128)(2,1)S(1)} %convolution_convert_fusion.refs_4_), channel_id=1, source_target_pairs={{0,248},{8,0},{16,8},{24,16},{32,24},{40,32},{48,40},{56,48},{64,5... | collective-permute-start | bytes 786440 | tf_op jit(solution)/shard_map/ppermute | solution.py:286
  16.4 36.4 %collective-permute-start.3 = (bf16[1024,128]{1,0:T(8,128)(2,1)S(1)}, bf16[1024,128]{1,0:T(8,128)(2,1)S(1)}, u32[]{:S(2)}, u32[]{:S(2)}) collective-permute-start(bf16[1024,128]{1,0:T(8,128)(2,1)S(1)} %convolution_convert_fusion.refs_4_), channel_id=1, source_target_pairs={{0,1},{1,2},{2,3},{3,4},{4,5},{5,6},{6,7},{7,0},{8,9},{9,10},{10,1... | collective-permute-start | bytes 786440 | tf_op jit(solution)/shard_map/ppermute | solution.py:286
  20.3 51.3 %collective-permute-start.4 = (bf16[1024,128]{1,0:T(8,128)(2,1)S(1)}, bf16[1024,128]{1,0:T(8,128)(2,1)}, u32[]{:S(2)}, u32[]{:S(2)}) collective-permute-start(bf16[1024,128]{1,0:T(8,128)(2,1)S(1)} %convolution_convert_fusion.refs_4_), channel_id=1, source_target_pairs={{0,7},{1,0},{2,1},{3,2},{4,3},{5,4},{6,5},{7,6},{8,15},{9,8},{10,9... | collective-permute-start | bytes 786440 | tf_op jit(solution)/shard_map/ppermute | solution.py:286
  43.9 63.0 %copy-start.7 = (bf16[1024,128]{1,0:T(8,128)(2,1)}, bf16[1024,128]{1,0:T(8,128)(2,1)S(1)}, u32[]{:S(2)}) copy-start(bf16[1024,128]{1,0:T(8,128)(2,1)S(1)} %collective-permute-done.refs_1_) | copy-start | bytes 786436
  43.9 27.6 %collective-permute-start.1 = (bf16[1024,128]{1,0:T(8,128)(2,1)S(1)}, bf16[1024,128]{1,0:T(8,128)(2,1)}, u32[]{:S(2)}, u32[]{:S(2)}) collective-permute-start(bf16[1024,128]{1,0:T(8,128)(2,1)S(1)} %collective-permute-done.refs_1_), channel_id=1, source_target_pairs={{0,1},{1,2},{2,3},{3,4},{4,5},{5,6},{6,7},{7,0},{8,9},{9,10},{10,1... | collective-permute-start | bytes 786440 | tf_op jit(solution)/shard_map/ppermute | solution.py:286
  49.9 21.7 %collective-permute-start.2 = (bf16[1024,128]{1,0:T(8,128)(2,1)S(1)}, bf16[1024,128]{1,0:T(8,128)(2,1)}, u32[]{:S(2)}, u32[]{:S(2)}) collective-permute-start(bf16[1024,128]{1,0:T(8,128)(2,1)S(1)} %collective-permute-done.refs_1_), channel_id=1, source_target_pairs={{0,7},{1,0},{2,1},{3,2},{4,3},{5,4},{6,5},{7,6},{8,15},{9,8},{10,9... | collective-permute-start | bytes 786440 | tf_op jit(solution)/shard_map/ppermute | solution.py:286
  51.9 30.8 %copy-start.9 = (bf16[1024,128]{1,0:T(8,128)(2,1)}, bf16[1024,128]{1,0:T(8,128)(2,1)S(1)}, u32[]{:S(2)}) copy-start(bf16[1024,128]{1,0:T(8,128)(2,1)S(1)} %collective-permute-done.5.refs_7_) | copy-start | bytes 786436
  51.9 19.6 %collective-permute-start.6 = (bf16[1024,128]{1,0:T(8,128)(2,1)S(1)}, bf16[1024,128]{1,0:T(8,128)(2,1)}, u32[]{:S(2)}, u32[]{:S(2)}) collective-permute-start(bf16[1024,128]{1,0:T(8,128)(2,1)S(1)} %collective-permute-done.5.refs_7_), channel_id=1, source_target_pairs={{0,1},{1,2},{2,3},{3,4},{4,5},{5,6},{6,7},{7,0},{8,9},{9,10},{10,1... | collective-permute-start | bytes 786440 | tf_op jit(solution)/shard_map/ppermute | solution.py:286
  52.9 18.7 %collective-permute-start.7 = (bf16[1024,128]{1,0:T(8,128)(2,1)S(1)}, bf16[1024,128]{1,0:T(8,128)(2,1)}, u32[]{:S(2)}, u32[]{:S(2)}) collective-permute-start(bf16[1024,128]{1,0:T(8,128)(2,1)S(1)} %collective-permute-done.5.refs_7_), channel_id=1, source_target_pairs={{0,7},{1,0},{2,1},{3,2},{4,3},{5,4},{6,5},{7,6},{8,15},{9,8},{10,9... | collective-permute-start | bytes 786440 | tf_op jit(solution)/shard_map/ppermute | solution.py:286
  58.1 13.5 %copy-start.6 = (bf16[8,32768]{1,0:T(8,128)(2,1)S(1)}, bf16[8,32768]{1,0:T(8,128)(2,1)}, u32[]{:S(2)}) copy-start(bf16[8,32768]{1,0:T(8,128)(2,1)} %basis_ref.7) | copy-start | bytes 1572868
  58.1 13.5 %copy-start.16 = (s32[32768]{0:T(1024)S(1)}, s32[32768]{0:T(1024)}, u32[]{:S(2)}) copy-start(s32[32768]{0:T(1024)} %ids_ref.7) | copy-start | bytes 393220
  58.1 13.5 %copy-start.17 = (bf16[128,128]{1,0:T(8,128)(2,1)S(1)}, bf16[128,128]{1,0:T(8,128)(2,1)}, u32[]{:S(2)}) copy-start(bf16[128,128]{1,0:T(8,128)(2,1)} %recv_ref.7) | copy-start | bytes 98308
  58.1 13.5 %copy-start.18 = (bf16[128,128]{1,0:T(8,128)(2,1)S(1)}, bf16[128,128]{1,0:T(8,128)(2,1)}, u32[]{:S(2)}) copy-start(bf16[128,128]{1,0:T(8,128)(2,1)} %wo_ref.7) | copy-start | bytes 98308
  58.1 13.5 %copy-start.20 = (bf16[8,128]{1,0:T(8,128)(2,1)S(1)}, bf16[8,128]{1,0:T(8,128)(2,1)}, u32[]{:S(2)}) copy-start(bf16[8,128]{1,0:T(8,128)(2,1)} %wb_ref.7) | copy-start | bytes 6148
  60.3 32.5 %all-to-all-start.1 = ((f32[32,1,1152]{2,1,0:T(1,128)}), f32[32,1,1152]{2,1,0:T(1,128)S(1)}, u32[]{:S(2)}, u32[]{:S(2)}) async-start(f32[32,1,1152]{2,1,0:T(1,128)} %copy.18), calls=%async_computation.1 | async-start | bytes 294912 | tf_op jit(solution)/shard_map/all_to_all | solution.py:306
  98.0 21.8 %all-to-all-start.2 = ((bf16[32,2,576]{2,1,0:T(2,128)(2,1)}), bf16[32,2,576]{2,1,0:T(2,128)(2,1)S(1)}, u32[]{:S(2)}, u32[]{:S(2)}) async-start(bf16[32,2,576]{2,1,0:T(2,128)(2,1)} %reshape.14), calls=%async_computation.2 | async-start | bytes 163840 | tf_op jit(solution)/shard_map/all_to_all | solution.py:310
  120.9 20.9 %all-to-all-start.3 = ((bf16[8,32,1152]{2,1,0:T(8,128)(2,1)}), bf16[8,32,1152]{2,1,0:T(8,128)(2,1)S(1)}, u32[]{:S(2)}, u32[]{:S(2)}) async-start(bf16[8,32,1152]{2,1,0:T(8,128)(2,1)} %broadcast_in_dim.20), calls=%async_computation.3 | async-start | bytes 1179648 | tf_op jit(solution)/shard_map/all_to_all | solution.py:312
  131.7 10.1 %copy-start.5 = (f32[3,1024]{1,0:T(4,128)S(1)}, f32[3,1024]{1,0:T(4,128)}, u32[]{:S(2)}) copy-start(f32[3,1024]{1,0:T(4,128)} %pos_ref.3) | copy-start | bytes 36868
  (12 other events, 16.4 us)

commit v2 on v1

v2 whole, which is shorter than its diff:
```python
import functools
import math

import jax
import jax.numpy as jnp
import numpy as np
from jax import lax
from jax.experimental import pallas as pl
from jax.experimental.pallas import tpu as pltpu
from jax.sharding import PartitionSpec as P

TOP = 6
SIDE = 2 * TOP + 1
XY_ROWS = 88
WAVE_ROWS = 2304
DEVICES = 256
ROWS_EACH = WAVE_ROWS // DEVICES
PARTS = (320, 320, 384)
UNROLL = 16
BUFFERS = 4
COS_TERMS = (
    0.999999989059022, -19.7392044994538, 64.93911745989, -85.4501395308031,
    60.1676309503793, -25.9675992464965, 6.52865815867317,
)
VMEM_LIMIT = 60 * 2**20


def wave_layout():
    flat = [(0, 0)] + [(kx, 0) for kx in range(1, TOP + 1)]
    flat += [(kx, ky) for ky in range(1, TOP + 1) for kx in range(-TOP, TOP + 1)]
    codes = np.full((WAVE_ROWS,), -1, np.int32)
    xy = np.zeros((XY_ROWS, 2), np.float32)

    def code(kx, ky, kz):
        return ((kz + TOP) * SIDE + ky + TOP) * SIDE + kx + TOP

    for row, (kx, ky) in enumerate(flat):
        xy[row] = kx, ky
        for kz in range(1, TOP + 1):
            base = (kz - 1) * 4 * XY_ROWS + row
            codes[base] = code(kx, ky, kz)
            codes[base + 2 * XY_ROWS] = code(kx, ky, kz)
            if row > 0:
                codes[base + XY_ROWS] = code(-kx, -ky, kz)
                codes[base + 3 * XY_ROWS] = code(-kx, -ky, kz)
        base = TOP * 4 * XY_ROWS + row
        codes[base] = code(kx, ky, 0)
        if row > 0:
            codes[base + XY_ROWS] = code(kx, ky, 0)
    return xy, codes.reshape(ROWS_EACH, DEVICES)


XY, CODES = wave_layout()


def turn_waves(turns):
    rest = turns - jnp.floor(turns + 0.5)
    quarter = rest - 0.25
    quarter = jnp.where(quarter < -0.5, quarter + 1.0, quarter)

    def cosine(part):
        square = part * part
        total = jnp.full_like(square, COS_TERMS[-1])
        for term in COS_TERMS[-2::-1]:
            total = total * square + term
        return total

    return cosine(rest), cosine(quarter)


def table_tile(xy_ref, pos_ref, first, width):
    wide = (XY_ROWS, width)
    coords = [jnp.broadcast_to(pos_ref[d : d + 1, first : first + width], wide) for d in range(2)]
    flat_turns = (
        jnp.broadcast_to(xy_ref[:, 0:1], wide) * coords[0]
        + jnp.broadcast_to(xy_ref[:, 1:2], wide) * coords[1]
    )
    cos_xy, sin_xy = turn_waves(flat_turns)
    steps = lax.broadcasted_iota(jnp.int32, (8, width), 0).astype(jnp.float32)
    cos_z, sin_z = turn_waves(
        steps * jnp.broadcast_to(pos_ref[2:3, first : first + width], (8, width))
    )
    rows = []
    for kz in range(1, TOP + 1):
        cos_k = jnp.broadcast_to(cos_z[kz : kz + 1], wide)
        sin_k = jnp.broadcast_to(sin_z[kz : kz + 1], wide)
        both_cos, both_sin = cos_xy * cos_k, sin_xy * sin_k
        sin_cos, cos_sin = sin_xy * cos_k, cos_xy * sin_k
        rows += [both_cos - both_sin, both_cos + both_sin, cos_sin + sin_cos, cos_sin - sin_cos]
    rows += [cos_xy, sin_xy, jnp.zeros((WAVE_ROWS - 26 * XY_ROWS, width), jnp.float32)]
    return jnp.concatenate(rows, axis=0).astype(jnp.bfloat16)


def factor_kernel(count_ref, xy_ref, pos_ref, features_ref, sums_ref, table_ref):
    atoms, channels = features_ref.shape
    features = features_ref[...]
    live = lax.broadcasted_iota(jnp.int32, (atoms, channels), 0) < count_ref[0]
    masked = jnp.where(live, features.astype(jnp.float32), 0.0).astype(jnp.bfloat16)
    for first in range(0, atoms, 128):
        table_ref[:, first : first + 128] = table_tile(xy_ref, pos_ref, first, 128)
    for r in range(ROWS_EACH):
        sums_ref[:, r * channels : (r + 1) * channels] = jnp.dot(
            table_ref[r * DEVICES : (r + 1) * DEVICES, :],
            masked,
            preferred_element_type=jnp.float32,
        )


def factor_call(atom_count, positions, features):
    atoms, channels = features.shape
    vmem = pl.BlockSpec(memory_space=pltpu.VMEM)
    return pl.pallas_call(
        factor_kernel,
        in_specs=[pl.BlockSpec(memory_space=pltpu.SMEM), vmem, vmem, vmem],
        out_specs=vmem,
        out_shape=jax.ShapeDtypeStruct((DEVICES, ROWS_EACH * channels), jnp.float32),
        scratch_shapes=[pltpu.VMEM((WAVE_ROWS, atoms), jnp.bfloat16)],
        compiler_params=pltpu.CompilerParams(vmem_limit_bytes=VMEM_LIMIT),
        name="factor_sums",
    )(atom_count, jnp.asarray(XY), positions, features)


def stage_kernel(sums_ref, out_ref):
    total = sums_ref[0]
    for at in range(1, sums_ref.shape[0]):
        total = total + sums_ref[at]
    for at in range(out_ref.shape[0]):
        out_ref[at] = total[at : at + 1]


def stage_call(sums):
    return pl.pallas_call(
        stage_kernel,
        out_shape=jax.ShapeDtypeStruct((sums.shape[1], 1, sums.shape[2]), jnp.float32),
        name="stage_sums",
    )(sums)


def filter_kernel(norm_factor, sums_ref, weight_ref, mix_ref, out_ref):
    channels = mix_ref.shape[0]
    count = sums_ref.shape[0]
    total = sums_ref[0]
    for at in range(1, count):
        total = total + sums_ref[at]
    rows = [total[:, r * channels : (r + 1) * channels] for r in range(ROWS_EACH)]
    rows.append(jnp.zeros((16 - ROWS_EACH, channels), jnp.float32))
    scaled = jnp.concatenate(rows, axis=0) * norm_factor * weight_ref[...]
    mixed = jnp.dot(
        scaled, mix_ref[...], precision=lax.Precision.HIGHEST, preferred_element_type=jnp.float32
    )
    line = jnp.concatenate([mixed[r : r + 1] for r in range(ROWS_EACH)], axis=1)
    for at in range(count):
        out_ref[at] = line


def filter_call(sums, weights, w_mix, norm_factor):
    return pl.pallas_call(
        functools.partial(filter_kernel, norm_factor),
        out_shape=jax.ShapeDtypeStruct(sums.shape, jnp.float32),
        name="filter_rows",
    )(sums, weights, w_mix)


def spread_kernel(rows_ref, out_ref, line_ref):
    for at in range(rows_ref.shape[0]):
        line_ref[at : at + 1, :] = rows_ref[at]
    lines = line_ref[...].astype(jnp.bfloat16)
    for at in range(out_ref.shape[0]):
        out_ref[at] = lines


def spread_call(rows, copies):
    count, _, width = rows.shape
    return pl.pallas_call(
        spread_kernel,
        out_shape=jax.ShapeDtypeStruct((copies, count, width), jnp.bfloat16),
        scratch_shapes=[pltpu.VMEM((count, width), jnp.float32)],
        name="spread_rows",
    )(rows)


def wave_weights(kgrid, k_filter, first):
    kx, ky, kz = kgrid[0], kgrid[1], kgrid[2]
    low = (kz < 0) | ((kz == 0) & ((ky < 0) | ((ky == 0) & (kx < 0))))
    sign = jnp.where(low, -1, 1)
    code = ((kz * sign + TOP) * SIDE + ky * sign + TOP) * SIDE + kx * sign + TOP
    mine = lax.dynamic_slice_in_dim(jnp.asarray(CODES), first, 1, 1)
    mine = jnp.pad(mine, ((0, 16 - ROWS_EACH), (0, 0)), constant_values=-1)
    same = (mine == code[None, :]).astype(jnp.float32)
    return jnp.dot(same, k_filter, precision=lax.Precision.HIGHEST)


def edge_kernel(
    degree, first, ids_ref, basis_ref, features_ref, recv_ref, wb_ref, wo_ref, *refs
):
    blocks, refs = refs[:9], refs[9:]
    (after_ref, out_ref, pool_ref, radial_ref, part_ref, own_ref, wide_ref), refs = refs[:7], refs[7:]
    buffers, arrivals = refs[:BUFFERS], refs[BUFFERS:]
    atoms, channels = out_ref.shape
    del after_ref
    edges = UNROLL * degree
    lines = edges // 128
    chunks = atoms // UNROLL

    def fetch(chunk, at):
        source = ids_ref.at[pl.ds(first * degree // 128 + chunk * lines, lines), :]
        return pltpu.make_async_copy(source, buffers[at], arrivals[at])

    for at in range(BUFFERS):
        fetch(at, at).start()

    slab_even = lax.rem(lax.axis_index("slab"), 2) == 0
    sub_even = lax.rem(lax.axis_index("sub"), 2) == 0
    slab_place = (1, jnp.where(slab_even, 2, 0), jnp.where(slab_even, 0, 2))
    sub_place = (1, jnp.where(sub_even, 2, 0), jnp.where(sub_even, 0, 2))
    for at, block in enumerate(blocks):
        rows = block.shape[0]
        place = pl.multiple_of((slab_place[at // 3] * 3 + sub_place[at % 3]) * rows, rows)
        pool_ref[pl.ds(place, rows), :] = block[...].astype(jnp.float32)

    own_ref[...] = jnp.dot(
        features_ref[first : first + atoms, :], recv_ref[...], preferred_element_type=jnp.float32
    )

    basis_rows = wb_ref.shape[0]
    groups = 128 // basis_rows
    stacked = jnp.concatenate([wb_ref[...].astype(jnp.float32)] * groups, axis=0)
    group_of = lax.broadcasted_iota(jnp.int32, stacked.shape, 0) // basis_rows
    for g in range(groups):
        wide_ref[:, g * channels : (g + 1) * channels] = jnp.where(
            group_of == g, stacked, 0.0
        ).astype(jnp.bfloat16)

    span = groups * 128

    def radial_block(step, carry):
        base = pl.multiple_of(step * span, span)
        values = basis_ref[:, pl.ds(pl.multiple_of(first * degree + base, span), span)]
        values = values.astype(jnp.float32)
        stack = jnp.concatenate([values[:, g * 128 : (g + 1) * 128] for g in range(groups)], axis=0)
        turned = stack.T.astype(jnp.bfloat16)
        for g in range(0, groups, 2):
            both = jnp.dot(
                turned,
                wide_ref[:, g * channels : (g + 2) * channels],
                preferred_element_type=jnp.float32,
            )
            radial_ref[pl.ds(base + g * 128, 128), :] = both[:, :channels]
            radial_ref[pl.ds(base + (g + 1) * 128, 128), :] = both[:, channels:]
        return carry

    lax.fori_loop(0, atoms * degree // span, radial_block, 0)
    sublane = lax.broadcasted_iota(jnp.int32, (8, channels), 0)
    at_sublane = [sublane == r for r in range(8)]

    def some_atoms(chunk, ids):
        own = own_ref.at[pl.ds(pl.multiple_of(chunk * UNROLL, UNROLL), UNROLL), :]
        part = part_ref.at[pl.ds(pl.multiple_of(chunk * UNROLL * 8, UNROLL * 8), UNROLL * 8), :]
        radial = radial_ref.at[pl.ds(pl.multiple_of(chunk * edges, edges), edges), :]
        for u in range(UNROLL):
            mine = jnp.broadcast_to(own[u : u + 1, :], (8, channels))
            total = None
            for edge in range(u * degree, (u + 1) * degree, 8):
                sent = None
                for r in range(8):
                    sender = ids[(edge + r) // 128, (edge + r) % 128]
                    row = jnp.broadcast_to(pool_ref[pl.ds(sender, 1), :], (8, channels))
                    sent = row if sent is None else jnp.where(at_sublane[r], row, sent)
                half = (sent + radial[edge : edge + 8, :] + mine) * 0.5
                hidden = (half + half * jnp.tanh(half)).astype(jnp.bfloat16).astype(jnp.float32)
                total = hidden if total is None else total + hidden
            part[u * 8 : u * 8 + 8, :] = total

    def round_of_chunks(step, carry):
        for at in range(BUFFERS):
            chunk = step * BUFFERS + at
            fetch(chunk, at).wait()
            some_atoms(chunk, buffers[at])
            fetch(jnp.minimum(chunk + BUFFERS, chunks - 1), at).start()
        return carry

    lax.fori_loop(0, chunks // BUFFERS, round_of_chunks, 0)
    for at in range(BUFFERS):
        fetch(chunks - 1, at).wait()
    summed = part_ref[pl.ds(0, atoms, stride=8), :]
    for r in range(1, 8):
        summed = summed + part_ref[pl.ds(r, atoms, stride=8), :]
    high = summed.astype(jnp.bfloat16)
    low = (summed - high.astype(jnp.float32)).astype(jnp.bfloat16)
    message = jnp.dot(high, wo_ref[...], preferred_element_type=jnp.float32) + jnp.dot(
        low, wo_ref[...], preferred_element_type=jnp.float32
    )
    out_ref[...] = message * (1.0 / math.sqrt(degree))


def edge_call(part, after, senders, edge_basis, features, w_recv, w_basis, w_out, blocks):
    channels = features.shape[1]
    degree = senders.shape[0] // features.shape[0]
    atoms, first = PARTS[part], sum(PARTS[:part])
    vmem = pl.BlockSpec(memory_space=pltpu.VMEM)
    rows = sum(block.shape[0] for block in blocks)
    return pl.pallas_call(
        functools.partial(edge_kernel, degree, first),
        in_specs=[vmem] * (6 + len(blocks)) + [pl.BlockSpec(memory_space=pl.ANY)],
        out_specs=vmem,
        out_shape=jax.ShapeDtypeStruct((atoms, channels), jnp.float32),
        scratch_shapes=[
            pltpu.VMEM((rows, channels), jnp.float32),
            pltpu.VMEM((atoms * degree, channels), jnp.float32),
            pltpu.VMEM((atoms * 8, channels), jnp.float32),
            pltpu.VMEM((atoms, channels), jnp.float32),
            pltpu.VMEM((128, 128 // w_basis.shape[0] * channels), jnp.bfloat16),
        ]
        + [pltpu.SMEM((UNROLL * degree // 128, 128), jnp.int32)] * BUFFERS
        + [pltpu.SemaphoreType.DMA] * BUFFERS,
        compiler_params=pltpu.CompilerParams(vmem_limit_bytes=VMEM_LIMIT),
        cost_estimate=pl.CostEstimate(
            flops=8 * 10**9, bytes_accessed=4 * 10**6, transcendentals=10**6
        ),
        name="edge_part_%d" % part,
    )(
        senders.reshape(-1, 128), edge_basis, features, w_recv, w_basis, w_out, *blocks, after
    )


def final_kernel(scale, count_ref, xy_ref, pos_ref, factors_ref, *refs):
    parts, out_ref = refs[:-1], refs[-1]
    channels = out_ref.shape[1]
    factors = jnp.concatenate(
        [factors_ref[:, r * channels : (r + 1) * channels] for r in range(ROWS_EACH)], axis=0
    )
    total, first = out_ref.shape[0], 0
    for part in parts:
        out_ref[first : first + part.shape[0], :] = part[...]
        first += part.shape[0]
    atoms = 256
    for first in range(0, total, atoms):
        table = table_tile(xy_ref, pos_ref, first, atoms)
        field = lax.dot_general(
            factors, table, (((0,), (0,)), ((), ())), preferred_element_type=jnp.float32
        )
        live = first + lax.broadcasted_iota(jnp.int32, (atoms, channels), 0) < count_ref[0]
        near = out_ref[first : first + atoms, :]
        out_ref[first : first + atoms, :] = jnp.where(live, near + field.T * scale, 0.0)


def final_call(atom_count, positions, factors, parts, scale):
    atoms = sum(part.shape[0] for part in parts)
    channels = parts[0].shape[1]
    vmem = pl.BlockSpec(memory_space=pltpu.VMEM)
    return pl.pallas_call(
        functools.partial(final_kernel, scale),
        in_specs=[pl.BlockSpec(memory_space=pltpu.SMEM)] + [vmem] * (3 + len(parts)),
        out_specs=vmem,
        out_shape=jax.ShapeDtypeStruct((atoms, channels), jnp.float32),
        compiler_params=pltpu.CompilerParams(vmem_limit_bytes=VMEM_LIMIT),
        name="updated_rows",
    )(
        atom_count,
        jnp.asarray(XY),
        positions,
        factors,
        *parts,
    )


def moved(array, target):
    slabs, subs = lax.axis_size("slab"), lax.axis_size("sub")
    pairs = []
    for s in range(slabs):
        for b in range(subs):
            to_s, to_b = target(s, b)
            pairs.append((s * subs + b, to_s % slabs * subs + to_b % subs))
    return lax.ppermute(array, ("slab", "sub"), pairs)


def to_core(s, b):
    return s ^ 1, b


def to_outer(s, b):
    return s + (1 if s % 2 else -1), b


def to_column(s, b):
    return s, b ^ 1


def to_beyond(s, b):
    return s, b + (-2 if b % 2 else 2)


def per_device(
    features, positions, atom_count, kgrid, k_filter, w_mix, w_recv, w_send, w_basis, w_out,
    edge_basis, senders,
):
    atoms, channels = features.shape
    total_k = kgrid.shape[1]
    subs, slabs = lax.axis_size("sub"), lax.axis_size("slab")
    send_proj = jnp.dot(features, w_send, preferred_element_type=jnp.float32).astype(jnp.bfloat16)
    outer = moved(send_proj, to_outer)
    near = moved(send_proj, to_column)
    core = moved(send_proj, to_core)
    outer_near = moved(outer, to_column)
    beyond = moved(near, to_beyond)
    core_near = moved(near, to_core)
    outer_beyond = moved(outer_near, to_beyond)
    core_beyond = moved(beyond, to_core)
    blocks = [
        send_proj, near, beyond, core, core_near, core_beyond, outer, outer_near, outer_beyond
    ]

    sums = factor_call(atom_count, positions, features)
    sums = lax.all_to_all(sums, "sub", 0, 0, tiled=True)
    stage_one = stage_call(sums.reshape(subs, slabs, -1))
    sums = lax.all_to_all(stage_one, "slab", 0, 0, tiled=True)
    first = lax.axis_index("sub") * slabs + lax.axis_index("slab")
    weights = wave_weights(kgrid, k_filter, first)
    filtered = filter_call(sums, weights, w_mix, 1.0 / math.sqrt(atoms * DEVICES))
    rows = lax.all_to_all(filtered, "slab", 0, 0, tiled=True)
    spread = spread_call(rows, subs)
    factors = lax.all_to_all(spread.reshape(DEVICES, -1), "sub", 0, 0, tiled=True)

    after = [stage_one, filtered, spread]
    parts = [
        edge_call(p, after[p], senders, edge_basis, features, w_recv, w_basis, w_out, blocks)
        for p in range(len(PARTS))
    ]
    return final_call(atom_count, positions, factors, parts, 4.0 / math.sqrt(total_k))


def solution(mesh):
    placed = (
        P(("slab", "sub"), None),
        P(None, ("slab", "sub")),
        P(("slab", "sub")),
        P(), P(), P(), P(), P(), P(), P(),
        P(None, ("slab", "sub")),
        P(("slab", "sub")),
    )
    return jax.shard_map(
        per_device, mesh=mesh, in_specs=placed, out_specs=P(("slab", "sub"), None), check_vma=False
    )
```

time: 146 us -> 118 us (0.81)
  waiting for transfers between devices: 20.8 us -> 5.5 us
  local copies, waits for them, and re-layouts: 15 us -> 4.58 us
  other arithmetic: 2.96 us -> 0.06 us
  Pallas kernels: 49 us -> 51.8 us
  starting transfers between devices: 54.5 us -> 52.6 us
    ppermute x8, waiting for transfers between devices: 20.8 us -> 5.49 us  [moved(): return lax.ppermute(array, ('slab', 'sub'), pairs)]
    unnamed x52 -> x20, local copies, waits for them, and re-layouts: 11.3 us -> 3.88 us
    ppermute x8, starting transfers between devices: 20.3 us -> 22.6 us  [moved(): return lax.ppermute(array, ('slab', 'sub'), pairs)]
    all_to_all x1, starting transfers between devices: 7.61 us -> 5.43 us  [per_device(): sums = lax.all_to_all(sums, 'sub', 0, 0, tiled=True)]
    all_to_all x3, starting transfers between devices: 26.5 us -> 24.5 us  [the longest x1 9.36 us: per_device(): sums = lax.all_to_all(stage_one, 'slab', 0, 0, tiled=True)]
    all_to_all x1 -> x0, other arithmetic: 1.51 us -> none  [per_device(): spread = lax.all_to_all(filtered, 'slab', 0, 0, tiled=True)]
    pallas_call x4 -> x5, Pallas kernels: 40.4 us -> 40.9 us  [the longest x3 37 us: edge_call(): pl.pallas_call(functools.partial(edge_kernel, degree, first), in_specs=[v...]
  transfers between devices with their start and end apart: 12 -> 12, of which waited for: 1 -> 1; matrix products, arithmetic and copies ran while one was open for 3% -> 2% of each run, Pallas kernels for 28% -> 37%
where the time goes in v2:
time: 118 us
  starting transfers between devices  52.6 us (45%)
  Pallas kernels  51.8 us (44%)
  waiting for transfers between devices  5.5 us (5%)
  local copies, waits for them, and re-layouts  4.58 us (4%)
  matrix products  2.32 us (2%)
    pallas_call x3, Pallas kernels, edge_call(): pl.pallas_call(functools.partial(edge_kernel, degree, first), in_specs=[v...  37 us
    ppermute x8, starting transfers between devices, moved(): return lax.ppermute(array, ('slab', 'sub'), pairs)  22.6 us
    all_to_all x1, starting transfers between devices, per_device(): sums = lax.all_to_all(stage_one, 'slab', 0, 0, tiled=True)  9.36 us
    all_to_all x1, starting transfers between devices, per_device(): rows = lax.all_to_all(filtered, 'slab', 0, 0, tiled=True)  8.29 us
    all_to_all x1, starting transfers between devices, per_device(): lax.all_to_all(spread.reshape(DEVICES, -1), 'sub', 0, 0, tiled=True)  6.89 us
    ppermute x8, waiting for transfers between devices, moved(): return lax.ppermute(array, ('slab', 'sub'), pairs)  5.49 us
    all_to_all x1, starting transfers between devices, per_device(): sums = lax.all_to_all(sums, 'sub', 0, 0, tiled=True)  5.43 us
    pallas_call x1, Pallas kernels, factor_call(): pl.pallas_call(factor_kernel, in_specs=[pl.BlockSpec(memory_space=pltpu.S...  5.02 us
  transfers between devices with their start and end apart: 12, of which 1 were waited for; matrix products, arithmetic and copies ran while one was open for 2% of the time, Pallas kernels for 37%

profile of v2, /device:TPU:1, one launch (start us, length us, event | category | flops | bytes accessed | tf_op | source)
XLA Modules:
  0.0 117.7 jit_solution(5974308777362407942)
XLA Ops:
  0.0 1.3 %convolution_convert_fusion.refs_0_ = bf16[1024,128]{1,0:T(8,128)(2,1)S(1)} fusion(bf16[1024,128]{1,0:T(8,128)(2,1)} %features_ref.7, bf16[128,128]{1,0:T(8,128)(2,1)} %param.21), kind=kOutput, calls=%fused_computation | convolution fusion | flops 33685504 | bytes 557056 | tf_op jit(solution)/shard_map/dot_general | solution.py:400
  1.3 3.8 %collective-permute-start = (bf16[1024,128]{1,0:T(8,128)(2,1)S(1)}, bf16[1024,128]{1,0:T(8,128)(2,1)S(1)}, u32[]{:S(2)}, u32[]{:S(2)}) collective-permute-start(bf16[1024,128]{1,0:T(8,128)(2,1)S(1)} %convolution_convert_fusion.refs_0_), channel_id=1, source_target_pairs={{0,1},{1,0},{2,3},{3,2},{4,5},{5,4},{6,7},{7,6},{8,9},{9,8},{10,11... | collective-permute-start | bytes 786440 | tf_op jit(solution)/shard_map/ppermute | solution.py:374
  5.1 1.2 %collective-permute-start.5 = (bf16[1024,128]{1,0:T(8,128)(2,1)S(1)}, bf16[1024,128]{1,0:T(8,128)(2,1)S(1)}, u32[]{:S(2)}, u32[]{:S(2)}) collective-permute-start(bf16[1024,128]{1,0:T(8,128)(2,1)S(1)} %convolution_convert_fusion.refs_0_), channel_id=1, source_target_pairs={{0,248},{1,249},{2,250},{3,251},{4,252},{5,253},{6,254},{7,255},{8... | collective-permute-start | bytes 786440 | tf_op jit(solution)/shard_map/ppermute | solution.py:374
  7.0 5.0 %factor_sums.1 = f32[256,1152]{1,0:T(8,128)} custom-call(s32[1]{0:T(128)S(6)} %copy.15.count_ref, f32[88,2]{1,0:T(8,128)} %constant.28.clone.xy_ref, f32[3,1024]{1,0:T(4,128)} %pos_ref.3, bf16[1024,128]{1,0:T(8,128)(2,1)} %features_ref.7), custom_call_target="tpu_custom_call" | custom-call | tf_op jit(solution)/shard_map/factor_sums/pallas_call | solution.py:112
  12.0 5.4 %all-to-all-start = ((f32[8,32,1152]{2,1,0:T(8,128)}), f32[8,32,1152]{2,1,0:T(8,128)S(1)}, u32[]{:S(2)}, u32[]{:S(2)}) async-start(f32[8,32,1152]{2,1,0:T(8,128)} %bitcast.9), calls=%async_computation | async-start | bytes 2359296 | tf_op jit(solution)/shard_map/all_to_all | solution.py:414
  17.4 5.2 %collective-permute-start.2 = (bf16[1024,128]{1,0:T(8,128)(2,1)S(1)}, bf16[1024,128]{1,0:T(8,128)(2,1)S(1)}, u32[]{:S(2)}, u32[]{:S(2)}) collective-permute-start(bf16[1024,128]{1,0:T(8,128)(2,1)S(1)} %convolution_convert_fusion.refs_0_), channel_id=1, source_target_pairs={{0,8},{1,9},{2,10},{3,11},{4,12},{5,13},{6,14},{7,15},{8,0},{9,1},... | collective-permute-start | bytes 786440 | tf_op jit(solution)/shard_map/ppermute | solution.py:374
  22.7 1.7 %collective-permute-start.1 = (bf16[1024,128]{1,0:T(8,128)(2,1)S(1)}, bf16[1024,128]{1,0:T(8,128)(2,1)}, u32[]{:S(2)}, u32[]{:S(2)}) collective-permute-start(bf16[1024,128]{1,0:T(8,128)(2,1)S(1)} %collective-permute-done.refs_1_), channel_id=1, source_target_pairs={{0,2},{1,7},{2,4},{3,1},{4,6},{5,3},{6,0},{7,5},{8,10},{9,15},{10,... | collective-permute-start | bytes 786440 | tf_op jit(solution)/shard_map/ppermute | solution.py:374
  24.3 3.9 %collective-permute-start.6 = (bf16[1024,128]{1,0:T(8,128)(2,1)S(1)}, bf16[1024,128]{1,0:T(8,128)(2,1)}, u32[]{:S(2)}, u32[]{:S(2)}) collective-permute-start(bf16[1024,128]{1,0:T(8,128)(2,1)S(1)} %collective-permute-done.5.refs_6_), channel_id=1, source_target_pairs={{0,1},{1,0},{2,3},{3,2},{4,5},{5,4},{6,7},{7,6},{8,9},{9,8},{10,11... | collective-permute-start | bytes 786440 | tf_op jit(solution)/shard_map/ppermute | solution.py:374
  28.3 0.7 constant_dynamic-slice_fusion
  29.7 5.5 %collective-permute-done.1.refs_2_ = bf16[1024,128]{1,0:T(8,128)(2,1)} collective-permute-done((bf16[1024,128]{1,0:T(8,128)(2,1)S(1)}, bf16[1024,128]{1,0:T(8,128)(2,1)}, u32[]{:S(2)}, u32[]{:S(2)}) %collective-permute-start.1) | collective-permute-done | bytes 262176 | tf_op jit(solution)/shard_map/ppermute | solution.py:374
  35.1 6.2 %collective-permute-start.4 = (bf16[1024,128]{1,0:T(8,128)(2,1)}, bf16[1024,128]{1,0:T(8,128)(2,1)}, u32[]{:S(2)}, u32[]{:S(2)}) collective-permute-start(bf16[1024,128]{1,0:T(8,128)(2,1)} %collective-permute-done.1.refs_2_), channel_id=1, source_target_pairs={{0,8},{1,9},{2,10},{3,11},{4,12},{5,13},{6,14},{7,15},{8,0},{9,1},... | collective-permute-start | bytes 786440 | tf_op jit(solution)/shard_map/ppermute | solution.py:374
  41.3 1.1 fusion.weight_ref
  42.4 1.0 copy-done.1
  43.4 2.0 %stage_sums.1.refs_9_ = f32[32,1,1152]{2,1,0:T(1,128)} custom-call(f32[8,32,1152]{2,1,0:T(8,128)} %copy-done.1), custom_call_target="tpu_custom_call" | custom-call | tf_op jit(solution)/shard_map/stage_sums/pallas_call | solution.py:132
  45.4 9.4 %all-to-all-start.1 = ((f32[32,1,1152]{2,1,0:T(1,128)}), f32[32,1,1152]{2,1,0:T(1,128)S(1)}, u32[]{:S(2)}, u32[]{:S(2)}) async-start(f32[32,1,1152]{2,1,0:T(1,128)} %stage_sums.1.refs_9_), calls=%async_computation.1 | async-start | bytes 294912 | tf_op jit(solution)/shard_map/all_to_all | solution.py:416
  55.5 11.8 %edge_part_0.1.refs_0_ = f32[320,128]{1,0:T(8,128)} custom-call(s32[256,128]{1,0:T(8,128)} %bitcast.12, bf16[8,32768]{1,0:T(8,128)(2,1)} %basis_ref.5, bf16[1024,128]{1,0:T(8,128)(2,1)} %features_ref.7, bf16[128,128]{1,0:T(8,128)(2,1)} %recv_ref.5, bf16[8,128]{1,0:T(8,128)(2,1)} %wb_ref.5, bf16[128,128]{1,0:T(8,128)(2,1)} %wo_ref.5, ...), custom_call_target="tpu_custom_call" | custom-call | flops 8000000000 | bytes 4000000 | tf_op jit(solution)/shard_map/edge_part_0/pallas_call | solution.py:302
  68.0 1.8 %filter_rows.1.refs_9_ = f32[32,1,1152]{2,1,0:T(1,128)} custom-call(f32[32,1,1152]{2,1,0:T(1,128)} %copy-done.3, f32[16,128]{1,0:T(8,128)} %fusion.weight_ref, f32[128,128]{1,0:T(8,128)} %mix_ref.1), custom_call_target="tpu_custom_call" | custom-call | tf_op jit(solution)/shard_map/filter_rows/pallas_call | solution.py:157
  69.8 8.3 %all-to-all-start.2 = ((f32[32,1,1152]{2,1,0:T(1,128)}), f32[32,1,1152]{2,1,0:T(1,128)S(1)}, u32[]{:S(2)}, u32[]{:S(2)}) async-start(f32[32,1,1152]{2,1,0:T(1,128)} %filter_rows.1.refs_9_), calls=%async_computation.2 | async-start | bytes 294912 | tf_op jit(solution)/shard_map/all_to_all | solution.py:420
  78.1 11.8 %edge_part_1.1.refs_1_ = f32[320,128]{1,0:T(8,128)} custom-call(s32[256,128]{1,0:T(8,128)} %bitcast.13, bf16[8,32768]{1,0:T(8,128)(2,1)} %basis_ref.5, bf16[1024,128]{1,0:T(8,128)(2,1)} %features_ref.7, bf16[128,128]{1,0:T(8,128)(2,1)} %recv_ref.5, bf16[8,128]{1,0:T(8,128)(2,1)} %wb_ref.5, bf16[128,128]{1,0:T(8,128)(2,1)} %wo_ref.5, ...), custom_call_target="tpu_custom_call" | custom-call | flops 8000000000 | bytes 4000000 | tf_op jit(solution)/shard_map/edge_part_1/pallas_call | solution.py:302
  90.6 1.8 %spread_rows.1.refs_9_ = bf16[8,32,1152]{2,1,0:T(8,128)(2,1)} custom-call(f32[32,1,1152]{2,1,0:T(1,128)} %copy-done.4), custom_call_target="tpu_custom_call" | custom-call | tf_op jit(solution)/shard_map/spread_rows/pallas_call | solution.py:174
  92.4 6.9 %all-to-all-start.3 = ((bf16[8,32,1152]{2,1,0:T(8,128)(2,1)}), bf16[8,32,1152]{2,1,0:T(8,128)(2,1)S(1)}, u32[]{:S(2)}, u32[]{:S(2)}) async-start(bf16[8,32,1152]{2,1,0:T(8,128)(2,1)} %spread_rows.1.refs_9_), calls=%async_computation.3 | async-start | bytes 1179648 | tf_op jit(solution)/shard_map/all_to_all | solution.py:422
  99.3 13.4 %edge_part_2.1.refs_2_ = f32[384,128]{1,0:T(8,128)} custom-call(s32[256,128]{1,0:T(8,128)} %bitcast.14, bf16[8,32768]{1,0:T(8,128)(2,1)} %basis_ref.5, bf16[1024,128]{1,0:T(8,128)(2,1)} %features_ref.7, bf16[128,128]{1,0:T(8,128)(2,1)} %recv_ref.5, bf16[8,128]{1,0:T(8,128)(2,1)} %wb_ref.5, bf16[128,128]{1,0:T(8,128)(2,1)} %wo_ref.5, ...), custom_call_target="tpu_custom_call" | custom-call | flops 8000000000 | bytes 4000000 | tf_op jit(solution)/shard_map/edge_part_2/pallas_call | solution.py:302
  112.8 0.8 copy-done.2
  113.6 4.1 %updated_rows.1 = f32[1024,128]{1,0:T(8,128)} custom-call(s32[1]{0:T(128)S(6)} %copy.15.count_ref, f32[88,2]{1,0:T(8,128)} %constant.28.clone.xy_ref, f32[3,1024]{1,0:T(4,128)} %pos_ref.3, bf16[256,1152]{1,0:T(8,128)(2,1)} %bitcast.10, f32[320,128]{1,0:T(8,128)} %edge_part_0.1.refs_0_, f32[320,128]{1,0:T(8,128)} %edge_part_1.1.refs_1_, ...), custom_call_target="tpu_custom_call" | custom-call | tf_op jit(solution)/shard_map/updated_rows/pallas_call | solution.py:351
  (33 shorter events, 2.7 us)
Async XLA Ops:
  0.0 41.3 %copy-start = (f32[2048,128]{1,0:T(8,128)S(1)}, f32[2048,128]{1,0:T(8,128)}, u32[]{:S(2)}) copy-start(f32[2048,128]{1,0:T(8,128)} %param.18) | copy-start | bytes 3145732
  1.3 16.2 %copy-start.5 = (bf16[1024,128]{1,0:T(8,128)(2,1)}, bf16[1024,128]{1,0:T(8,128)(2,1)S(1)}, u32[]{:S(2)}) copy-start(bf16[1024,128]{1,0:T(8,128)(2,1)S(1)} %convolution_convert_fusion.refs_0_) | copy-start | bytes 786436
  1.3 21.4 %collective-permute-start = (bf16[1024,128]{1,0:T(8,128)(2,1)S(1)}, bf16[1024,128]{1,0:T(8,128)(2,1)S(1)}, u32[]{:S(2)}, u32[]{:S(2)}) collective-permute-start(bf16[1024,128]{1,0:T(8,128)(2,1)S(1)} %convolution_convert_fusion.refs_0_), channel_id=1, source_target_pairs={{0,1},{1,0},{2,3},{3,2},{4,5},{5,4},{6,7},{7,6},{8,9},{9,8},{10,11... | collective-permute-start | bytes 786440 | tf_op jit(solution)/shard_map/ppermute | solution.py:374
  5.1 19.2 %collective-permute-start.5 = (bf16[1024,128]{1,0:T(8,128)(2,1)S(1)}, bf16[1024,128]{1,0:T(8,128)(2,1)S(1)}, u32[]{:S(2)}, u32[]{:S(2)}) collective-permute-start(bf16[1024,128]{1,0:T(8,128)(2,1)S(1)} %convolution_convert_fusion.refs_0_), channel_id=1, source_target_pairs={{0,248},{1,249},{2,250},{3,251},{4,252},{5,253},{6,254},{7,255},{8... | collective-permute-start | bytes 786440 | tf_op jit(solution)/shard_map/ppermute | solution.py:374
  12.0 16.2 %copy-start.6 = (s32[3,2048]{1,0:T(4,128)S(1)}, s32[3,2048]{1,0:T(4,128)}, u32[]{:S(2)}) copy-start(s32[3,2048]{1,0:T(4,128)} %param.17) | copy-start | bytes 73732
  12.0 30.4 %all-to-all-start = ((f32[8,32,1152]{2,1,0:T(8,128)}), f32[8,32,1152]{2,1,0:T(8,128)S(1)}, u32[]{:S(2)}, u32[]{:S(2)}) async-start(f32[8,32,1152]{2,1,0:T(8,128)} %bitcast.9), calls=%async_computation | async-start | bytes 2359296 | tf_op jit(solution)/shard_map/all_to_all | solution.py:414
  17.4 37.3 %collective-permute-start.2 = (bf16[1024,128]{1,0:T(8,128)(2,1)S(1)}, bf16[1024,128]{1,0:T(8,128)(2,1)S(1)}, u32[]{:S(2)}, u32[]{:S(2)}) collective-permute-start(bf16[1024,128]{1,0:T(8,128)(2,1)S(1)} %convolution_convert_fusion.refs_0_), channel_id=1, source_target_pairs={{0,8},{1,9},{2,10},{3,11},{4,12},{5,13},{6,14},{7,15},{8,0},{9,1},... | collective-permute-start | bytes 786440 | tf_op jit(solution)/shard_map/ppermute | solution.py:374
  22.7 22.7 %copy-start.7 = (bf16[1024,128]{1,0:T(8,128)(2,1)}, bf16[1024,128]{1,0:T(8,128)(2,1)S(1)}, u32[]{:S(2)}) copy-start(bf16[1024,128]{1,0:T(8,128)(2,1)S(1)} %collective-permute-done.refs_1_) | copy-start | bytes 786436
  22.7 12.5 %collective-permute-start.1 = (bf16[1024,128]{1,0:T(8,128)(2,1)S(1)}, bf16[1024,128]{1,0:T(8,128)(2,1)}, u32[]{:S(2)}, u32[]{:S(2)}) collective-permute-start(bf16[1024,128]{1,0:T(8,128)(2,1)S(1)} %collective-permute-done.refs_1_), channel_id=1, source_target_pairs={{0,2},{1,7},{2,4},{3,1},{4,6},{5,3},{6,0},{7,5},{8,10},{9,15},{10,... | collective-permute-start | bytes 786440 | tf_op jit(solution)/shard_map/ppermute | solution.py:374
  24.3 21.1 %copy-start.8 = (bf16[1024,128]{1,0:T(8,128)(2,1)}, bf16[1024,128]{1,0:T(8,128)(2,1)S(1)}, u32[]{:S(2)}) copy-start(bf16[1024,128]{1,0:T(8,128)(2,1)S(1)} %collective-permute-done.5.refs_6_) | copy-start | bytes 786436
  24.3 16.9 %collective-permute-start.6 = (bf16[1024,128]{1,0:T(8,128)(2,1)S(1)}, bf16[1024,128]{1,0:T(8,128)(2,1)}, u32[]{:S(2)}, u32[]{:S(2)}) collective-permute-start(bf16[1024,128]{1,0:T(8,128)(2,1)S(1)} %collective-permute-done.5.refs_6_), channel_id=1, source_target_pairs={{0,1},{1,0},{2,3},{3,2},{4,5},{5,4},{6,7},{7,6},{8,9},{9,8},{10,11... | collective-permute-start | bytes 786440 | tf_op jit(solution)/shard_map/ppermute | solution.py:374
  29.0 25.8 %collective-permute-start.3 = (bf16[1024,128]{1,0:T(8,128)(2,1)S(1)}, bf16[1024,128]{1,0:T(8,128)(2,1)}, u32[]{:S(2)}, u32[]{:S(2)}) collective-permute-start(bf16[1024,128]{1,0:T(8,128)(2,1)S(1)} %collective-permute-done.refs_1_), channel_id=1, source_target_pairs={{0,8},{1,9},{2,10},{3,11},{4,12},{5,13},{6,14},{7,15},{8,0},{9,1},... | collective-permute-start | bytes 786440 | tf_op jit(solution)/shard_map/ppermute | solution.py:374
  35.1 19.7 %collective-permute-start.4 = (bf16[1024,128]{1,0:T(8,128)(2,1)}, bf16[1024,128]{1,0:T(8,128)(2,1)}, u32[]{:S(2)}, u32[]{:S(2)}) collective-permute-start(bf16[1024,128]{1,0:T(8,128)(2,1)} %collective-permute-done.1.refs_2_), channel_id=1, source_target_pairs={{0,8},{1,9},{2,10},{3,11},{4,12},{5,13},{6,14},{7,15},{8,0},{9,1},... | collective-permute-start | bytes 786440 | tf_op jit(solution)/shard_map/ppermute | solution.py:374
  41.3 13.5 %collective-permute-start.7 = (bf16[1024,128]{1,0:T(8,128)(2,1)}, bf16[1024,128]{1,0:T(8,128)(2,1)}, u32[]{:S(2)}, u32[]{:S(2)}) collective-permute-start(bf16[1024,128]{1,0:T(8,128)(2,1)} %collective-permute-done.6.refs_7_), channel_id=1, source_target_pairs={{0,2},{1,7},{2,4},{3,1},{4,6},{5,3},{6,0},{7,5},{8,10},{9,15},{10,... | collective-permute-start | bytes 786440 | tf_op jit(solution)/shard_map/ppermute | solution.py:374
  42.4 1.0 copy-start.1
  45.4 21.9 %all-to-all-start.1 = ((f32[32,1,1152]{2,1,0:T(1,128)}), f32[32,1,1152]{2,1,0:T(1,128)S(1)}, u32[]{:S(2)}, u32[]{:S(2)}) async-start(f32[32,1,1152]{2,1,0:T(1,128)} %stage_sums.1.refs_9_), calls=%async_computation.1 | async-start | bytes 294912 | tf_op jit(solution)/shard_map/all_to_all | solution.py:416
  54.8 0.7 copy-start.9
  67.3 0.7 copy-start.3
  69.8 20.1 %all-to-all-start.2 = ((f32[32,1,1152]{2,1,0:T(1,128)}), f32[32,1,1152]{2,1,0:T(1,128)S(1)}, u32[]{:S(2)}, u32[]{:S(2)}) async-start(f32[32,1,1152]{2,1,0:T(1,128)} %filter_rows.1.refs_9_), calls=%async_computation.2 | async-start | bytes 294912 | tf_op jit(solution)/shard_map/all_to_all | solution.py:420
  89.9 0.7 copy-start.4
  92.4 20.3 %all-to-all-start.3 = ((bf16[8,32,1152]{2,1,0:T(8,128)(2,1)}), bf16[8,32,1152]{2,1,0:T(8,128)(2,1)S(1)}, u32[]{:S(2)}, u32[]{:S(2)}) async-start(bf16[8,32,1152]{2,1,0:T(8,128)(2,1)} %spread_rows.1.refs_9_), calls=%async_computation.3 | async-start | bytes 1179648 | tf_op jit(solution)/shard_map/all_to_all | solution.py:422
  112.8 0.8 copy-start.2

commit v3 on v2

--- a/solution.py
+++ b/solution.py
@@ -15,14 +15,15 @@
 WAVE_ROWS = 2304
 DEVICES = 256
 ROWS_EACH = WAVE_ROWS // DEVICES
-PARTS = (320, 320, 384)
+PARTS = (256, 256, 512)
+PLANE = 4
 UNROLL = 16
 BUFFERS = 4
 COS_TERMS = (
     0.999999989059022, -19.7392044994538, 64.93911745989, -85.4501395308031,
     60.1676309503793, -25.9675992464965, 6.52865815867317,
 )
-VMEM_LIMIT = 60 * 2**20
+SMALL_VMEM, TABLE_VMEM, LARGE_VMEM = 6 * 2**20, 14 * 2**20, 60 * 2**20
 
 
 def wave_layout():
@@ -91,13 +92,43 @@
     return jnp.concatenate(rows, axis=0).astype(jnp.bfloat16)
 
 
-def factor_kernel(count_ref, xy_ref, pos_ref, features_ref, sums_ref, table_ref):
+def hbm():
+    return pl.BlockSpec(memory_space=pltpu.HBM)
+
+
+def vmem():
+    return pl.BlockSpec(memory_space=pltpu.VMEM)
+
+
+def limit(size):
+    return pltpu.CompilerParams(vmem_limit_bytes=size)
+
+
+def loads(sources, targets, arrivals):
+    copies = [
+        pltpu.make_async_copy(source, target, arrivals.at[at])
+        for at, (source, target) in enumerate(zip(sources, targets))
+    ]
+    for copy in copies:
+        copy.start()
+    return copies
+
+
+def factor_kernel(
+    count_ref, xy_hbm, pos_hbm, features_hbm, *refs
+):
+    after_refs, refs = refs[:-6], refs[-6:]
+    sums_ref, table_ref, xy_ref, pos_ref, features_ref, arrivals = refs
+    del after_refs
+    copies = loads((xy_hbm, pos_hbm, features_hbm), (xy_ref, pos_ref, features_ref), arrivals)
     atoms, channels = features_ref.shape
-    features = features_ref[...]
-    live = lax.broadcasted_iota(jnp.int32, (atoms, channels), 0) < count_ref[0]
-    masked = jnp.where(live, features.astype(jnp.float32), 0.0).astype(jnp.bfloat16)
+    copies[0].wait()
+    copies[1].wait()
     for first in range(0, atoms, 128):
         table_ref[:, first : first + 128] = table_tile(xy_ref, pos_ref, first, 128)
+    copies[2].wait()
+    live = lax.broadcasted_iota(jnp.int32, (atoms, channels), 0) < count_ref[0]
+    masked = jnp.where(live, features_ref[...].astype(jnp.float32), 0.0).astype(jnp.bfloat16)
     for r in range(ROWS_EACH):
         sums_ref[:, r * channels : (r + 1) * channels] = jnp.dot(
             table_ref[r * DEVICES : (r + 1) * DEVICES, :],
@@ -106,121 +137,140 @@
         )
 
 
-def factor_call(atom_count, positions, features):
+def factor_call(atom_count, positions, features, after):
     atoms, channels = features.shape
-    vmem = pl.BlockSpec(memory_space=pltpu.VMEM)
     return pl.pallas_call(
         factor_kernel,
-        in_specs=[pl.BlockSpec(memory_space=pltpu.SMEM), vmem, vmem, vmem],
-        out_specs=vmem,
+        in_specs=[pl.BlockSpec(memory_space=pltpu.SMEM), hbm(), hbm(), hbm()]
+        + [pl.BlockSpec(memory_space=pl.ANY)] * len(after),
+        out_specs=vmem(),
         out_shape=jax.ShapeDtypeStruct((DEVICES, ROWS_EACH * channels), jnp.float32),
-        scratch_shapes=[pltpu.VMEM((WAVE_ROWS, atoms), jnp.bfloat16)],
-        compiler_params=pltpu.CompilerParams(vmem_limit_bytes=VMEM_LIMIT),
+        scratch_shapes=[
+            pltpu.VMEM((WAVE_ROWS, atoms), jnp.bfloat16),
+            pltpu.VMEM(XY.shape, jnp.float32),
+            pltpu.VMEM(positions.shape, jnp.float32),
+            pltpu.VMEM(features.shape, jnp.bfloat16),
+            pltpu.SemaphoreType.DMA((3,)),
+        ],
+        compiler_params=limit(LARGE_VMEM),
         name="factor_sums",
-    )(atom_count, jnp.asarray(XY), positions, features)
+    )(atom_count, jnp.asarray(XY), positions, features, *after)
 
 
 def stage_kernel(sums_ref, out_ref):
+    rows = out_ref.shape[1]
+    total = sums_ref[0:rows, :]
+    for at in range(rows, sums_ref.shape[0], rows):
+        total = total + sums_ref[at : at + rows, :]
+    for at in range(out_ref.shape[0]):
+        out_ref[at] = total
+
+
+def stage_call(sums, sources, copies):
+    return pl.pallas_call(
+        stage_kernel,
+        out_specs=vmem(),
+        out_shape=jax.ShapeDtypeStruct(
+            (copies, sums.shape[0] // sources, sums.shape[1]), jnp.float32
+        ),
+        compiler_params=limit(SMALL_VMEM),
+        name="stage_sums",
+    )(sums)
+
+
+def filter_kernel(norm_factor, sums_ref, weight_ref, mix_hbm, out_ref, mix_ref, arrivals):
+    copies = loads((mix_hbm,), (mix_ref,), arrivals)
+    channels = mix_ref.shape[0]
     total = sums_ref[0]
     for at in range(1, sums_ref.shape[0]):
         total = total + sums_ref[at]
-    for at in range(out_ref.shape[0]):
-        out_ref[at] = total[at : at + 1]
-
-
-def stage_call(sums):
-    return pl.pallas_call(
-        stage_kernel,
-        out_shape=jax.ShapeDtypeStruct((sums.shape[1], 1, sums.shape[2]), jnp.float32),
-        name="stage_sums",
-    )(sums)
-
-
-def filter_kernel(norm_factor, sums_ref, weight_ref, mix_ref, out_ref):
-    channels = mix_ref.shape[0]
-    count = sums_ref.shape[0]
-    total = sums_ref[0]
-    for at in range(1, count):
-        total = total + sums_ref[at]
-    rows = [total[:, r * channels : (r + 1) * channels] for r in range(ROWS_EACH)]
-    rows.append(jnp.zeros((16 - ROWS_EACH, channels), jnp.float32))
-    scaled = jnp.concatenate(rows, axis=0) * norm_factor * weight_ref[...]
+    count = total.shape[0]
+    scaled = jnp.concatenate(
+        [total[:, r * channels : (r + 1) * channels] for r in range(ROWS_EACH)], axis=0
+    )
+    scaled = scaled * norm_factor * weight_ref[...]
+    copies[0].wait()
     mixed = jnp.dot(
         scaled, mix_ref[...], precision=lax.Precision.HIGHEST, preferred_element_type=jnp.float32
     )
-    line = jnp.concatenate([mixed[r : r + 1] for r in range(ROWS_EACH)], axis=1)
-    for at in range(count):
-        out_ref[at] = line
-
-
-def filter_call(sums, weights, w_mix, norm_factor):
+    lines = jnp.concatenate(
+        [mixed[r * count : (r + 1) * count] for r in range(ROWS_EACH)], axis=1
+    ).astype(jnp.bfloat16)
+    for at in range(out_ref.shape[0]):
+        out_ref[at] = lines
+
+
+def filter_call(sums, weights, w_mix, norm_factor, copies):
     return pl.pallas_call(
         functools.partial(filter_kernel, norm_factor),
-        out_shape=jax.ShapeDtypeStruct(sums.shape, jnp.float32),
+        in_specs=[vmem(), vmem(), hbm()],
+        out_specs=vmem(),
+        out_shape=jax.ShapeDtypeStruct((copies,) + sums.shape[1:], jnp.bfloat16),
+        scratch_shapes=[pltpu.VMEM(w_mix.shape, jnp.float32), pltpu.SemaphoreType.DMA((1,))],
+        compiler_params=limit(SMALL_VMEM),
         name="filter_rows",
     )(sums, weights, w_mix)
 
 
-def spread_kernel(rows_ref, out_ref, line_ref):
-    for at in range(rows_ref.shape[0]):
-        line_ref[at : at + 1, :] = rows_ref[at]
-    lines = line_ref[...].astype(jnp.bfloat16)
-    for at in range(out_ref.shape[0]):
-        out_ref[at] = lines
-
-
-def spread_call(rows, copies):
-    count, _, width = rows.shape
-    return pl.pallas_call(
-        spread_kernel,
-        out_shape=jax.ShapeDtypeStruct((copies, count, width), jnp.bfloat16),
-        scratch_shapes=[pltpu.VMEM((count, width), jnp.float32)],
-        name="spread_rows",
-    )(rows)
-
-
-def wave_weights(kgrid, k_filter, first):
+def wave_weights(kgrid, k_filter, first, count):
     kx, ky, kz = kgrid[0], kgrid[1], kgrid[2]
     low = (kz < 0) | ((kz == 0) & ((ky < 0) | ((ky == 0) & (kx < 0))))
     sign = jnp.where(low, -1, 1)
     code = ((kz * sign + TOP) * SIDE + ky * sign + TOP) * SIDE + kx * sign + TOP
-    mine = lax.dynamic_slice_in_dim(jnp.asarray(CODES), first, 1, 1)
-    mine = jnp.pad(mine, ((0, 16 - ROWS_EACH), (0, 0)), constant_values=-1)
-    same = (mine == code[None, :]).astype(jnp.float32)
+    mine = lax.dynamic_slice_in_dim(jnp.asarray(CODES), first, count, 1).reshape(-1)
+    same = (mine[:, None] == code[None, :]).astype(jnp.float32)
     return jnp.dot(same, k_filter, precision=lax.Precision.HIGHEST)
 
 
 def edge_kernel(
-    degree, first, ids_ref, basis_ref, features_ref, recv_ref, wb_ref, wo_ref, *refs
+    degree, first, ids_hbm, basis_hbm, features_hbm, recv_hbm, wb_hbm, wo_hbm, *refs
 ):
-    blocks, refs = refs[:9], refs[9:]
+    blocks, refs = refs[:7], refs[7:]
     (after_ref, out_ref, pool_ref, radial_ref, part_ref, own_ref, wide_ref), refs = refs[:7], refs[7:]
+    local, loaded, refs = refs[:6], refs[6], refs[7:]
+    ids_ref, basis_ref, features_ref, recv_ref, wb_ref, wo_ref = local
     buffers, arrivals = refs[:BUFFERS], refs[BUFFERS:]
     atoms, channels = out_ref.shape
     del after_ref
+    copies = loads(
+        (
+            ids_hbm.at[pl.ds(first * degree // 128, atoms * degree // 128), :],
+            basis_hbm.at[:, pl.ds(first * degree, atoms * degree)],
+            features_hbm.at[pl.ds(first, atoms), :],
+            recv_hbm,
+            wb_hbm,
+            wo_hbm,
+        ),
+        local,
+        loaded,
+    )
     edges = UNROLL * degree
     lines = edges // 128
     chunks = atoms // UNROLL
 
     def fetch(chunk, at):
-        source = ids_ref.at[pl.ds(first * degree // 128 + chunk * lines, lines), :]
+        source = ids_ref.at[pl.ds(chunk * lines, lines), :]
         return pltpu.make_async_copy(source, buffers[at], arrivals[at])
-
-    for at in range(BUFFERS):
-        fetch(at, at).start()
 
     slab_even = lax.rem(lax.axis_index("slab"), 2) == 0
     sub_even = lax.rem(lax.axis_index("sub"), 2) == 0
     slab_place = (1, jnp.where(slab_even, 2, 0), jnp.where(slab_even, 0, 2))
     sub_place = (1, jnp.where(sub_even, 2, 0), jnp.where(sub_even, 0, 2))
-    for at, block in enumerate(blocks):
-        rows = block.shape[0]
-        place = pl.multiple_of((slab_place[at // 3] * 3 + sub_place[at % 3]) * rows, rows)
-        pool_ref[pl.ds(place, rows), :] = block[...].astype(jnp.float32)
-
-    own_ref[...] = jnp.dot(
-        features_ref[first : first + atoms, :], recv_ref[...], preferred_element_type=jnp.float32
-    )
+    rows = blocks[0].shape[0]
+    at = 0
+    for block in blocks:
+        for first_row in range(0, block.shape[0], rows):
+            place = pl.multiple_of((slab_place[at // 3] * 3 + sub_place[at % 3]) * rows, rows)
+            pool_ref[pl.ds(place, rows), :] = block[first_row : first_row + rows, :].astype(
+                jnp.float32
+            )
+            at += 1
+
+    for copy in copies:
+        copy.wait()
+    for at in range(BUFFERS):
+        fetch(at, at).start()
+    own_ref[...] = jnp.dot(features_ref[...], recv_ref[...], preferred_element_type=jnp.float32)
 
     basis_rows = wb_ref.shape[0]
     groups = 128 // basis_rows
@@ -235,7 +285,7 @@
 
     def radial_block(step, carry):
         base = pl.multiple_of(step * span, span)
-        values = basis_ref[:, pl.ds(pl.multiple_of(first * degree + base, span), span)]
+        values = basis_ref[:, pl.ds(base, span)]
         values = values.astype(jnp.float32)
         stack = jnp.concatenate([values[:, g * 128 : (g + 1) * 128] for g in range(groups)], axis=0)
         turned = stack.T.astype(jnp.bfloat16)
@@ -297,12 +347,11 @@
     channels = features.shape[1]
     degree = senders.shape[0] // features.shape[0]
     atoms, first = PARTS[part], sum(PARTS[:part])
-    vmem = pl.BlockSpec(memory_space=pltpu.VMEM)
     rows = sum(block.shape[0] for block in blocks)
     return pl.pallas_call(
         functools.partial(edge_kernel, degree, first),
-        in_specs=[vmem] * (6 + len(blocks)) + [pl.BlockSpec(memory_space=pl.ANY)],
-        out_specs=vmem,
+        in_specs=[hbm()] * 6 + [vmem()] * len(blocks) + [pl.BlockSpec(memory_space=pl.ANY)],
+        out_specs=vmem(),
         out_shape=jax.ShapeDtypeStruct((atoms, channels), jnp.float32),
         scratch_shapes=[
             pltpu.VMEM((rows, channels), jnp.float32),
@@ -310,10 +359,17 @@
             pltpu.VMEM((atoms * 8, channels), jnp.float32),
             pltpu.VMEM((atoms, channels), jnp.float32),
             pltpu.VMEM((128, 128 // w_basis.shape[0] * channels), jnp.bfloat16),
+            pltpu.VMEM((atoms * degree // 128, 128), jnp.int32),
+            pltpu.VMEM((edge_basis.shape[0], atoms * degree), jnp.bfloat16),
+            pltpu.VMEM((atoms, channels), jnp.bfloat16),
+            pltpu.VMEM(w_recv.shape, jnp.bfloat16),
+            pltpu.VMEM(w_basis.shape, jnp.bfloat16),
+            pltpu.VMEM(w_out.shape, jnp.bfloat16),
+            pltpu.SemaphoreType.DMA((6,)),
         ]
         + [pltpu.SMEM((UNROLL * degree // 128, 128), jnp.int32)] * BUFFERS
         + [pltpu.SemaphoreType.DMA] * BUFFERS,
-        compiler_params=pltpu.CompilerParams(vmem_limit_bytes=VMEM_LIMIT),
+        compiler_params=limit(LARGE_VMEM),
         cost_estimate=pl.CostEstimate(
             flops=8 * 10**9, bytes_accessed=4 * 10**6, transcendentals=10**6
         ),
@@ -323,22 +379,23 @@
     )
 
 
-def final_kernel(scale, count_ref, xy_ref, pos_ref, factors_ref, *refs):
-    parts, out_ref = refs[:-1], refs[-1]
+def final_kernel(scale, count_ref, xy_hbm, pos_hbm, factors_ref, *refs):
+    parts, (out_ref, xy_ref, pos_ref, arrivals) = refs[:-4], refs[-4:]
+    copies = loads((xy_hbm, pos_hbm), (xy_ref, pos_ref), arrivals)
     channels = out_ref.shape[1]
     factors = jnp.concatenate(
         [factors_ref[:, r * channels : (r + 1) * channels] for r in range(ROWS_EACH)], axis=0
-    )
+    ).T
     total, first = out_ref.shape[0], 0
     for part in parts:
         out_ref[first : first + part.shape[0], :] = part[...]
         first += part.shape[0]
+    for copy in copies:
+        copy.wait()
     atoms = 256
     for first in range(0, total, atoms):
         table = table_tile(xy_ref, pos_ref, first, atoms)
-        field = lax.dot_general(
-            factors, table, (((0,), (0,)), ((), ())), preferred_element_type=jnp.float32
-        )
+        field = jnp.dot(factors, table, preferred_element_type=jnp.float32)
         live = first + lax.broadcasted_iota(jnp.int32, (atoms, channels), 0) < count_ref[0]
         near = out_ref[first : first + atoms, :]
         out_ref[first : first + atoms, :] = jnp.where(live, near + field.T * scale, 0.0)
@@ -347,21 +404,20 @@
 def final_call(atom_count, positions, factors, parts, scale):
     atoms = sum(part.shape[0] for part in parts)
     channels = parts[0].shape[1]
-    vmem = pl.BlockSpec(memory_space=pltpu.VMEM)
     return pl.pallas_call(
         functools.partial(final_kernel, scale),
-        in_specs=[pl.BlockSpec(memory_space=pltpu.SMEM)] + [vmem] * (3 + len(parts)),
-        out_specs=vmem,
+        in_specs=[pl.BlockSpec(memory_space=pltpu.SMEM), hbm(), hbm(), vmem()]
+        + [vmem()] * len(parts),
+        out_specs=vmem(),
         out_shape=jax.ShapeDtypeStruct((atoms, channels), jnp.float32),
-        compiler_params=pltpu.CompilerParams(vmem_limit_bytes=VMEM_LIMIT),
+        scratch_shapes=[
+            pltpu.VMEM(XY.shape, jnp.float32),
+            pltpu.VMEM(positions.shape, jnp.float32),
+            pltpu.SemaphoreType.DMA((2,)),
+        ],
+        compiler_params=limit(TABLE_VMEM),
         name="updated_rows",
-    )(
-        atom_count,
-        jnp.asarray(XY),
-        positions,
-        factors,
-        *parts,
-    )
+    )(atom_count, jnp.asarray(XY), positions, factors, *parts)
 
 
 def moved(array, target):
@@ -387,7 +443,26 @@
 
 
 def to_beyond(s, b):
-    return s, b + (-2 if b % 2 else 2)
+    return s, b + (-1 if b % 2 == 0 else 1)
+
+
+def plane_groups(slabs, subs):
+    return [
+        [(z * PLANE + q) * subs + b for b in range(subs) for q in range(PLANE)]
+        for z in range(slabs // PLANE)
+    ]
+
+
+def line_groups(slabs, subs):
+    return [
+        [(z * PLANE + q) * subs + b for z in range(slabs // PLANE)]
+        for b in range(subs)
+        for q in range(PLANE)
+    ]
+
+
+def exchanged(array, groups):
+    return lax.all_to_all(array, ("slab", "sub"), 0, 0, axis_index_groups=groups, tiled=True)
 
 
 def per_device(
@@ -400,28 +475,25 @@
     send_proj = jnp.dot(features, w_send, preferred_element_type=jnp.float32).astype(jnp.bfloat16)
     outer = moved(send_proj, to_outer)
     near = moved(send_proj, to_column)
-    core = moved(send_proj, to_core)
-    outer_near = moved(outer, to_column)
-    beyond = moved(near, to_beyond)
-    core_near = moved(near, to_core)
-    outer_beyond = moved(outer_near, to_beyond)
-    core_beyond = moved(beyond, to_core)
-    blocks = [
-        send_proj, near, beyond, core, core_near, core_beyond, outer, outer_near, outer_beyond
-    ]
-
-    sums = factor_call(atom_count, positions, features)
-    sums = lax.all_to_all(sums, "sub", 0, 0, tiled=True)
-    stage_one = stage_call(sums.reshape(subs, slabs, -1))
-    sums = lax.all_to_all(stage_one, "slab", 0, 0, tiled=True)
-    first = lax.axis_index("sub") * slabs + lax.axis_index("slab")
-    weights = wave_weights(kgrid, k_filter, first)
-    filtered = filter_call(sums, weights, w_mix, 1.0 / math.sqrt(atoms * DEVICES))
-    rows = lax.all_to_all(filtered, "slab", 0, 0, tiled=True)
-    spread = spread_call(rows, subs)
-    factors = lax.all_to_all(spread.reshape(DEVICES, -1), "sub", 0, 0, tiled=True)
-
-    after = [stage_one, filtered, spread]
+    beyond = moved(send_proj, to_beyond)
+    outer_near = moved(send_proj, lambda s, b: to_outer(*to_column(s, b)))
+    outer_beyond = moved(send_proj, lambda s, b: to_outer(*to_beyond(s, b)))
+    core = moved(jnp.concatenate([send_proj, near, beyond]), to_core)
+    blocks = [send_proj, near, beyond, core, outer, outer_near, outer_beyond]
+
+    plane, line = plane_groups(slabs, subs), line_groups(slabs, subs)
+    mine = lax.axis_index("sub") * PLANE + lax.axis_index("slab") % PLANE
+    sums = factor_call(atom_count, positions, features, ())
+    stage_one = stage_call(exchanged(sums, plane), len(plane[0]), len(line[0]))
+    count = stage_one.shape[1]
+    weights = wave_weights(kgrid, k_filter, mine * count, count)
+    norm_factor = 1.0 / math.sqrt(atoms * DEVICES)
+    filtered = filter_call(
+        exchanged(stage_one, line), weights, w_mix, norm_factor, len(plane[0])
+    )
+    factors = exchanged(filtered, plane).reshape(DEVICES, -1)
+
+    after = [sums, stage_one, filtered]
     parts = [
         edge_call(p, after[p], senders, edge_basis, features, w_recv, w_basis, w_out, blocks)
         for p in range(len(PARTS))

time: 118 us -> 105 us (0.89)
  starting transfers between devices: 52.6 us -> 44.9 us
  Pallas kernels: 51.8 us -> 48.9 us
  local copies, waits for them, and re-layouts: 4.58 us -> 2.36 us
  waiting for transfers between devices: 5.5 us -> 3.56 us
    ppermute x8 -> x6, starting transfers between devices: 22.6 us -> 12.1 us  [moved(): return lax.ppermute(array, ('slab', 'sub'), pairs)]
    ppermute x8 -> x6, waiting for transfers between devices: 5.49 us -> 0.02 us  [moved(): return lax.ppermute(array, ('slab', 'sub'), pairs)]
    all_to_all x4 -> x3, waiting for transfers between devices: 0.01 us -> 3.55 us  [exchanged(): lax.all_to_all(array, ('slab', 'sub'), 0, 0, axis_index_groups=groups, ti...]
    all_to_all x4 -> x3, starting transfers between devices: 30 us -> 32.9 us  [exchanged(): lax.all_to_all(array, ('slab', 'sub'), 0, 0, axis_index_groups=groups, ti...]
    unnamed x20, local copies, waits for them, and re-layouts: 3.88 us -> 0.99 us
    pallas_call x6 -> x5, Pallas kernels: 42.7 us -> 40.6 us  [the longest x3 38.6 us: edge_call(): pl.pallas_call(functools.partial(edge_kernel, degree, first), in_specs=[h...]
  transfers between devices with their start and end apart: 12 -> 9, of which waited for: 1 -> 1; matrix products, arithmetic and copies ran while one was open for 2% -> 4% of each run, Pallas kernels for 37% -> 42%
where the time goes in v3:
time: 105 us
  Pallas kernels  48.9 us (47%)
  starting transfers between devices  44.9 us (43%)
  waiting for transfers between devices  3.56 us (3%)
  matrix products  2.47 us (2%)
  local copies, waits for them, and re-layouts  2.36 us (2%)
  other arithmetic  1.14 us (1%)
  between operations  1.09 us (1%)
    pallas_call x3, Pallas kernels, edge_call(): pl.pallas_call(functools.partial(edge_kernel, degree, first), in_specs=[h...  38.6 us
    all_to_all x3, starting transfers between devices, exchanged(): lax.all_to_all(array, ('slab', 'sub'), 0, 0, axis_index_groups=groups, ti...  32.9 us
    ppermute x6, starting transfers between devices, moved(): return lax.ppermute(array, ('slab', 'sub'), pairs)  12.1 us
    pallas_call x1, Pallas kernels, factor_call(): pl.pallas_call(factor_kernel, in_specs=[pl.BlockSpec(memory_space=pltpu.S...  5.27 us
    all_to_all x3, waiting for transfers between devices, exchanged(): lax.all_to_all(array, ('slab', 'sub'), 0, 0, axis_index_groups=groups, ti...  3.55 us
    pallas_call x1, Pallas kernels, final_call(): pl.pallas_call(functools.partial(final_kernel, scale), in_specs=[pl.Block...  3.1 us
  transfers between devices with their start and end apart: 9, of which 1 were waited for; matrix products, arithmetic and copies ran while one was open for 4% of the time, Pallas kernels for 42%

profile of v3, /device:TPU:1, one launch (start us, length us, event | category | flops | bytes accessed | tf_op | source)
XLA Modules:
  0.0 104.5 jit_solution(4555805693657155534)
XLA Ops:
  0.0 1.3 %convolution_convert_fusion.refs_0_ = bf16[1024,128]{1,0:T(8,128)(2,1)S(1)} fusion(bf16[1024,128]{1,0:T(8,128)(2,1)} %features_hbm.7, bf16[128,128]{1,0:T(8,128)(2,1)} %param.21), kind=kOutput, calls=%fused_computation | convolution fusion | flops 33685504 | bytes 557056 | tf_op jit(solution)/shard_map/dot_general | solution.py:475
  1.3 3.8 %collective-permute-start = (bf16[1024,128]{1,0:T(8,128)(2,1)S(1)}, bf16[1024,128]{1,0:T(8,128)(2,1)S(1)}, u32[]{:S(2)}, u32[]{:S(2)}) collective-permute-start(bf16[1024,128]{1,0:T(8,128)(2,1)S(1)} %convolution_convert_fusion.refs_0_), channel_id=1, source_target_pairs={{0,1},{1,0},{2,3},{3,2},{4,5},{5,4},{6,7},{7,6},{8,9},{9,8},{10,11... | collective-permute-start | bytes 786440 | tf_op jit(solution)/shard_map/ppermute | solution.py:430
  5.1 2.3 %collective-permute-start.1 = (bf16[1024,128]{1,0:T(8,128)(2,1)S(1)}, bf16[1024,128]{1,0:T(8,128)(2,1)}, u32[]{:S(2)}, u32[]{:S(2)}) collective-permute-start(bf16[1024,128]{1,0:T(8,128)(2,1)S(1)} %convolution_convert_fusion.refs_0_), channel_id=1, source_target_pairs={{0,7},{1,2},{2,1},{3,4},{4,3},{5,6},{6,5},{7,0},{8,15},{9,10},{10,... | collective-permute-start | bytes 786440 | tf_op jit(solution)/shard_map/ppermute | solution.py:430
  7.4 2.4 %collective-permute-start.3 = (bf16[1024,128]{1,0:T(8,128)(2,1)S(1)}, bf16[1024,128]{1,0:T(8,128)(2,1)}, u32[]{:S(2)}, u32[]{:S(2)}) collective-permute-start(bf16[1024,128]{1,0:T(8,128)(2,1)S(1)} %convolution_convert_fusion.refs_0_), channel_id=1, source_target_pairs={{0,248},{1,249},{2,250},{3,251},{4,252},{5,253},{6,254},{7,255},{8... | collective-permute-start | bytes 786440 | tf_op jit(solution)/shard_map/ppermute | solution.py:430
  9.8 0.2 collective-permute-start.4
  9.9 3.1 %collective-permute-start.5 = (bf16[1024,128]{1,0:T(8,128)(2,1)S(1)}, bf16[1024,128]{1,0:T(8,128)(2,1)}, u32[]{:S(2)}, u32[]{:S(2)}) collective-permute-start(bf16[1024,128]{1,0:T(8,128)(2,1)S(1)} %convolution_convert_fusion.refs_0_), channel_id=1, source_target_pairs={{0,255},{1,250},{2,249},{3,252},{4,251},{5,254},{6,253},{7,248},{8... | collective-permute-start | bytes 786440 | tf_op jit(solution)/shard_map/ppermute | solution.py:430
  13.6 5.3 %factor_sums.1.refs_7_ = f32[256,1152]{1,0:T(8,128)} custom-call(s32[1]{0:T(128)S(6)} %copy.15.count_ref, f32[88,2]{1,0:T(8,128)} %constant.40.clone.xy_hbm, f32[3,1024]{1,0:T(4,128)} %pos_hbm.3, bf16[1024,128]{1,0:T(8,128)(2,1)} %features_hbm.7), custom_call_target="tpu_custom_call" | custom-call | tf_op jit(solution)/shard_map/factor_sums/pallas_call | solution.py:142
  18.9 10.4 %all-to-all-start = ((f32[32,8,1152]{2,1,0:T(8,128)}), f32[32,8,1152]{2,1,0:T(8,128)S(1)}, u32[]{:S(2)}, u32[]{:S(2)}) async-start(f32[32,8,1152]{2,1,0:T(8,128)} %bitcast.10), calls=%async_computation | async-start | bytes 2359296 | tf_op jit(solution)/shard_map/all_to_all | solution.py:465
  29.4 1.1 %pad_maximum_fusion = bf16[3072,128]{1,0:T(8,128)(2,1)S(1)} fusion(bf16[1024,128]{1,0:T(8,128)(2,1)} %collective-permute-done.1.refs_2_, bf16[1024,128]{1,0:T(8,128)(2,1)S(1)} %collective-permute-done.refs_1_, bf16[1024,128]{1,0:T(8,128)(2,1)S(1)} %convolution_convert_fusion.refs_0_), kind=kLoop, calls=%fused_computation.1 | loop fusion | flops 2359296 | bytes 1572864 | tf_op jit(solution)/shard_map/concatenate | solution.py:481
  30.5 0.3 collective-permute-start.2
  30.8 0.1 add_add_fusion
  30.9 0.8 constant_dynamic-slice_fusion
  31.6 0.6 eq.27
  32.2 1.2 %fusion.weight_ref = f32[72,128]{1,0:T(8,128)S(1)} fusion(f32[2048,128]{1,0:T(8,128)S(1)} %copy-done, s32[2048]{0:T(1024)S(1)} %bitcast.11, s32[72]{0:T(128)} %eq.27), kind=kOutput, calls=%fused_computation.2 | convolution fusion | flops 226639872 | bytes 1093920 | tf_op jit(solution)/shard_map/dot_general | solution.py:222
  33.5 10.6 %edge_part_0.1.refs_0_ = f32[256,128]{1,0:T(8,128)} custom-call(s32[256,128]{1,0:T(8,128)} %bitcast.12, bf16[8,32768]{1,0:T(8,128)(2,1)} %basis_hbm.5, bf16[1024,128]{1,0:T(8,128)(2,1)} %features_hbm.7, bf16[128,128]{1,0:T(8,128)(2,1)} %recv_hbm.5, bf16[8,128]{1,0:T(8,128)(2,1)} %wb_hbm.5, bf16[128,128]{1,0:T(8,128)(2,1)} %wo_hbm.5, ...), custom_call_target="tpu_custom_call" | custom-call | flops 8000000000 | bytes 4000000 | tf_op jit(solution)/shard_map/edge_part_0/pallas_call | solution.py:351
  44.1 3.5 %all-to-all-done = f32[32,8,1152]{2,1,0:T(8,128)S(1)} async-done(((f32[32,8,1152]{2,1,0:T(8,128)}), f32[32,8,1152]{2,1,0:T(8,128)S(1)}, u32[]{:S(2)}, u32[]{:S(2)}) %all-to-all-start) | async-done | bytes 1179680 | tf_op jit(solution)/shard_map/all_to_all | solution.py:465
  47.7 0.8 stage_sums.1.refs_7_
  48.5 11.2 %all-to-all-start.1 = ((f32[8,8,1152]{2,1,0:T(8,128)}), f32[8,8,1152]{2,1,0:T(8,128)S(1)}, u32[]{:S(2)}, u32[]{:S(2)}) async-start(f32[8,8,1152]{2,1,0:T(8,128)} %stage_sums.1.refs_7_), calls=%async_computation.1 | async-start | bytes 589824 | tf_op jit(solution)/shard_map/all_to_all | solution.py:465
  59.7 10.7 %edge_part_1.1.refs_1_ = f32[256,128]{1,0:T(8,128)} custom-call(s32[256,128]{1,0:T(8,128)} %bitcast.13, bf16[8,32768]{1,0:T(8,128)(2,1)} %basis_hbm.5, bf16[1024,128]{1,0:T(8,128)(2,1)} %features_hbm.7, bf16[128,128]{1,0:T(8,128)(2,1)} %recv_hbm.5, bf16[8,128]{1,0:T(8,128)(2,1)} %wb_hbm.5, bf16[128,128]{1,0:T(8,128)(2,1)} %wo_hbm.5, ...), custom_call_target="tpu_custom_call" | custom-call | flops 8000000000 | bytes 4000000 | tf_op jit(solution)/shard_map/edge_part_1/pallas_call | solution.py:351
  70.4 1.2 %filter_rows.1.refs_7_ = bf16[32,8,1152]{2,1,0:T(8,128)(2,1)} custom-call(f32[8,8,1152]{2,1,0:T(8,128)S(1)} %all-to-all-done.1.sums_ref, f32[72,128]{1,0:T(8,128)S(1)} %fusion.weight_ref, f32[128,128]{1,0:T(8,128)S(1)} %copy-done.6), custom_call_target="tpu_custom_call" | custom-call | tf_op jit(solution)/shard_map/filter_rows/pallas_call | solution.py:204
  71.6 11.3 %all-to-all-start.2 = ((bf16[32,8,1152]{2,1,0:T(8,128)(2,1)}), bf16[32,8,1152]{2,1,0:T(8,128)(2,1)S(1)}, u32[]{:S(2)}, u32[]{:S(2)}) async-start(bf16[32,8,1152]{2,1,0:T(8,128)(2,1)} %filter_rows.1.refs_7_), calls=%async_computation.2 | async-start | bytes 1179648 | tf_op jit(solution)/shard_map/all_to_all | solution.py:465
  82.9 17.3 %edge_part_2.1.refs_2_ = f32[512,128]{1,0:T(8,128)} custom-call(s32[256,128]{1,0:T(8,128)} %bitcast.14, bf16[8,32768]{1,0:T(8,128)(2,1)} %basis_hbm.5, bf16[1024,128]{1,0:T(8,128)(2,1)} %features_hbm.7, bf16[128,128]{1,0:T(8,128)(2,1)} %recv_hbm.5, bf16[8,128]{1,0:T(8,128)(2,1)} %wb_hbm.5, bf16[128,128]{1,0:T(8,128)(2,1)} %wo_hbm.5, ...), custom_call_target="tpu_custom_call" | custom-call | flops 8000000000 | bytes 4000000 | tf_op jit(solution)/shard_map/edge_part_2/pallas_call | solution.py:351
  100.3 0.9 copy-done.1
  101.2 3.1 %updated_rows.1 = f32[1024,128]{1,0:T(8,128)} custom-call(s32[1]{0:T(128)S(6)} %copy.15.count_ref, f32[88,2]{1,0:T(8,128)S(1)} %copy-done.2, f32[3,1024]{1,0:T(4,128)S(1)} %copy-done.5, bf16[256,1152]{1,0:T(8,128)(2,1)S(1)} %bitcast.9, f32[256,128]{1,0:T(8,128)S(1)} %copy-done.3, f32[256,128]{1,0:T(8,128)S(1)} %copy-done.4, f32[512,128]{1,0:T(8,128)S(1)} %copy-done.1), custom_call_target="tpu_custom_call" | custom-call | tf_op jit(solution)/shard_map/updated_rows/pallas_call | solution.py:407
  (27 shorter events, 0.1 us)
Async XLA Ops:
  0.0 32.2 %copy-start = (f32[2048,128]{1,0:T(8,128)S(1)}, f32[2048,128]{1,0:T(8,128)}, u32[]{:S(2)}) copy-start(f32[2048,128]{1,0:T(8,128)} %param.18) | copy-start | bytes 3145732
  1.3 28.1 %copy-start.7 = (bf16[1024,128]{1,0:T(8,128)(2,1)}, bf16[1024,128]{1,0:T(8,128)(2,1)S(1)}, u32[]{:S(2)}) copy-start(bf16[1024,128]{1,0:T(8,128)(2,1)S(1)} %convolution_convert_fusion.refs_0_) | copy-start | bytes 786436
  1.3 28.1 %collective-permute-start = (bf16[1024,128]{1,0:T(8,128)(2,1)S(1)}, bf16[1024,128]{1,0:T(8,128)(2,1)S(1)}, u32[]{:S(2)}, u32[]{:S(2)}) collective-permute-start(bf16[1024,128]{1,0:T(8,128)(2,1)S(1)} %convolution_convert_fusion.refs_0_), channel_id=1, source_target_pairs={{0,1},{1,0},{2,3},{3,2},{4,5},{5,4},{6,7},{7,6},{8,9},{9,8},{10,11... | collective-permute-start | bytes 786440 | tf_op jit(solution)/shard_map/ppermute | solution.py:430
  5.1 24.3 %collective-permute-start.1 = (bf16[1024,128]{1,0:T(8,128)(2,1)S(1)}, bf16[1024,128]{1,0:T(8,128)(2,1)}, u32[]{:S(2)}, u32[]{:S(2)}) collective-permute-start(bf16[1024,128]{1,0:T(8,128)(2,1)S(1)} %convolution_convert_fusion.refs_0_), channel_id=1, source_target_pairs={{0,7},{1,2},{2,1},{3,4},{4,3},{5,6},{6,5},{7,0},{8,15},{9,10},{10,... | collective-permute-start | bytes 786440 | tf_op jit(solution)/shard_map/ppermute | solution.py:430
  7.4 26.1 %collective-permute-start.3 = (bf16[1024,128]{1,0:T(8,128)(2,1)S(1)}, bf16[1024,128]{1,0:T(8,128)(2,1)}, u32[]{:S(2)}, u32[]{:S(2)}) collective-permute-start(bf16[1024,128]{1,0:T(8,128)(2,1)S(1)} %convolution_convert_fusion.refs_0_), channel_id=1, source_target_pairs={{0,248},{1,249},{2,250},{3,251},{4,252},{5,253},{6,254},{7,255},{8... | collective-permute-start | bytes 786440 | tf_op jit(solution)/shard_map/ppermute | solution.py:430
  9.8 23.7 %collective-permute-start.4 = (bf16[1024,128]{1,0:T(8,128)(2,1)S(1)}, bf16[1024,128]{1,0:T(8,128)(2,1)}, u32[]{:S(2)}, u32[]{:S(2)}) collective-permute-start(bf16[1024,128]{1,0:T(8,128)(2,1)S(1)} %convolution_convert_fusion.refs_0_), channel_id=1, source_target_pairs={{0,249},{1,248},{2,251},{3,250},{4,253},{5,252},{6,255},{7,254},{8... | collective-permute-start | bytes 786440 | tf_op jit(solution)/shard_map/ppermute | solution.py:430
  9.9 23.6 %collective-permute-start.5 = (bf16[1024,128]{1,0:T(8,128)(2,1)S(1)}, bf16[1024,128]{1,0:T(8,128)(2,1)}, u32[]{:S(2)}, u32[]{:S(2)}) collective-permute-start(bf16[1024,128]{1,0:T(8,128)(2,1)S(1)} %convolution_convert_fusion.refs_0_), channel_id=1, source_target_pairs={{0,255},{1,250},{2,249},{3,252},{4,251},{5,254},{6,253},{7,248},{8... | collective-permute-start | bytes 786440 | tf_op jit(solution)/shard_map/ppermute | solution.py:430
  18.9 28.8 %all-to-all-start = ((f32[32,8,1152]{2,1,0:T(8,128)}), f32[32,8,1152]{2,1,0:T(8,128)S(1)}, u32[]{:S(2)}, u32[]{:S(2)}) async-start(f32[32,8,1152]{2,1,0:T(8,128)} %bitcast.10), calls=%async_computation | async-start | bytes 2359296 | tf_op jit(solution)/shard_map/all_to_all | solution.py:465
  29.3 1.5 %copy-start.9 = (s32[3,2048]{1,0:T(4,128)S(1)}, s32[3,2048]{1,0:T(4,128)}, u32[]{:S(2)}) copy-start(s32[3,2048]{1,0:T(4,128)} %param.17) | copy-start | bytes 73732
  29.3 2.9 %copy-start.8 = (bf16[1024,128]{1,0:T(8,128)(2,1)}, bf16[1024,128]{1,0:T(8,128)(2,1)S(1)}, u32[]{:S(2)}) copy-start(bf16[1024,128]{1,0:T(8,128)(2,1)S(1)} %collective-permute-done.refs_1_) | copy-start | bytes 786436
  30.5 3.0 %collective-permute-start.2 = (bf16[3072,128]{1,0:T(8,128)(2,1)S(1)}, bf16[3072,128]{1,0:T(8,128)(2,1)}, u32[]{:S(2)}, u32[]{:S(2)}) collective-permute-start(bf16[3072,128]{1,0:T(8,128)(2,1)S(1)} %pad_maximum_fusion), channel_id=1, source_target_pairs={{0,8},{1,9},{2,10},{3,11},{4,12},{5,13},{6,14},{7,15},{8,0},{9,1},... | collective-permute-start | bytes 2359304 | tf_op jit(solution)/shard_map/ppermute | solution.py:430
  48.5 21.9 %all-to-all-start.1 = ((f32[8,8,1152]{2,1,0:T(8,128)}), f32[8,8,1152]{2,1,0:T(8,128)S(1)}, u32[]{:S(2)}, u32[]{:S(2)}) async-start(f32[8,8,1152]{2,1,0:T(8,128)} %stage_sums.1.refs_7_), calls=%async_computation.1 | async-start | bytes 589824 | tf_op jit(solution)/shard_map/all_to_all | solution.py:465
  59.7 10.7 %copy-start.6 = (f32[128,128]{1,0:T(8,128)S(1)}, f32[128,128]{1,0:T(8,128)}, u32[]{:S(2)}) copy-start(f32[128,128]{1,0:T(8,128)} %mix_hbm.1) | copy-start | bytes 196612
  71.6 28.6 %all-to-all-start.2 = ((bf16[32,8,1152]{2,1,0:T(8,128)(2,1)}), bf16[32,8,1152]{2,1,0:T(8,128)(2,1)S(1)}, u32[]{:S(2)}, u32[]{:S(2)}) async-start(bf16[32,8,1152]{2,1,0:T(8,128)(2,1)} %filter_rows.1.refs_7_), calls=%async_computation.2 | async-start | bytes 1179648 | tf_op jit(solution)/shard_map/all_to_all | solution.py:465
  82.9 17.4 %copy-start.2 = (f32[88,2]{1,0:T(8,128)S(1)}, f32[88,2]{1,0:T(8,128)}, u32[]{:S(2)}) copy-start(f32[88,2]{1,0:T(8,128)} %constant.40.clone.xy_hbm) | copy-start | bytes 2116
  82.9 17.4 %copy-start.3 = (f32[256,128]{1,0:T(8,128)S(1)}, f32[256,128]{1,0:T(8,128)}, u32[]{:S(2)}) copy-start(f32[256,128]{1,0:T(8,128)} %edge_part_0.1.refs_0_) | copy-start | bytes 393220
  82.9 17.4 %copy-start.4 = (f32[256,128]{1,0:T(8,128)S(1)}, f32[256,128]{1,0:T(8,128)}, u32[]{:S(2)}) copy-start(f32[256,128]{1,0:T(8,128)} %edge_part_1.1.refs_1_) | copy-start | bytes 393220
  82.9 17.4 %copy-start.5 = (f32[3,1024]{1,0:T(4,128)S(1)}, f32[3,1024]{1,0:T(4,128)}, u32[]{:S(2)}) copy-start(f32[3,1024]{1,0:T(4,128)} %pos_hbm.3) | copy-start | bytes 36868
  100.3 1.0 copy-start.1

commit v4 on v3

--- a/solution.py
+++ b/solution.py
@@ -15,7 +15,7 @@
 WAVE_ROWS = 2304
 DEVICES = 256
 ROWS_EACH = WAVE_ROWS // DEVICES
-PARTS = (256, 256, 512)
+PARTS = (512, 512)
 PLANE = 4
 UNROLL = 16
 BUFFERS = 4
@@ -222,93 +222,127 @@
     return jnp.dot(same, k_filter, precision=lax.Precision.HIGHEST)
 
 
-def edge_kernel(
-    degree, first, ids_hbm, basis_hbm, features_hbm, recv_hbm, wb_hbm, wo_hbm, *refs
-):
+def receive_kernel(degree, basis_ref, features_ref, recv_ref, wb_ref, after_ref, out_ref, wide_ref):
+    atoms, channels = features_ref.shape
+    basis_rows = wb_ref.shape[0]
+    groups = 128 // basis_rows
+    del after_ref
+
+    @pl.when(pl.program_id(0) == 0)
+    def _():
+        stacked = jnp.concatenate([wb_ref[...].astype(jnp.float32)] * groups, axis=0)
+        group_of = lax.broadcasted_iota(jnp.int32, stacked.shape, 0) // basis_rows
+        for g in range(groups):
+            wide_ref[:, g * channels : (g + 1) * channels] = jnp.where(
+                group_of == g, stacked, 0.0
+            ).astype(jnp.bfloat16)
+
+    own = jnp.dot(features_ref[...], recv_ref[...], preferred_element_type=jnp.float32)
+    values = basis_ref[...].astype(jnp.float32)
+    stack = jnp.concatenate([values[:, g * 128 : (g + 1) * 128] for g in range(groups)], axis=0)
+    turned = stack.T.astype(jnp.bfloat16)
+    each = 128 // degree
+    for g in range(0, groups, 2):
+        both = jnp.dot(
+            turned,
+            wide_ref[:, g * channels : (g + 2) * channels],
+            preferred_element_type=jnp.float32,
+        )
+        for side in range(2):
+            first = (g + side) * each
+            mine = jnp.concatenate(
+                [
+                    jnp.broadcast_to(own[atom : atom + 1], (degree, channels))
+                    for atom in range(first, first + each)
+                ],
+                axis=0,
+            )
+            out_ref[(g + side) * 128 : (g + side + 1) * 128, :] = (
+                both[:, side * channels : (side + 1) * channels] + mine
+            ) * 0.5
+
+
+def receive_call(features, edge_basis, w_recv, w_basis, after):
+    atoms, channels = features.shape
+    basis_rows, edges = edge_basis.shape
+    degree = edges // atoms
+    span = 128 // basis_rows * 128
+    whole = lambda array: pl.BlockSpec(array.shape, lambda i: (0, 0))
+    return pl.pallas_call(
+        functools.partial(receive_kernel, degree),
+        grid=(edges // span,),
+        in_specs=[
+            pl.BlockSpec((basis_rows, span), lambda i: (0, i)),
+            pl.BlockSpec((span // degree, channels), lambda i: (i, 0)),
+            whole(w_recv),
+            whole(w_basis),
+            pl.BlockSpec(memory_space=pl.ANY),
+        ],
+        out_specs=pl.BlockSpec((span, channels), lambda i: (i, 0)),
+        out_shape=jax.ShapeDtypeStruct((edges, channels), jnp.float32),
+        scratch_shapes=[pltpu.VMEM((128, 128 // basis_rows * channels), jnp.bfloat16)],
+        compiler_params=limit(TABLE_VMEM),
+        cost_estimate=pl.CostEstimate(
+            flops=5 * 10**9, bytes_accessed=18 * 10**6, transcendentals=0
+        ),
+        name="receive_rows",
+    )(edge_basis, features, w_recv, w_basis, after)
+
+
+def edge_kernel(degree, first, ids_hbm, base_hbm, wo_hbm, *refs):
     blocks, refs = refs[:7], refs[7:]
-    (after_ref, out_ref, pool_ref, radial_ref, part_ref, own_ref, wide_ref), refs = refs[:7], refs[7:]
-    local, loaded, refs = refs[:6], refs[6], refs[7:]
-    ids_ref, basis_ref, features_ref, recv_ref, wb_ref, wo_ref = local
+    (after_ref, out_ref, pool_ref, part_ref, base_ref, ids_ref, wo_ref), refs = refs[:7], refs[7:]
+    loaded, streamed, refs = refs[0], refs[1], refs[2:]
     buffers, arrivals = refs[:BUFFERS], refs[BUFFERS:]
     atoms, channels = out_ref.shape
     del after_ref
-    copies = loads(
-        (
-            ids_hbm.at[pl.ds(first * degree // 128, atoms * degree // 128), :],
-            basis_hbm.at[:, pl.ds(first * degree, atoms * degree)],
-            features_hbm.at[pl.ds(first, atoms), :],
-            recv_hbm,
-            wb_hbm,
-            wo_hbm,
-        ),
-        local,
-        loaded,
-    )
     edges = UNROLL * degree
     lines = edges // 128
     chunks = atoms // UNROLL
+    rounds = chunks // BUFFERS
+    span = edges * BUFFERS
+    copies = loads(
+        (ids_hbm.at[pl.ds(first * degree // 128, atoms * degree // 128), :], wo_hbm),
+        (ids_ref, wo_ref),
+        loaded,
+    )
+
+    def stream(step):
+        slot = lax.rem(step, 2)
+        start = pl.multiple_of(first * degree + step * span, span)
+        return pltpu.make_async_copy(
+            base_hbm.at[pl.ds(start, span), :], base_ref.at[slot], streamed.at[slot]
+        )
 
     def fetch(chunk, at):
         source = ids_ref.at[pl.ds(chunk * lines, lines), :]
         return pltpu.make_async_copy(source, buffers[at], arrivals[at])
 
+    stream(0).start()
     slab_even = lax.rem(lax.axis_index("slab"), 2) == 0
     sub_even = lax.rem(lax.axis_index("sub"), 2) == 0
     slab_place = (1, jnp.where(slab_even, 2, 0), jnp.where(slab_even, 0, 2))
     sub_place = (1, jnp.where(sub_even, 2, 0), jnp.where(sub_even, 0, 2))
+    for copy in copies:
+        copy.wait()
+    for at in range(BUFFERS):
+        fetch(at, at).start()
     rows = blocks[0].shape[0]
     at = 0
     for block in blocks:
         for first_row in range(0, block.shape[0], rows):
             place = pl.multiple_of((slab_place[at // 3] * 3 + sub_place[at % 3]) * rows, rows)
-            pool_ref[pl.ds(place, rows), :] = block[first_row : first_row + rows, :].astype(
-                jnp.float32
+            pool_ref[pl.ds(place, rows), :] = (
+                block[first_row : first_row + rows, :].astype(jnp.float32) * 0.5
             )
             at += 1
 
-    for copy in copies:
-        copy.wait()
-    for at in range(BUFFERS):
-        fetch(at, at).start()
-    own_ref[...] = jnp.dot(features_ref[...], recv_ref[...], preferred_element_type=jnp.float32)
-
-    basis_rows = wb_ref.shape[0]
-    groups = 128 // basis_rows
-    stacked = jnp.concatenate([wb_ref[...].astype(jnp.float32)] * groups, axis=0)
-    group_of = lax.broadcasted_iota(jnp.int32, stacked.shape, 0) // basis_rows
-    for g in range(groups):
-        wide_ref[:, g * channels : (g + 1) * channels] = jnp.where(
-            group_of == g, stacked, 0.0
-        ).astype(jnp.bfloat16)
-
-    span = groups * 128
-
-    def radial_block(step, carry):
-        base = pl.multiple_of(step * span, span)
-        values = basis_ref[:, pl.ds(base, span)]
-        values = values.astype(jnp.float32)
-        stack = jnp.concatenate([values[:, g * 128 : (g + 1) * 128] for g in range(groups)], axis=0)
-        turned = stack.T.astype(jnp.bfloat16)
-        for g in range(0, groups, 2):
-            both = jnp.dot(
-                turned,
-                wide_ref[:, g * channels : (g + 2) * channels],
-                preferred_element_type=jnp.float32,
-            )
-            radial_ref[pl.ds(base + g * 128, 128), :] = both[:, :channels]
-            radial_ref[pl.ds(base + (g + 1) * 128, 128), :] = both[:, channels:]
-        return carry
-
-    lax.fori_loop(0, atoms * degree // span, radial_block, 0)
     sublane = lax.broadcasted_iota(jnp.int32, (8, channels), 0)
     at_sublane = [sublane == r for r in range(8)]
 
-    def some_atoms(chunk, ids):
-        own = own_ref.at[pl.ds(pl.multiple_of(chunk * UNROLL, UNROLL), UNROLL), :]
+    def some_atoms(chunk, ids, base):
         part = part_ref.at[pl.ds(pl.multiple_of(chunk * UNROLL * 8, UNROLL * 8), UNROLL * 8), :]
-        radial = radial_ref.at[pl.ds(pl.multiple_of(chunk * edges, edges), edges), :]
         for u in range(UNROLL):
-            mine = jnp.broadcast_to(own[u : u + 1, :], (8, channels))
             total = None
             for edge in range(u * degree, (u + 1) * degree, 8):
                 sent = None
@@ -316,20 +350,27 @@
                     sender = ids[(edge + r) // 128, (edge + r) % 128]
                     row = jnp.broadcast_to(pool_ref[pl.ds(sender, 1), :], (8, channels))
                     sent = row if sent is None else jnp.where(at_sublane[r], row, sent)
-                half = (sent + radial[edge : edge + 8, :] + mine) * 0.5
+                half = sent + base[edge : edge + 8, :]
                 hidden = (half + half * jnp.tanh(half)).astype(jnp.bfloat16).astype(jnp.float32)
                 total = hidden if total is None else total + hidden
             part[u * 8 : u * 8 + 8, :] = total
 
     def round_of_chunks(step, carry):
+        stream(step).wait()
+
+        @pl.when(step + 1 < rounds)
+        def _():
+            stream(step + 1).start()
+
+        slot = base_ref.at[lax.rem(step, 2)]
         for at in range(BUFFERS):
             chunk = step * BUFFERS + at
             fetch(chunk, at).wait()
-            some_atoms(chunk, buffers[at])
+            some_atoms(chunk, buffers[at], slot.at[pl.ds(at * edges, edges), :])
             fetch(jnp.minimum(chunk + BUFFERS, chunks - 1), at).start()
         return carry
 
-    lax.fori_loop(0, chunks // BUFFERS, round_of_chunks, 0)
+    lax.fori_loop(0, rounds, round_of_chunks, 0)
     for at in range(BUFFERS):
         fetch(chunks - 1, at).wait()
     summed = part_ref[pl.ds(0, atoms, stride=8), :]
@@ -343,40 +384,33 @@
     out_ref[...] = message * (1.0 / math.sqrt(degree))
 
 
-def edge_call(part, after, senders, edge_basis, features, w_recv, w_basis, w_out, blocks):
-    channels = features.shape[1]
-    degree = senders.shape[0] // features.shape[0]
+def edge_call(part, after, senders, base, w_out, blocks):
+    channels = base.shape[1]
+    degree = base.shape[0] // blocks[0].shape[0]
     atoms, first = PARTS[part], sum(PARTS[:part])
     rows = sum(block.shape[0] for block in blocks)
     return pl.pallas_call(
         functools.partial(edge_kernel, degree, first),
-        in_specs=[hbm()] * 6 + [vmem()] * len(blocks) + [pl.BlockSpec(memory_space=pl.ANY)],
+        in_specs=[hbm()] * 3 + [vmem()] * len(blocks) + [pl.BlockSpec(memory_space=pl.ANY)],
         out_specs=vmem(),
         out_shape=jax.ShapeDtypeStruct((atoms, channels), jnp.float32),
         scratch_shapes=[
             pltpu.VMEM((rows, channels), jnp.float32),
-            pltpu.VMEM((atoms * degree, channels), jnp.float32),
             pltpu.VMEM((atoms * 8, channels), jnp.float32),
-            pltpu.VMEM((atoms, channels), jnp.float32),
-            pltpu.VMEM((128, 128 // w_basis.shape[0] * channels), jnp.bfloat16),
+            pltpu.VMEM((2, UNROLL * BUFFERS * degree, channels), jnp.float32),
             pltpu.VMEM((atoms * degree // 128, 128), jnp.int32),
-            pltpu.VMEM((edge_basis.shape[0], atoms * degree), jnp.bfloat16),
-            pltpu.VMEM((atoms, channels), jnp.bfloat16),
-            pltpu.VMEM(w_recv.shape, jnp.bfloat16),
-            pltpu.VMEM(w_basis.shape, jnp.bfloat16),
             pltpu.VMEM(w_out.shape, jnp.bfloat16),
-            pltpu.SemaphoreType.DMA((6,)),
+            pltpu.SemaphoreType.DMA((2,)),
+            pltpu.SemaphoreType.DMA((2,)),
         ]
         + [pltpu.SMEM((UNROLL * degree // 128, 128), jnp.int32)] * BUFFERS
         + [pltpu.SemaphoreType.DMA] * BUFFERS,
         compiler_params=limit(LARGE_VMEM),
         cost_estimate=pl.CostEstimate(
-            flops=8 * 10**9, bytes_accessed=4 * 10**6, transcendentals=10**6
+            flops=12 * 10**9, bytes_accessed=12 * 10**6, transcendentals=2 * 10**6
         ),
         name="edge_part_%d" % part,
-    )(
-        senders.reshape(-1, 128), edge_basis, features, w_recv, w_basis, w_out, *blocks, after
-    )
+    )(senders.reshape(-1, 128), base, w_out, *blocks, after)
 
 
 def final_kernel(scale, count_ref, xy_hbm, pos_hbm, factors_ref, *refs):
@@ -493,10 +527,10 @@
     )
     factors = exchanged(filtered, plane).reshape(DEVICES, -1)
 
-    after = [sums, stage_one, filtered]
+    base = receive_call(features, edge_basis, w_recv, w_basis, sums)
+    after = [stage_one, filtered]
     parts = [
-        edge_call(p, after[p], senders, edge_basis, features, w_recv, w_basis, w_out, blocks)
-        for p in range(len(PARTS))
+        edge_call(p, after[p], senders, base, w_out, blocks) for p in range(len(PARTS))
     ]
     return final_call(atom_count, positions, factors, parts, 4.0 / math.sqrt(total_k))
 

time: 105 us -> 96.3 us (0.917)
  starting transfers between devices: 44.9 us -> 33.7 us
  local copies, waits for them, and re-layouts: 2.36 us -> 8.87 us
  Pallas kernels: 48.9 us -> 45.4 us
  waiting for transfers between devices: 3.56 us -> 2.4 us
    all_to_all x3, starting transfers between devices: 32.9 us -> 21.8 us  [exchanged(): lax.all_to_all(array, ('slab', 'sub'), 0, 0, axis_index_groups=groups, ti...]
    pallas_call x3 -> x2, Pallas kernels: 38.6 us -> 29.2 us  [edge_call(): pl.pallas_call(functools.partial(edge_kernel, degree, first), in_specs=[h...]
    unnamed x20 -> x28, local copies, waits for them, and re-layouts: 0.99 us -> 8.7 us
    pallas_call x0 -> x1, Pallas kernels: none -> 5.86 us  [receive_call(): pl.pallas_call(functools.partial(receive_kernel, degree), grid=(edges //...]
    all_to_all x3, waiting for transfers between devices: 3.55 us -> 2.38 us  [exchanged(): lax.all_to_all(array, ('slab', 'sub'), 0, 0, axis_index_groups=groups, ti...]
  transfers between devices with their start and end apart: 9 -> 9, of which waited for: 1 -> 1; matrix products, arithmetic and copies ran while one was open for 4% -> 2% of each run, Pallas kernels for 42% -> 43%
where the time goes in v4:
time: 96.3 us; the launch traced here: 95.3 us
  Pallas kernels  45.4 us (47%)
  starting transfers between devices  33.7 us (35%)
  local copies, waits for them, and re-layouts  8.87 us (9%)
  matrix products  2.53 us (3%)
  waiting for transfers between devices  2.4 us (2%)
  other arithmetic  1.23 us (1%)
  between operations  1.1 us (1%)
    pallas_call x2, Pallas kernels, edge_call(): pl.pallas_call(functools.partial(edge_kernel, degree, first), in_specs=[h...  29.2 us
    all_to_all x3, starting transfers between devices, exchanged(): lax.all_to_all(array, ('slab', 'sub'), 0, 0, axis_index_groups=groups, ti...  21.8 us
    ppermute x6, starting transfers between devices, moved(): return lax.ppermute(array, ('slab', 'sub'), pairs)  12 us
    unnamed x28, local copies, waits for them, and re-layouts  8.7 us
    pallas_call x1, Pallas kernels, receive_call(): pl.pallas_call(functools.partial(receive_kernel, degree), grid=(edges //...  5.86 us
    pallas_call x1, Pallas kernels, factor_call(): pl.pallas_call(factor_kernel, in_specs=[pl.BlockSpec(memory_space=pltpu.S...  5.26 us
    pallas_call x1, Pallas kernels, final_call(): pl.pallas_call(functools.partial(final_kernel, scale), in_specs=[pl.Block...  3.1 us
    all_to_all x3, waiting for transfers between devices, exchanged(): lax.all_to_all(array, ('slab', 'sub'), 0, 0, axis_index_groups=groups, ti...  2.38 us
  transfers between devices with their start and end apart: 9, of which 1 were waited for; matrix products, arithmetic and copies ran while one was open for 2% of the time, Pallas kernels for 43%

profile of v4, /device:TPU:1, one launch (start us, length us, event | category | flops | bytes accessed | tf_op | source)
XLA Modules:
  0.0 95.3 jit_solution(15205313692805942613)
XLA Ops:
  0.0 2.0 %convolution_convert_fusion.refs_0_ = bf16[1024,128]{1,0:T(8,128)(2,1)} fusion(bf16[1024,128]{1,0:T(8,128)(2,1)} %features_ref.1, bf16[128,128]{1,0:T(8,128)(2,1)} %param.21), kind=kOutput, calls=%fused_computation | convolution fusion | flops 33685504 | bytes 557056 | tf_op jit(solution)/shard_map/dot_general | solution.py:509
  2.0 3.7 %collective-permute-start = (bf16[1024,128]{1,0:T(8,128)(2,1)}, bf16[1024,128]{1,0:T(8,128)(2,1)}, u32[]{:S(2)}, u32[]{:S(2)}) collective-permute-start(bf16[1024,128]{1,0:T(8,128)(2,1)} %convolution_convert_fusion.refs_0_), channel_id=1, source_target_pairs={{0,1},{1,0},{2,3},{3,2},{4,5},{5,4},{6,7},{7,6},{8,9},{9,8},{10,11... | collective-permute-start | bytes 786440 | tf_op jit(solution)/shard_map/ppermute | solution.py:464
  5.7 2.3 %collective-permute-start.1 = (bf16[1024,128]{1,0:T(8,128)(2,1)}, bf16[1024,128]{1,0:T(8,128)(2,1)}, u32[]{:S(2)}, u32[]{:S(2)}) collective-permute-start(bf16[1024,128]{1,0:T(8,128)(2,1)} %convolution_convert_fusion.refs_0_), channel_id=1, source_target_pairs={{0,7},{1,2},{2,1},{3,4},{4,3},{5,6},{6,5},{7,0},{8,15},{9,10},{10,... | collective-permute-start | bytes 786440 | tf_op jit(solution)/shard_map/ppermute | solution.py:464
  8.0 2.4 %collective-permute-start.3 = (bf16[1024,128]{1,0:T(8,128)(2,1)}, bf16[1024,128]{1,0:T(8,128)(2,1)}, u32[]{:S(2)}, u32[]{:S(2)}) collective-permute-start(bf16[1024,128]{1,0:T(8,128)(2,1)} %convolution_convert_fusion.refs_0_), channel_id=1, source_target_pairs={{0,248},{1,249},{2,250},{3,251},{4,252},{5,253},{6,254},{7,255},{8... | collective-permute-start | bytes 786440 | tf_op jit(solution)/shard_map/ppermute | solution.py:464
  10.4 0.2 collective-permute-start.4
  10.6 3.1 %collective-permute-start.5 = (bf16[1024,128]{1,0:T(8,128)(2,1)}, bf16[1024,128]{1,0:T(8,128)(2,1)}, u32[]{:S(2)}, u32[]{:S(2)}) collective-permute-start(bf16[1024,128]{1,0:T(8,128)(2,1)} %convolution_convert_fusion.refs_0_), channel_id=1, source_target_pairs={{0,255},{1,250},{2,249},{3,252},{4,251},{5,254},{6,253},{7,248},{8... | collective-permute-start | bytes 786440 | tf_op jit(solution)/shard_map/ppermute | solution.py:464
  14.3 5.3 %factor_sums.1.after_ref = f32[256,1152]{1,0:T(8,128)} custom-call(s32[1]{0:T(128)S(6)} %copy.15.count_ref, f32[88,2]{1,0:T(8,128)} %constant.40.clone.xy_hbm, f32[3,1024]{1,0:T(4,128)} %pos_hbm.3, bf16[1024,128]{1,0:T(8,128)(2,1)} %features_ref.1), custom_call_target="tpu_custom_call" | custom-call | tf_op jit(solution)/shard_map/factor_sums/pallas_call | solution.py:142
  19.6 10.5 %all-to-all-start = ((f32[32,8,1152]{2,1,0:T(8,128)}), f32[32,8,1152]{2,1,0:T(8,128)S(1)}, u32[]{:S(2)}, u32[]{:S(2)}) async-start(f32[32,8,1152]{2,1,0:T(8,128)} %bitcast.8), calls=%async_computation | async-start | bytes 2359296 | tf_op jit(solution)/shard_map/all_to_all | solution.py:499
  30.1 0.9 copy-done.3
  31.1 1.0 %copy-done.4 = bf16[8,32768]{1,0:T(8,128)(2,1)S(1)} copy-done((bf16[8,32768]{1,0:T(8,128)(2,1)S(1)}, bf16[8,32768]{1,0:T(8,128)(2,1)}, u32[]{:S(2)}) %copy-start.4) | copy-done | bytes 524312
  32.1 5.9 %receive_rows.1.base_hbm = f32[32768,128]{1,0:T(8,128)S(1)} custom-call(bf16[8,32768]{1,0:T(8,128)(2,1)S(1)} %copy-done.4, bf16[1024,128]{1,0:T(8,128)(2,1)S(1)} %copy-done.3, bf16[128,128]{1,0:T(8,128)(2,1)S(1)} %copy-done.10, bf16[8,128]{1,0:T(8,128)(2,1)S(1)} %copy-done.11, f32[256,1152]{1,0:T(8,128)S(1)} %copy-done.2), custom_call_target="tpu_custom_call" | custom-call | flops 5000000000 | bytes 18000000 | tf_op jit(solution)/shard_map/receive_rows/pallas_call | solution.py:271
  38.0 5.7 %copy-done.1 = f32[32768,128]{1,0:T(8,128)} copy-done((f32[32768,128]{1,0:T(8,128)}, f32[32768,128]{1,0:T(8,128)S(1)}, u32[]{:S(2)}) %copy-start.1) | copy-done | bytes 16777240
  43.7 1.2 %pad_maximum_fusion = bf16[3072,128]{1,0:T(8,128)(2,1)S(1)} fusion(bf16[1024,128]{1,0:T(8,128)(2,1)} %collective-permute-done.1.refs_2_, bf16[1024,128]{1,0:T(8,128)(2,1)} %collective-permute-done.refs_1_, bf16[1024,128]{1,0:T(8,128)(2,1)} %convolution_convert_fusion.refs_0_), kind=kLoop, calls=%fused_computation.1 | loop fusion | flops 2359296 | bytes 1572864 | tf_op jit(solution)/shard_map/concatenate | solution.py:515
  44.9 0.3 collective-permute-start.2
  45.5 0.6 fusion.weight_ref
  46.1 2.4 %all-to-all-done = f32[32,8,1152]{2,1,0:T(8,128)S(1)} async-done(((f32[32,8,1152]{2,1,0:T(8,128)}), f32[32,8,1152]{2,1,0:T(8,128)S(1)}, u32[]{:S(2)}, u32[]{:S(2)}) %all-to-all-start) | async-done | bytes 1179680 | tf_op jit(solution)/shard_map/all_to_all | solution.py:499
  48.4 0.8 stage_sums.1.refs_7_
  49.2 4.2 %all-to-all-start.1 = ((f32[8,8,1152]{2,1,0:T(8,128)}), f32[8,8,1152]{2,1,0:T(8,128)S(1)}, u32[]{:S(2)}, u32[]{:S(2)}) async-start(f32[8,8,1152]{2,1,0:T(8,128)} %stage_sums.1.refs_7_), calls=%async_computation.1 | async-start | bytes 589824 | tf_op jit(solution)/shard_map/all_to_all | solution.py:499
  53.5 14.6 %edge_part_0.1.refs_0_ = f32[512,128]{1,0:T(8,128)} custom-call(s32[256,128]{1,0:T(8,128)} %bitcast.12, f32[32768,128]{1,0:T(8,128)} %copy-done.1, bf16[128,128]{1,0:T(8,128)(2,1)} %wo_hbm.3, bf16[1024,128]{1,0:T(8,128)(2,1)} %convolution_convert_fusion.refs_0_, bf16[1024,128]{1,0:T(8,128)(2,1)} %collective-permute-done.refs_1_, ...), custom_call_target="tpu_custom_call" | custom-call | flops 12000000000 | bytes 12000000 | tf_op jit(solution)/shard_map/edge_part_0/pallas_call | solution.py:392
  68.1 1.2 %filter_rows.1.refs_7_ = bf16[32,8,1152]{2,1,0:T(8,128)(2,1)} custom-call(f32[8,8,1152]{2,1,0:T(8,128)S(1)} %all-to-all-done.1.sums_ref, f32[72,128]{1,0:T(8,128)S(1)} %fusion.weight_ref, f32[128,128]{1,0:T(8,128)S(1)} %copy-done.9), custom_call_target="tpu_custom_call" | custom-call | tf_op jit(solution)/shard_map/filter_rows/pallas_call | solution.py:204
  69.3 7.0 %all-to-all-start.2 = ((bf16[32,8,1152]{2,1,0:T(8,128)(2,1)}), bf16[32,8,1152]{2,1,0:T(8,128)(2,1)S(1)}, u32[]{:S(2)}, u32[]{:S(2)}) async-start(bf16[32,8,1152]{2,1,0:T(8,128)(2,1)} %filter_rows.1.refs_7_), calls=%async_computation.2 | async-start | bytes 1179648 | tf_op jit(solution)/shard_map/all_to_all | solution.py:499
  76.4 14.6 %edge_part_1.1.refs_1_ = f32[512,128]{1,0:T(8,128)} custom-call(s32[256,128]{1,0:T(8,128)} %bitcast.13, f32[32768,128]{1,0:T(8,128)} %copy-done.1, bf16[128,128]{1,0:T(8,128)(2,1)} %wo_hbm.3, bf16[1024,128]{1,0:T(8,128)(2,1)} %convolution_convert_fusion.refs_0_, bf16[1024,128]{1,0:T(8,128)(2,1)} %collective-permute-done.refs_1_, ...), custom_call_target="tpu_custom_call" | custom-call | flops 12000000000 | bytes 12000000 | tf_op jit(solution)/shard_map/edge_part_1/pallas_call | solution.py:392
  91.1 0.9 copy-done.6
  92.0 3.1 %updated_rows.1 = f32[1024,128]{1,0:T(8,128)} custom-call(s32[1]{0:T(128)S(6)} %copy.15.count_ref, f32[88,2]{1,0:T(8,128)S(1)} %copy-done.7, f32[3,1024]{1,0:T(4,128)S(1)} %copy-done.8, bf16[256,1152]{1,0:T(8,128)(2,1)S(1)} %bitcast.10, f32[512,128]{1,0:T(8,128)S(1)} %copy-done.5, f32[512,128]{1,0:T(8,128)S(1)} %copy-done.6), custom_call_target="tpu_custom_call" | custom-call | tf_op jit(solution)/shard_map/updated_rows/pallas_call | solution.py:441
  (35 shorter events, 0.3 us)
Async XLA Ops:
  0.0 45.5 %copy-start = (f32[2048,128]{1,0:T(8,128)S(1)}, f32[2048,128]{1,0:T(8,128)}, u32[]{:S(2)}) copy-start(f32[2048,128]{1,0:T(8,128)} %param.18) | copy-start | bytes 3145732
  2.0 41.8 %collective-permute-start = (bf16[1024,128]{1,0:T(8,128)(2,1)}, bf16[1024,128]{1,0:T(8,128)(2,1)}, u32[]{:S(2)}, u32[]{:S(2)}) collective-permute-start(bf16[1024,128]{1,0:T(8,128)(2,1)} %convolution_convert_fusion.refs_0_), channel_id=1, source_target_pairs={{0,1},{1,0},{2,3},{3,2},{4,5},{5,4},{6,7},{7,6},{8,9},{9,8},{10,11... | collective-permute-start | bytes 786440 | tf_op jit(solution)/shard_map/ppermute | solution.py:464
  5.7 38.0 %collective-permute-start.1 = (bf16[1024,128]{1,0:T(8,128)(2,1)}, bf16[1024,128]{1,0:T(8,128)(2,1)}, u32[]{:S(2)}, u32[]{:S(2)}) collective-permute-start(bf16[1024,128]{1,0:T(8,128)(2,1)} %convolution_convert_fusion.refs_0_), channel_id=1, source_target_pairs={{0,7},{1,2},{2,1},{3,4},{4,3},{5,6},{6,5},{7,0},{8,15},{9,10},{10,... | collective-permute-start | bytes 786440 | tf_op jit(solution)/shard_map/ppermute | solution.py:464
  8.0 45.5 %collective-permute-start.3 = (bf16[1024,128]{1,0:T(8,128)(2,1)}, bf16[1024,128]{1,0:T(8,128)(2,1)}, u32[]{:S(2)}, u32[]{:S(2)}) collective-permute-start(bf16[1024,128]{1,0:T(8,128)(2,1)} %convolution_convert_fusion.refs_0_), channel_id=1, source_target_pairs={{0,248},{1,249},{2,250},{3,251},{4,252},{5,253},{6,254},{7,255},{8... | collective-permute-start | bytes 786440 | tf_op jit(solution)/shard_map/ppermute | solution.py:464
  10.4 43.1 %collective-permute-start.4 = (bf16[1024,128]{1,0:T(8,128)(2,1)}, bf16[1024,128]{1,0:T(8,128)(2,1)}, u32[]{:S(2)}, u32[]{:S(2)}) collective-permute-start(bf16[1024,128]{1,0:T(8,128)(2,1)} %convolution_convert_fusion.refs_0_), channel_id=1, source_target_pairs={{0,249},{1,248},{2,251},{3,250},{4,253},{5,252},{6,255},{7,254},{8... | collective-permute-start | bytes 786440 | tf_op jit(solution)/shard_map/ppermute | solution.py:464
  10.6 42.9 %collective-permute-start.5 = (bf16[1024,128]{1,0:T(8,128)(2,1)}, bf16[1024,128]{1,0:T(8,128)(2,1)}, u32[]{:S(2)}, u32[]{:S(2)}) collective-permute-start(bf16[1024,128]{1,0:T(8,128)(2,1)} %convolution_convert_fusion.refs_0_), channel_id=1, source_target_pairs={{0,255},{1,250},{2,249},{3,252},{4,251},{5,254},{6,253},{7,248},{8... | collective-permute-start | bytes 786440 | tf_op jit(solution)/shard_map/ppermute | solution.py:464
  19.5 10.6 %copy-start.2 = (f32[256,1152]{1,0:T(8,128)S(1)}, f32[256,1152]{1,0:T(8,128)}, u32[]{:S(2)}) copy-start(f32[256,1152]{1,0:T(8,128)} %factor_sums.1.after_ref) | copy-start | bytes 3538948
  19.5 10.6 %copy-start.10 = (bf16[128,128]{1,0:T(8,128)(2,1)S(1)}, bf16[128,128]{1,0:T(8,128)(2,1)}, u32[]{:S(2)}) copy-start(bf16[128,128]{1,0:T(8,128)(2,1)} %recv_ref.1) | copy-start | bytes 98308
  19.5 10.6 %copy-start.11 = (bf16[8,128]{1,0:T(8,128)(2,1)S(1)}, bf16[8,128]{1,0:T(8,128)(2,1)}, u32[]{:S(2)}) copy-start(bf16[8,128]{1,0:T(8,128)(2,1)} %wb_ref.1) | copy-start | bytes 6148
  19.6 28.9 %all-to-all-start = ((f32[32,8,1152]{2,1,0:T(8,128)}), f32[32,8,1152]{2,1,0:T(8,128)S(1)}, u32[]{:S(2)}, u32[]{:S(2)}) async-start(f32[32,8,1152]{2,1,0:T(8,128)} %bitcast.8), calls=%async_computation | async-start | bytes 2359296 | tf_op jit(solution)/shard_map/all_to_all | solution.py:499
  30.1 1.0 %copy-start.3 = (bf16[1024,128]{1,0:T(8,128)(2,1)S(1)}, bf16[1024,128]{1,0:T(8,128)(2,1)}, u32[]{:S(2)}) copy-start(bf16[1024,128]{1,0:T(8,128)(2,1)} %features_ref.1) | copy-start | bytes 786436
  31.1 1.0 %copy-start.4 = (bf16[8,32768]{1,0:T(8,128)(2,1)S(1)}, bf16[8,32768]{1,0:T(8,128)(2,1)}, u32[]{:S(2)}) copy-start(bf16[8,32768]{1,0:T(8,128)(2,1)} %basis_ref.1) | copy-start | bytes 1572868
  38.0 5.7 %copy-start.1 = (f32[32768,128]{1,0:T(8,128)}, f32[32768,128]{1,0:T(8,128)S(1)}, u32[]{:S(2)}) copy-start(f32[32768,128]{1,0:T(8,128)S(1)} %receive_rows.1.base_hbm) | copy-start | bytes 50331652
  43.7 1.5 %copy-start.12 = (s32[3,2048]{1,0:T(4,128)S(1)}, s32[3,2048]{1,0:T(4,128)}, u32[]{:S(2)}) copy-start(s32[3,2048]{1,0:T(4,128)} %param.17) | copy-start | bytes 73732
  43.7 1.6 %copy-start.13 = (s32[9,256]{1,0:T(8,128)S(1)}, s32[9,256]{1,0:T(8,128)}, u32[]{:S(2)}) copy-start(s32[9,256]{1,0:T(8,128)} %constant.41.clone) | copy-start | bytes 27652
  44.9 8.6 %collective-permute-start.2 = (bf16[3072,128]{1,0:T(8,128)(2,1)S(1)}, bf16[3072,128]{1,0:T(8,128)(2,1)}, u32[]{:S(2)}, u32[]{:S(2)}) collective-permute-start(bf16[3072,128]{1,0:T(8,128)(2,1)S(1)} %pad_maximum_fusion), channel_id=1, source_target_pairs={{0,8},{1,9},{2,10},{3,11},{4,12},{5,13},{6,14},{7,15},{8,0},{9,1},... | collective-permute-start | bytes 2359304 | tf_op jit(solution)/shard_map/ppermute | solution.py:464
  49.2 18.9 %all-to-all-start.1 = ((f32[8,8,1152]{2,1,0:T(8,128)}), f32[8,8,1152]{2,1,0:T(8,128)S(1)}, u32[]{:S(2)}, u32[]{:S(2)}) async-start(f32[8,8,1152]{2,1,0:T(8,128)} %stage_sums.1.refs_7_), calls=%async_computation.1 | async-start | bytes 589824 | tf_op jit(solution)/shard_map/all_to_all | solution.py:499
  53.5 14.6 %copy-start.9 = (f32[128,128]{1,0:T(8,128)S(1)}, f32[128,128]{1,0:T(8,128)}, u32[]{:S(2)}) copy-start(f32[128,128]{1,0:T(8,128)} %mix_hbm.1) | copy-start | bytes 196612
  69.3 21.7 %all-to-all-start.2 = ((bf16[32,8,1152]{2,1,0:T(8,128)(2,1)}), bf16[32,8,1152]{2,1,0:T(8,128)(2,1)S(1)}, u32[]{:S(2)}, u32[]{:S(2)}) async-start(bf16[32,8,1152]{2,1,0:T(8,128)(2,1)} %filter_rows.1.refs_7_), calls=%async_computation.2 | async-start | bytes 1179648 | tf_op jit(solution)/shard_map/all_to_all | solution.py:499
  76.3 14.7 %copy-start.5 = (f32[512,128]{1,0:T(8,128)S(1)}, f32[512,128]{1,0:T(8,128)}, u32[]{:S(2)}) copy-start(f32[512,128]{1,0:T(8,128)} %edge_part_0.1.refs_0_) | copy-start | bytes 786436
  76.4 14.7 %copy-start.7 = (f32[88,2]{1,0:T(8,128)S(1)}, f32[88,2]{1,0:T(8,128)}, u32[]{:S(2)}) copy-start(f32[88,2]{1,0:T(8,128)} %constant.40.clone.xy_hbm) | copy-start | bytes 2116
  76.4 14.7 %copy-start.8 = (f32[3,1024]{1,0:T(4,128)S(1)}, f32[3,1024]{1,0:T(4,128)}, u32[]{:S(2)}) copy-start(f32[3,1024]{1,0:T(4,128)} %pos_hbm.3) | copy-start | bytes 36868
  91.0 1.0 %copy-start.6 = (f32[512,128]{1,0:T(8,128)S(1)}, f32[512,128]{1,0:T(8,128)}, u32[]{:S(2)}) copy-start(f32[512,128]{1,0:T(8,128)} %edge_part_1.1.refs_1_) | copy-start | bytes 786436

commit v5 on v3

--- a/solution.py
+++ b/solution.py
@@ -15,7 +15,9 @@
 WAVE_ROWS = 2304
 DEVICES = 256
 ROWS_EACH = WAVE_ROWS // DEVICES
-PARTS = (256, 256, 512)
+HALF_ROWS = WAVE_ROWS // 2
+HALF_TOP = TOP // 2
+PARTS = (512, 512)
 PLANE = 4
 UNROLL = 16
 BUFFERS = 4
@@ -29,7 +31,7 @@
 def wave_layout():
     flat = [(0, 0)] + [(kx, 0) for kx in range(1, TOP + 1)]
     flat += [(kx, ky) for ky in range(1, TOP + 1) for kx in range(-TOP, TOP + 1)]
-    codes = np.full((WAVE_ROWS,), -1, np.int32)
+    codes = np.full((2, HALF_ROWS), -1, np.int32)
     xy = np.zeros((XY_ROWS, 2), np.float32)
 
     def code(kx, ky, kz):
@@ -38,16 +40,19 @@
     for row, (kx, ky) in enumerate(flat):
         xy[row] = kx, ky
         for kz in range(1, TOP + 1):
-            base = (kz - 1) * 4 * XY_ROWS + row
-            codes[base] = code(kx, ky, kz)
-            codes[base + 2 * XY_ROWS] = code(kx, ky, kz)
+            half, at = divmod(kz - 1, HALF_TOP)
+            base = at * 4 * XY_ROWS + row
+            codes[half, base] = code(kx, ky, kz)
+            codes[half, base + 2 * XY_ROWS] = code(kx, ky, kz)
             if row > 0:
-                codes[base + XY_ROWS] = code(-kx, -ky, kz)
-                codes[base + 3 * XY_ROWS] = code(-kx, -ky, kz)
-        base = TOP * 4 * XY_ROWS + row
-        codes[base] = code(kx, ky, 0)
+                codes[half, base + XY_ROWS] = code(-kx, -ky, kz)
+                codes[half, base + 3 * XY_ROWS] = code(-kx, -ky, kz)
+        base = HALF_TOP * 4 * XY_ROWS + row
+        codes[0, base] = code(kx, ky, 0)
         if row > 0:
-            codes[base + XY_ROWS] = code(kx, ky, 0)
+            codes[1, base] = code(kx, ky, 0)
+    each = DEVICES // 2
+    codes = codes.reshape(2, ROWS_EACH, each).transpose(1, 0, 2)
     return xy, codes.reshape(ROWS_EACH, DEVICES)
 
 
@@ -69,26 +74,34 @@
     return cosine(rest), cosine(quarter)
 
 
-def table_tile(xy_ref, pos_ref, first, width):
+def flat_waves(xy_ref, pos_ref, first, width):
     wide = (XY_ROWS, width)
     coords = [jnp.broadcast_to(pos_ref[d : d + 1, first : first + width], wide) for d in range(2)]
     flat_turns = (
         jnp.broadcast_to(xy_ref[:, 0:1], wide) * coords[0]
         + jnp.broadcast_to(xy_ref[:, 1:2], wide) * coords[1]
     )
-    cos_xy, sin_xy = turn_waves(flat_turns)
-    steps = lax.broadcasted_iota(jnp.int32, (8, width), 0).astype(jnp.float32)
+    return turn_waves(flat_turns)
+
+
+def half_table(flat, pos_ref, first, half):
+    cos_xy, sin_xy = flat
+    wide = cos_xy.shape
+    width = wide[1]
+    steps = lax.broadcasted_iota(jnp.int32, (8, width), 0) + (1 + HALF_TOP * half)
     cos_z, sin_z = turn_waves(
-        steps * jnp.broadcast_to(pos_ref[2:3, first : first + width], (8, width))
+        steps.astype(jnp.float32)
+        * jnp.broadcast_to(pos_ref[2:3, first : first + width], (8, width))
     )
     rows = []
-    for kz in range(1, TOP + 1):
-        cos_k = jnp.broadcast_to(cos_z[kz : kz + 1], wide)
-        sin_k = jnp.broadcast_to(sin_z[kz : kz + 1], wide)
+    for at in range(HALF_TOP):
+        cos_k = jnp.broadcast_to(cos_z[at : at + 1], wide)
+        sin_k = jnp.broadcast_to(sin_z[at : at + 1], wide)
         both_cos, both_sin = cos_xy * cos_k, sin_xy * sin_k
         sin_cos, cos_sin = sin_xy * cos_k, cos_xy * sin_k
         rows += [both_cos - both_sin, both_cos + both_sin, cos_sin + sin_cos, cos_sin - sin_cos]
-    rows += [cos_xy, sin_xy, jnp.zeros((WAVE_ROWS - 26 * XY_ROWS, width), jnp.float32)]
+    rows.append(jnp.where(half == 0, cos_xy, sin_xy))
+    rows.append(jnp.zeros((HALF_ROWS - (4 * HALF_TOP + 1) * XY_ROWS, width), jnp.float32))
     return jnp.concatenate(rows, axis=0).astype(jnp.bfloat16)
 
 
@@ -114,47 +127,119 @@
     return copies
 
 
-def factor_kernel(
-    count_ref, xy_hbm, pos_hbm, features_hbm, *refs
-):
-    after_refs, refs = refs[:-6], refs[-6:]
-    sums_ref, table_ref, xy_ref, pos_ref, features_ref, arrivals = refs
-    del after_refs
-    copies = loads((xy_hbm, pos_hbm, features_hbm), (xy_ref, pos_ref, features_ref), arrivals)
+def packed_rows(atoms):
+    return 3 * 8 * atoms // 128
+
+
+def prepare_kernel(count_ref, pos_hbm, features_hbm, packed_ref, *refs):
+    pos_ref, features_ref, wide_ref, arrivals = refs
+    copies = loads((pos_hbm, features_hbm), (pos_ref, features_ref), arrivals)
     atoms, channels = features_ref.shape
-    copies[0].wait()
-    copies[1].wait()
-    for first in range(0, atoms, 128):
-        table_ref[:, first : first + 128] = table_tile(xy_ref, pos_ref, first, 128)
-    copies[2].wait()
+    wide_ref[...] = jnp.zeros_like(wide_ref)
+    for copy in copies:
+        copy.wait()
     live = lax.broadcasted_iota(jnp.int32, (atoms, channels), 0) < count_ref[0]
     masked = jnp.where(live, features_ref[...].astype(jnp.float32), 0.0).astype(jnp.bfloat16)
-    for r in range(ROWS_EACH):
-        sums_ref[:, r * channels : (r + 1) * channels] = jnp.dot(
-            table_ref[r * DEVICES : (r + 1) * DEVICES, :],
-            masked,
-            preferred_element_type=jnp.float32,
-        )
-
-
-def factor_call(atom_count, positions, features, after):
+    packed_ref[0:atoms, :] = masked
+    wide_ref[0:3, :] = pos_ref[...]
+    rest = wide_ref[...]
+    pieces = []
+    for _ in range(3):
+        piece = rest.astype(jnp.bfloat16).astype(jnp.float32)
+        rest = rest - piece
+        pieces += [piece[:, at : at + 128] for at in range(0, atoms, 128)]
+    packed_ref[atoms:, :] = jnp.concatenate(pieces, axis=0).astype(jnp.bfloat16)
+
+
+def prepare_call(atom_count, positions, features):
     atoms, channels = features.shape
     return pl.pallas_call(
-        factor_kernel,
-        in_specs=[pl.BlockSpec(memory_space=pltpu.SMEM), hbm(), hbm(), hbm()]
-        + [pl.BlockSpec(memory_space=pl.ANY)] * len(after),
-        out_specs=vmem(),
-        out_shape=jax.ShapeDtypeStruct((DEVICES, ROWS_EACH * channels), jnp.float32),
+        prepare_kernel,
+        in_specs=[pl.BlockSpec(memory_space=pltpu.SMEM), hbm(), hbm()],
+        out_specs=vmem(),
+        out_shape=jax.ShapeDtypeStruct((atoms + packed_rows(atoms), channels), jnp.bfloat16),
         scratch_shapes=[
-            pltpu.VMEM((WAVE_ROWS, atoms), jnp.bfloat16),
-            pltpu.VMEM(XY.shape, jnp.float32),
             pltpu.VMEM(positions.shape, jnp.float32),
             pltpu.VMEM(features.shape, jnp.bfloat16),
+            pltpu.VMEM((8, atoms), jnp.float32),
+            pltpu.SemaphoreType.DMA((2,)),
+        ],
+        compiler_params=limit(SMALL_VMEM),
+        name="prepare_rows",
+    )(atom_count, positions, features)
+
+
+def project_kernel(packed_ref, send_ref, after_ref, out_ref):
+    del after_ref
+    rows = packed_ref[0 : out_ref.shape[0], :]
+    out_ref[...] = jnp.dot(rows, send_ref[...], preferred_element_type=jnp.float32).astype(
+        jnp.bfloat16
+    )
+
+
+def project_call(packed, w_send, atoms, after):
+    return pl.pallas_call(
+        project_kernel,
+        in_specs=[vmem(), vmem(), pl.BlockSpec(memory_space=pl.ANY)],
+        out_specs=vmem(),
+        out_shape=jax.ShapeDtypeStruct((atoms, w_send.shape[1]), jnp.bfloat16),
+        compiler_params=limit(SMALL_VMEM),
+        name="project_rows",
+    )(packed, w_send, after)
+
+
+def factor_kernel(xy_hbm, packed_any, other_any, *refs):
+    sums_ref, table_ref, xy_ref, packed_ref, pos_ref, arrivals = refs
+    copies = loads(
+        (xy_hbm, packed_any, other_any), (xy_ref, packed_ref.at[0], packed_ref.at[1]), arrivals
+    )
+    half = lax.rem(lax.axis_index("slab"), 2)
+    atoms = pos_ref.shape[1]
+    channels = packed_ref.shape[2]
+    for copy in copies:
+        copy.wait()
+    tiles = atoms // 128
+    for side in range(2):
+        values = packed_ref[side, atoms:, :].astype(jnp.float32)
+        for at in range(tiles):
+            total = None
+            for piece in range(3):
+                start = (piece * tiles + at) * 8
+                part = values[start : start + 8]
+                total = part if total is None else total + part
+            pos_ref[:, at * 128 : (at + 1) * 128] = total
+        for first in range(0, atoms, 128):
+            table_ref[:, side * atoms + first : side * atoms + first + 128] = half_table(
+                flat_waves(xy_ref, pos_ref, first, 128), pos_ref, first, half
+            )
+    each = sums_ref.shape[0]
+    for r in range(ROWS_EACH):
+        rows = table_ref[r * each : (r + 1) * each, :]
+        sums_ref[:, r * channels : (r + 1) * channels] = jnp.dot(
+            rows[:, :atoms], packed_ref[0, :atoms, :], preferred_element_type=jnp.float32
+        ) + jnp.dot(
+            rows[:, atoms:], packed_ref[1, :atoms, :], preferred_element_type=jnp.float32
+        )
+
+
+def factor_call(packed, other, atoms):
+    channels = packed.shape[1]
+    anywhere = pl.BlockSpec(memory_space=pl.ANY)
+    return pl.pallas_call(
+        factor_kernel,
+        in_specs=[hbm(), anywhere, anywhere],
+        out_specs=vmem(),
+        out_shape=jax.ShapeDtypeStruct((DEVICES // 2, ROWS_EACH * channels), jnp.float32),
+        scratch_shapes=[
+            pltpu.VMEM((HALF_ROWS, 2 * atoms), jnp.bfloat16),
+            pltpu.VMEM(XY.shape, jnp.float32),
+            pltpu.VMEM((2,) + packed.shape, jnp.bfloat16),
+            pltpu.VMEM((8, atoms), jnp.float32),
             pltpu.SemaphoreType.DMA((3,)),
         ],
-        compiler_params=limit(LARGE_VMEM),
+        compiler_params=limit(TABLE_VMEM),
         name="factor_sums",
-    )(atom_count, jnp.asarray(XY), positions, features, *after)
+    )(jnp.asarray(XY), packed, other)
 
 
 def stage_kernel(sums_ref, out_ref):
@@ -227,7 +312,7 @@
 ):
     blocks, refs = refs[:7], refs[7:]
     (after_ref, out_ref, pool_ref, radial_ref, part_ref, own_ref, wide_ref), refs = refs[:7], refs[7:]
-    local, loaded, refs = refs[:6], refs[6], refs[7:]
+    local, held, loaded, landed, refs = refs[:6], refs[6:13], refs[13], refs[14], refs[15:]
     ids_ref, basis_ref, features_ref, recv_ref, wb_ref, wo_ref = local
     buffers, arrivals = refs[:BUFFERS], refs[BUFFERS:]
     atoms, channels = out_ref.shape
@@ -244,6 +329,7 @@
         local,
         loaded,
     )
+    landing = loads(blocks, held, landed)
     edges = UNROLL * degree
     lines = edges // 128
     chunks = atoms // UNROLL
@@ -256,16 +342,6 @@
     sub_even = lax.rem(lax.axis_index("sub"), 2) == 0
     slab_place = (1, jnp.where(slab_even, 2, 0), jnp.where(slab_even, 0, 2))
     sub_place = (1, jnp.where(sub_even, 2, 0), jnp.where(sub_even, 0, 2))
-    rows = blocks[0].shape[0]
-    at = 0
-    for block in blocks:
-        for first_row in range(0, block.shape[0], rows):
-            place = pl.multiple_of((slab_place[at // 3] * 3 + sub_place[at % 3]) * rows, rows)
-            pool_ref[pl.ds(place, rows), :] = block[first_row : first_row + rows, :].astype(
-                jnp.float32
-            )
-            at += 1
-
     for copy in copies:
         copy.wait()
     for at in range(BUFFERS):
@@ -284,22 +360,40 @@
     span = groups * 128
 
     def radial_block(step, carry):
-        base = pl.multiple_of(step * span, span)
-        values = basis_ref[:, pl.ds(base, span)]
-        values = values.astype(jnp.float32)
-        stack = jnp.concatenate([values[:, g * 128 : (g + 1) * 128] for g in range(groups)], axis=0)
-        turned = stack.T.astype(jnp.bfloat16)
+        turned = []
+        for at in range(2):
+            values = basis_ref[:, pl.ds(pl.multiple_of((step * 2 + at) * span, span), span)]
+            values = values.astype(jnp.float32)
+            stack = jnp.concatenate(
+                [values[:, g * 128 : (g + 1) * 128] for g in range(groups)], axis=0
+            )
+            turned.append(stack.T.astype(jnp.bfloat16))
+        turned = jnp.concatenate(turned, axis=0)
         for g in range(0, groups, 2):
             both = jnp.dot(
                 turned,
                 wide_ref[:, g * channels : (g + 2) * channels],
                 preferred_element_type=jnp.float32,
             )
-            radial_ref[pl.ds(base + g * 128, 128), :] = both[:, :channels]
-            radial_ref[pl.ds(base + (g + 1) * 128, 128), :] = both[:, channels:]
+            for at in range(2):
+                base = pl.multiple_of((step * 2 + at) * span, span) + g * 128
+                half = both[at * 128 : (at + 1) * 128]
+                radial_ref[pl.ds(base, 128), :] = half[:, :channels]
+                radial_ref[pl.ds(base + 128, 128), :] = half[:, channels:]
         return carry
 
-    lax.fori_loop(0, atoms * degree // span, radial_block, 0)
+    lax.fori_loop(0, atoms * degree // span // 2, radial_block, 0)
+    rows = blocks[0].shape[0]
+    at = 0
+    for copy, block in zip(landing, held):
+        copy.wait()
+        for first_row in range(0, block.shape[0], rows):
+            place = pl.multiple_of((slab_place[at // 3] * 3 + sub_place[at % 3]) * rows, rows)
+            pool_ref[pl.ds(place, rows), :] = block[first_row : first_row + rows, :].astype(
+                jnp.float32
+            )
+            at += 1
+
     sublane = lax.broadcasted_iota(jnp.int32, (8, channels), 0)
     at_sublane = [sublane == r for r in range(8)]
 
@@ -350,7 +444,7 @@
     rows = sum(block.shape[0] for block in blocks)
     return pl.pallas_call(
         functools.partial(edge_kernel, degree, first),
-        in_specs=[hbm()] * 6 + [vmem()] * len(blocks) + [pl.BlockSpec(memory_space=pl.ANY)],
+        in_specs=[hbm()] * 6 + [pl.BlockSpec(memory_space=pl.ANY)] * (len(blocks) + 1),
         out_specs=vmem(),
         out_shape=jax.ShapeDtypeStruct((atoms, channels), jnp.float32),
         scratch_shapes=[
@@ -365,8 +459,9 @@
             pltpu.VMEM(w_recv.shape, jnp.bfloat16),
             pltpu.VMEM(w_basis.shape, jnp.bfloat16),
             pltpu.VMEM(w_out.shape, jnp.bfloat16),
-            pltpu.SemaphoreType.DMA((6,)),
         ]
+        + [pltpu.VMEM(block.shape, jnp.bfloat16) for block in blocks]
+        + [pltpu.SemaphoreType.DMA((6,)), pltpu.SemaphoreType.DMA((len(blocks),))]
         + [pltpu.SMEM((UNROLL * degree // 128, 128), jnp.int32)] * BUFFERS
         + [pltpu.SemaphoreType.DMA] * BUFFERS,
         compiler_params=limit(LARGE_VMEM),
@@ -383,8 +478,14 @@
     parts, (out_ref, xy_ref, pos_ref, arrivals) = refs[:-4], refs[-4:]
     copies = loads((xy_hbm, pos_hbm), (xy_ref, pos_ref), arrivals)
     channels = out_ref.shape[1]
+    each = DEVICES // 2
     factors = jnp.concatenate(
-        [factors_ref[:, r * channels : (r + 1) * channels] for r in range(ROWS_EACH)], axis=0
+        [
+            factors_ref[half * each : (half + 1) * each, r * channels : (r + 1) * channels]
+            for half in range(2)
+            for r in range(ROWS_EACH)
+        ],
+        axis=0,
     ).T
     total, first = out_ref.shape[0], 0
     for part in parts:
@@ -394,7 +495,10 @@
         copy.wait()
     atoms = 256
     for first in range(0, total, atoms):
-        table = table_tile(xy_ref, pos_ref, first, atoms)
+        flat = flat_waves(xy_ref, pos_ref, first, atoms)
+        table = jnp.concatenate(
+            [half_table(flat, pos_ref, first, half) for half in range(2)], axis=0
+        )
         field = jnp.dot(factors, table, preferred_element_type=jnp.float32)
         live = first + lax.broadcasted_iota(jnp.int32, (atoms, channels), 0) < count_ref[0]
         near = out_ref[first : first + atoms, :]
@@ -420,6 +524,25 @@
     )(atom_count, jnp.asarray(XY), positions, factors, *parts)
 
 
+def column_kernel(own_ref, near_ref, beyond_ref, after_ref, out_ref):
+    del after_ref
+    rows = own_ref.shape[0]
+    for at, block in enumerate((own_ref, near_ref, beyond_ref)):
+        out_ref[at * rows : (at + 1) * rows, :] = block[...]
+
+
+def column_call(blocks, after):
+    rows, channels = blocks[0].shape
+    return pl.pallas_call(
+        column_kernel,
+        in_specs=[vmem()] * 3 + [pl.BlockSpec(memory_space=pl.ANY)],
+        out_specs=vmem(),
+        out_shape=jax.ShapeDtypeStruct((3 * rows, channels), blocks[0].dtype),
+        compiler_params=limit(SMALL_VMEM),
+        name="column_rows",
+    )(*blocks, after)
+
+
 def moved(array, target):
     slabs, subs = lax.axis_size("slab"), lax.axis_size("sub")
     pairs = []
@@ -448,9 +571,20 @@
 
 def plane_groups(slabs, subs):
     return [
-        [(z * PLANE + q) * subs + b for b in range(subs) for q in range(PLANE)]
+        [
+            (z * PLANE + 2 * q + core) * subs + b
+            for core in range(2)
+            for b in range(subs)
+            for q in range(PLANE // 2)
+        ]
         for z in range(slabs // PLANE)
     ]
+
+
+def core_groups(slabs, subs):
+    planes = plane_groups(slabs, subs)
+    half = len(planes[0]) // 2
+    return [group[core * half : (core + 1) * half] for group in planes for core in range(2)]
 
 
 def line_groups(slabs, subs):
@@ -472,19 +606,24 @@
     atoms, channels = features.shape
     total_k = kgrid.shape[1]
     subs, slabs = lax.axis_size("sub"), lax.axis_size("slab")
-    send_proj = jnp.dot(features, w_send, preferred_element_type=jnp.float32).astype(jnp.bfloat16)
+    packed = prepare_call(atom_count, positions, features)
+    other = moved(packed, to_core)
+    send_proj = project_call(packed, w_send, atoms, other)
     outer = moved(send_proj, to_outer)
     near = moved(send_proj, to_column)
     beyond = moved(send_proj, to_beyond)
     outer_near = moved(send_proj, lambda s, b: to_outer(*to_column(s, b)))
     outer_beyond = moved(send_proj, lambda s, b: to_outer(*to_beyond(s, b)))
-    core = moved(jnp.concatenate([send_proj, near, beyond]), to_core)
+
+    plane, line = plane_groups(slabs, subs), line_groups(slabs, subs)
+    slab = lax.axis_index("slab")
+    mine = (slab % 2) * (len(plane[0]) // 2) + lax.axis_index("sub") * (PLANE // 2)
+    mine = mine + slab % PLANE // 2
+    sums = factor_call(packed, other, atoms)
+    core = moved(column_call((send_proj, near, beyond), outer_beyond), to_core)
     blocks = [send_proj, near, beyond, core, outer, outer_near, outer_beyond]
-
-    plane, line = plane_groups(slabs, subs), line_groups(slabs, subs)
-    mine = lax.axis_index("sub") * PLANE + lax.axis_index("slab") % PLANE
-    sums = factor_call(atom_count, positions, features, ())
-    stage_one = stage_call(exchanged(sums, plane), len(plane[0]), len(line[0]))
+    cores = core_groups(slabs, subs)
+    stage_one = stage_call(exchanged(sums, cores), len(cores[0]), len(line[0]))
     count = stage_one.shape[1]
     weights = wave_weights(kgrid, k_filter, mine * count, count)
     norm_factor = 1.0 / math.sqrt(atoms * DEVICES)
@@ -493,7 +632,7 @@
     )
     factors = exchanged(filtered, plane).reshape(DEVICES, -1)
 
-    after = [sums, stage_one, filtered]
+    after = [stage_one, filtered]
     parts = [
         edge_call(p, after[p], senders, edge_basis, features, w_recv, w_basis, w_out, blocks)
         for p in range(len(PARTS))

time: 105 us -> 92.1 us (0.88)
  Pallas kernels: 48.9 us -> 41.6 us
  starting transfers between devices: 44.9 us -> 37.8 us
  waiting for transfers between devices: 3.56 us -> 6.04 us
  matrix products: 2.47 us -> 0.57 us
  local copies, waits for them, and re-layouts: 2.36 us -> 4.2 us
  other arithmetic: 1.14 us -> 0.06 us
    all_to_all x3, starting transfers between devices: 32.9 us -> 24.2 us  [exchanged(): lax.all_to_all(array, ('slab', 'sub'), 0, 0, axis_index_groups=groups, ti...]
    pallas_call x3 -> x2, Pallas kernels: 38.6 us -> 31.6 us  [edge_call(): pl.pallas_call(functools.partial(edge_kernel, degree, first), in_specs=[h...]
    ppermute x6 -> x7, waiting for transfers between devices: 0.02 us -> 6.03 us  [moved(): return lax.ppermute(array, ('slab', 'sub'), pairs)]
    all_to_all x3, waiting for transfers between devices: 3.55 us -> 0.01 us  [exchanged(): lax.all_to_all(array, ('slab', 'sub'), 0, 0, axis_index_groups=groups, ti...]
    unnamed x20 -> x34, local copies, waits for them, and re-layouts: 0.99 us -> 4.05 us
    ppermute x6 -> x7, starting transfers between devices: 12.1 us -> 13.7 us  [moved(): return lax.ppermute(array, ('slab', 'sub'), pairs)]
    dot_general x1 -> x0, matrix products: 1.25 us -> none  [per_device(): jnp.dot(features, w_send, preferred_element_type=jnp.float32)]
    concatenate x1 -> x0, other arithmetic: 1.09 us -> none  [per_device(): core = moved(jnp.concatenate([send_proj, near, beyond]), to_core)]
  transfers between devices with their start and end apart: 9 -> 10, of which waited for: 1 -> 2; matrix products, arithmetic and copies ran while one was open for 4% -> 1% of each run, Pallas kernels for 42% -> 40%
where the time goes in v5:
time: 92.1 us; the launch traced here: 91.6 us
  Pallas kernels  41.6 us (45%)
  starting transfers between devices  37.8 us (41%)
  waiting for transfers between devices  6.04 us (7%)
  local copies, waits for them, and re-layouts  4.2 us (5%)
  between operations  1.23 us (1%)
    pallas_call x2, Pallas kernels, edge_call(): pl.pallas_call(functools.partial(edge_kernel, degree, first), in_specs=[h...  31.6 us
    all_to_all x3, starting transfers between devices, exchanged(): lax.all_to_all(array, ('slab', 'sub'), 0, 0, axis_index_groups=groups, ti...  24.2 us
    ppermute x7, starting transfers between devices, moved(): return lax.ppermute(array, ('slab', 'sub'), pairs)  13.7 us
    ppermute x7, waiting for transfers between devices, moved(): return lax.ppermute(array, ('slab', 'sub'), pairs)  6.03 us
    pallas_call x1, Pallas kernels, factor_call(): pl.pallas_call(factor_kernel, in_specs=[hbm(), anywhere, anywhere], out_s...  4.5 us
    unnamed x34, local copies, waits for them, and re-layouts  4.05 us
    pallas_call x1, Pallas kernels, final_call(): pl.pallas_call(functools.partial(final_kernel, scale), in_specs=[pl.Block...  3.1 us
  transfers between devices with their start and end apart: 10, of which 2 were waited for; matrix products, arithmetic and copies ran while one was open for 1% of the time, Pallas kernels for 40%

profile of v5, /device:TPU:1, one launch (start us, length us, event | category | flops | bytes accessed | tf_op | source)
XLA Modules:
  0.0 91.6 jit_solution(581974265891549932)
XLA Ops:
  0.8 0.9 %copy-done.7 = bf16[1024,128]{1,0:T(8,128)(2,1)S(1)} copy-done((bf16[1024,128]{1,0:T(8,128)(2,1)S(1)}, bf16[1024,128]{1,0:T(8,128)(2,1)}, u32[]{:S(2)}) %copy-start.7) | copy-done | bytes 262168
  1.7 0.7 copy-done.9
  2.6 3.3 %collective-permute-start = (bf16[1216,128]{1,0:T(8,128)(2,1)S(1)}, bf16[1216,128]{1,0:T(8,128)(2,1)S(1)}, u32[]{:S(2)}, u32[]{:S(2)}) collective-permute-start(bf16[1216,128]{1,0:T(8,128)(2,1)S(1)} %prepare_rows.1.packed_any.packed_ref), channel_id=1, source_target_pairs={{0,8},{1,9},{2,10},{3,11},{4,12},{5,13},{6,14},{7,15},{8,0},{9,1},... | collective-permute-start | bytes 933896 | tf_op jit(solution)/shard_map/ppermute | solution.py:553
  6.0 1.2 %collective-permute-done.other_any.after_ref = bf16[1216,128]{1,0:T(8,128)(2,1)S(1)} collective-permute-done((bf16[1216,128]{1,0:T(8,128)(2,1)S(1)}, bf16[1216,128]{1,0:T(8,128)(2,1)S(1)}, u32[]{:S(2)}, u32[]{:S(2)}) %collective-permute-start) | collective-permute-done | bytes 311328 | tf_op jit(solution)/shard_map/ppermute | solution.py:553
  7.2 0.2 project_rows.1.own_ref.refs_0_
  7.4 1.3 %collective-permute-start.1 = (bf16[1024,128]{1,0:T(8,128)(2,1)S(1)}, bf16[1024,128]{1,0:T(8,128)(2,1)S(1)}, u32[]{:S(2)}, u32[]{:S(2)}) collective-permute-start(bf16[1024,128]{1,0:T(8,128)(2,1)S(1)} %project_rows.1.own_ref.refs_0_), channel_id=1, source_target_pairs={{0,1},{1,0},{2,3},{3,2},{4,5},{5,4},{6,7},{7,6},{8,9},{9,8},{10,11... | collective-permute-start | bytes 786440 | tf_op jit(solution)/shard_map/ppermute | solution.py:553
  8.7 2.3 %collective-permute-start.2 = (bf16[1024,128]{1,0:T(8,128)(2,1)S(1)}, bf16[1024,128]{1,0:T(8,128)(2,1)S(1)}, u32[]{:S(2)}, u32[]{:S(2)}) collective-permute-start(bf16[1024,128]{1,0:T(8,128)(2,1)S(1)} %project_rows.1.own_ref.refs_0_), channel_id=1, source_target_pairs={{0,7},{1,2},{2,1},{3,4},{4,3},{5,6},{6,5},{7,0},{8,15},{9,10},{10,... | collective-permute-start | bytes 786440 | tf_op jit(solution)/shard_map/ppermute | solution.py:553
  11.0 3.4 %collective-permute-start.3 = (bf16[1024,128]{1,0:T(8,128)(2,1)S(1)}, bf16[1024,128]{1,0:T(8,128)(2,1)S(1)}, u32[]{:S(2)}, u32[]{:S(2)}) collective-permute-start(bf16[1024,128]{1,0:T(8,128)(2,1)S(1)} %project_rows.1.own_ref.refs_0_), channel_id=1, source_target_pairs={{0,255},{1,250},{2,249},{3,252},{4,251},{5,254},{6,253},{7,248},{8... | collective-permute-start | bytes 786440 | tf_op jit(solution)/shard_map/ppermute | solution.py:553
  14.4 4.5 %factor_sums.1 = f32[128,1152]{1,0:T(8,128)} custom-call(f32[88,2]{1,0:T(8,128)S(1)} %copy-done.8, bf16[1216,128]{1,0:T(8,128)(2,1)S(1)} %prepare_rows.1.packed_any.packed_ref, bf16[1216,128]{1,0:T(8,128)(2,1)S(1)} %collective-permute-done.other_any.after_ref), custom_call_target="tpu_custom_call" | custom-call | tf_op jit(solution)/shard_map/factor_sums/pallas_call | solution.py:228
  18.9 4.9 %all-to-all-start = ((f32[16,8,1152]{2,1,0:T(8,128)}), f32[16,8,1152]{2,1,0:T(8,128)S(1)}, u32[]{:S(2)}, u32[]{:S(2)}) async-start(f32[16,8,1152]{2,1,0:T(8,128)} %bitcast), calls=%async_computation | async-start | bytes 1179648 | tf_op jit(solution)/shard_map/all_to_all | solution.py:599
  23.9 4.8 %collective-permute-done.3.after_ref.refs_6_ = bf16[1024,128]{1,0:T(8,128)(2,1)S(1)} collective-permute-done((bf16[1024,128]{1,0:T(8,128)(2,1)S(1)}, bf16[1024,128]{1,0:T(8,128)(2,1)S(1)}, u32[]{:S(2)}, u32[]{:S(2)}) %collective-permute-start.3) | collective-permute-done | bytes 262176 | tf_op jit(solution)/shard_map/ppermute | solution.py:553
  28.7 0.6 copy-done.4
  29.5 1.2 %collective-permute-start.5 = (bf16[1024,128]{1,0:T(8,128)(2,1)S(1)}, bf16[1024,128]{1,0:T(8,128)(2,1)S(1)}, u32[]{:S(2)}, u32[]{:S(2)}) collective-permute-start(bf16[1024,128]{1,0:T(8,128)(2,1)S(1)} %project_rows.1.own_ref.refs_0_), channel_id=1, source_target_pairs={{0,248},{1,249},{2,250},{3,251},{4,252},{5,253},{6,254},{7,255},{8... | collective-permute-start | bytes 786440 | tf_op jit(solution)/shard_map/ppermute | solution.py:553
  30.7 2.2 %collective-permute-start.6 = (bf16[1024,128]{1,0:T(8,128)(2,1)S(1)}, bf16[1024,128]{1,0:T(8,128)(2,1)S(1)}, u32[]{:S(2)}, u32[]{:S(2)}) collective-permute-start(bf16[1024,128]{1,0:T(8,128)(2,1)S(1)} %project_rows.1.own_ref.refs_0_), channel_id=1, source_target_pairs={{0,249},{1,248},{2,251},{3,250},{4,253},{5,252},{6,255},{7,254},{8... | collective-permute-start | bytes 786440 | tf_op jit(solution)/shard_map/ppermute | solution.py:553
  33.0 0.6 fusion.weight_ref
  33.6 0.8 stage_sums.1.refs_7_
  34.4 10.5 %all-to-all-start.1 = ((f32[8,8,1152]{2,1,0:T(8,128)}), f32[8,8,1152]{2,1,0:T(8,128)S(1)}, u32[]{:S(2)}, u32[]{:S(2)}) async-start(f32[8,8,1152]{2,1,0:T(8,128)} %stage_sums.1.refs_7_), calls=%async_computation.1 | async-start | bytes 589824 | tf_op jit(solution)/shard_map/all_to_all | solution.py:599
  44.9 0.7 copy-done.15
  45.7 15.8 %edge_part_0.1.refs_0_ = f32[512,128]{1,0:T(8,128)} custom-call(s32[256,128]{1,0:T(8,128)} %bitcast.9, bf16[8,32768]{1,0:T(8,128)(2,1)} %basis_hbm.3, bf16[1024,128]{1,0:T(8,128)(2,1)} %features_hbm.5, bf16[128,128]{1,0:T(8,128)(2,1)} %recv_hbm.3, bf16[8,128]{1,0:T(8,128)(2,1)} %wb_hbm.3, bf16[128,128]{1,0:T(8,128)(2,1)} %wo_hbm.3, ...), custom_call_target="tpu_custom_call" | custom-call | flops 8000000000 | bytes 4000000 | tf_op jit(solution)/shard_map/edge_part_0/pallas_call | solution.py:445
  61.5 1.2 %filter_rows.1.refs_7_ = bf16[32,8,1152]{2,1,0:T(8,128)(2,1)} custom-call(f32[8,8,1152]{2,1,0:T(8,128)S(1)} %all-to-all-done.1.sums_ref, f32[72,128]{1,0:T(8,128)S(1)} %fusion.weight_ref, f32[128,128]{1,0:T(8,128)S(1)} %copy-done.11), custom_call_target="tpu_custom_call" | custom-call | tf_op jit(solution)/shard_map/filter_rows/pallas_call | solution.py:289
  62.7 8.8 %all-to-all-start.2 = ((bf16[32,8,1152]{2,1,0:T(8,128)(2,1)}), bf16[32,8,1152]{2,1,0:T(8,128)(2,1)S(1)}, u32[]{:S(2)}, u32[]{:S(2)}) async-start(bf16[32,8,1152]{2,1,0:T(8,128)(2,1)} %filter_rows.1.refs_7_), calls=%async_computation.2 | async-start | bytes 1179648 | tf_op jit(solution)/shard_map/all_to_all | solution.py:599
  71.5 15.8 %edge_part_1.1.refs_1_ = f32[512,128]{1,0:T(8,128)} custom-call(s32[256,128]{1,0:T(8,128)} %bitcast.10, bf16[8,32768]{1,0:T(8,128)(2,1)} %basis_hbm.3, bf16[1024,128]{1,0:T(8,128)(2,1)} %features_hbm.5, bf16[128,128]{1,0:T(8,128)(2,1)} %recv_hbm.3, bf16[8,128]{1,0:T(8,128)(2,1)} %wb_hbm.3, bf16[128,128]{1,0:T(8,128)(2,1)} %wo_hbm.3, ...), custom_call_target="tpu_custom_call" | custom-call | flops 8000000000 | bytes 4000000 | tf_op jit(solution)/shard_map/edge_part_1/pallas_call | solution.py:445
  87.4 0.9 %copy-done.6 = f32[512,128]{1,0:T(8,128)S(1)} copy-done((f32[512,128]{1,0:T(8,128)S(1)}, f32[512,128]{1,0:T(8,128)}, u32[]{:S(2)}) %copy-start.6) | copy-done | bytes 262168
  88.3 3.1 %updated_rows.1 = f32[1024,128]{1,0:T(8,128)} custom-call(s32[1]{0:T(128)S(6)} %copy.15.count_ref, f32[88,2]{1,0:T(8,128)S(1)} %copy-done.8, f32[3,1024]{1,0:T(4,128)S(1)} %copy-done.10, bf16[256,1152]{1,0:T(8,128)(2,1)S(1)} %bitcast.7, f32[512,128]{1,0:T(8,128)S(1)} %copy-done.5, f32[512,128]{1,0:T(8,128)S(1)} %copy-done.6), custom_call_target="tpu_custom_call" | custom-call | tf_op jit(solution)/shard_map/updated_rows/pallas_call | solution.py:511
  (43 shorter events, 0.6 us)
Async XLA Ops:
  0.0 33.0 %copy-start = (f32[2048,128]{1,0:T(8,128)S(1)}, f32[2048,128]{1,0:T(8,128)}, u32[]{:S(2)}) copy-start(f32[2048,128]{1,0:T(8,128)} %param.18) | copy-start | bytes 3145732
  0.7 1.0 %copy-start.7 = (bf16[1024,128]{1,0:T(8,128)(2,1)S(1)}, bf16[1024,128]{1,0:T(8,128)(2,1)}, u32[]{:S(2)}) copy-start(bf16[1024,128]{1,0:T(8,128)(2,1)} %features_hbm.5) | copy-start | bytes 786436
  2.4 4.8 %copy-start.12 = (bf16[128,128]{1,0:T(8,128)(2,1)S(1)}, bf16[128,128]{1,0:T(8,128)(2,1)}, u32[]{:S(2)}) copy-start(bf16[128,128]{1,0:T(8,128)(2,1)} %send_ref.1) | copy-start | bytes 98308
  2.6 11.8 %copy-start.8 = (f32[88,2]{1,0:T(8,128)S(1)}, f32[88,2]{1,0:T(8,128)}, u32[]{:S(2)}) copy-start(f32[88,2]{1,0:T(8,128)} %constant.61.clone.xy_hbm) | copy-start | bytes 2116
  2.6 4.6 %collective-permute-start = (bf16[1216,128]{1,0:T(8,128)(2,1)S(1)}, bf16[1216,128]{1,0:T(8,128)(2,1)S(1)}, u32[]{:S(2)}, u32[]{:S(2)}) collective-permute-start(bf16[1216,128]{1,0:T(8,128)(2,1)S(1)} %prepare_rows.1.packed_any.packed_ref), channel_id=1, source_target_pairs={{0,8},{1,9},{2,10},{3,11},{4,12},{5,13},{6,14},{7,15},{8,0},{9,1},... | collective-permute-start | bytes 933896 | tf_op jit(solution)/shard_map/ppermute | solution.py:553
  7.4 23.3 %copy-start.1 = (bf16[1024,128]{1,0:T(8,128)(2,1)}, bf16[1024,128]{1,0:T(8,128)(2,1)S(1)}, u32[]{:S(2)}) copy-start(bf16[1024,128]{1,0:T(8,128)(2,1)S(1)} %project_rows.1.own_ref.refs_0_) | copy-start | bytes 786436
  7.4 16.4 %collective-permute-start.1 = (bf16[1024,128]{1,0:T(8,128)(2,1)S(1)}, bf16[1024,128]{1,0:T(8,128)(2,1)S(1)}, u32[]{:S(2)}, u32[]{:S(2)}) collective-permute-start(bf16[1024,128]{1,0:T(8,128)(2,1)S(1)} %project_rows.1.own_ref.refs_0_), channel_id=1, source_target_pairs={{0,1},{1,0},{2,3},{3,2},{4,5},{5,4},{6,7},{7,6},{8,9},{9,8},{10,11... | collective-permute-start | bytes 786440 | tf_op jit(solution)/shard_map/ppermute | solution.py:553
  8.7 15.2 %collective-permute-start.2 = (bf16[1024,128]{1,0:T(8,128)(2,1)S(1)}, bf16[1024,128]{1,0:T(8,128)(2,1)S(1)}, u32[]{:S(2)}, u32[]{:S(2)}) collective-permute-start(bf16[1024,128]{1,0:T(8,128)(2,1)S(1)} %project_rows.1.own_ref.refs_0_), channel_id=1, source_target_pairs={{0,7},{1,2},{2,1},{3,4},{4,3},{5,6},{6,5},{7,0},{8,15},{9,10},{10,... | collective-permute-start | bytes 786440 | tf_op jit(solution)/shard_map/ppermute | solution.py:553
  11.0 17.7 %collective-permute-start.3 = (bf16[1024,128]{1,0:T(8,128)(2,1)S(1)}, bf16[1024,128]{1,0:T(8,128)(2,1)S(1)}, u32[]{:S(2)}, u32[]{:S(2)}) collective-permute-start(bf16[1024,128]{1,0:T(8,128)(2,1)S(1)} %project_rows.1.own_ref.refs_0_), channel_id=1, source_target_pairs={{0,255},{1,250},{2,249},{3,252},{4,251},{5,254},{6,253},{7,248},{8... | collective-permute-start | bytes 786440 | tf_op jit(solution)/shard_map/ppermute | solution.py:553
  18.9 14.7 %all-to-all-start = ((f32[16,8,1152]{2,1,0:T(8,128)}), f32[16,8,1152]{2,1,0:T(8,128)S(1)}, u32[]{:S(2)}, u32[]{:S(2)}) async-start(f32[16,8,1152]{2,1,0:T(8,128)} %bitcast), calls=%async_computation | async-start | bytes 1179648 | tf_op jit(solution)/shard_map/all_to_all | solution.py:599
  23.8 5.6 %copy-start.13 = (s32[3,2048]{1,0:T(4,128)S(1)}, s32[3,2048]{1,0:T(4,128)}, u32[]{:S(2)}) copy-start(s32[3,2048]{1,0:T(4,128)} %param.17) | copy-start | bytes 73732
  23.8 4.9 %copy-start.2 = (bf16[1024,128]{1,0:T(8,128)(2,1)}, bf16[1024,128]{1,0:T(8,128)(2,1)S(1)}, u32[]{:S(2)}) copy-start(bf16[1024,128]{1,0:T(8,128)(2,1)S(1)} %collective-permute-done.1.near_ref.refs_1_) | copy-start | bytes 786436
  23.8 4.9 %copy-start.3 = (bf16[1024,128]{1,0:T(8,128)(2,1)}, bf16[1024,128]{1,0:T(8,128)(2,1)S(1)}, u32[]{:S(2)}) copy-start(bf16[1024,128]{1,0:T(8,128)(2,1)S(1)} %collective-permute-done.2.beyond_ref.refs_2_) | copy-start | bytes 786436
  29.4 15.5 %collective-permute-start.4 = (bf16[3072,128]{1,0:T(8,128)(2,1)S(1)}, bf16[3072,128]{1,0:T(8,128)(2,1)}, u32[]{:S(2)}, u32[]{:S(2)}) collective-permute-start(bf16[3072,128]{1,0:T(8,128)(2,1)S(1)} %column_rows.1), channel_id=1, source_target_pairs={{0,8},{1,9},{2,10},{3,11},{4,12},{5,13},{6,14},{7,15},{8,0},{9,1},... | collective-permute-start | bytes 2359304 | tf_op jit(solution)/shard_map/ppermute | solution.py:553
  29.4 3.4 %copy-start.14 = (s32[9,256]{1,0:T(8,128)S(1)}, s32[9,256]{1,0:T(8,128)}, u32[]{:S(2)}) copy-start(s32[9,256]{1,0:T(8,128)} %constant.62.clone) | copy-start | bytes 27652
  29.5 15.4 %collective-permute-start.5 = (bf16[1024,128]{1,0:T(8,128)(2,1)S(1)}, bf16[1024,128]{1,0:T(8,128)(2,1)S(1)}, u32[]{:S(2)}, u32[]{:S(2)}) collective-permute-start(bf16[1024,128]{1,0:T(8,128)(2,1)S(1)} %project_rows.1.own_ref.refs_0_), channel_id=1, source_target_pairs={{0,248},{1,249},{2,250},{3,251},{4,252},{5,253},{6,254},{7,255},{8... | collective-permute-start | bytes 786440 | tf_op jit(solution)/shard_map/ppermute | solution.py:553
  30.7 14.2 %collective-permute-start.6 = (bf16[1024,128]{1,0:T(8,128)(2,1)S(1)}, bf16[1024,128]{1,0:T(8,128)(2,1)S(1)}, u32[]{:S(2)}, u32[]{:S(2)}) collective-permute-start(bf16[1024,128]{1,0:T(8,128)(2,1)S(1)} %project_rows.1.own_ref.refs_0_), channel_id=1, source_target_pairs={{0,249},{1,248},{2,251},{3,250},{4,253},{5,252},{6,255},{7,254},{8... | collective-permute-start | bytes 786440 | tf_op jit(solution)/shard_map/ppermute | solution.py:553
  34.4 27.1 %all-to-all-start.1 = ((f32[8,8,1152]{2,1,0:T(8,128)}), f32[8,8,1152]{2,1,0:T(8,128)S(1)}, u32[]{:S(2)}, u32[]{:S(2)}) async-start(f32[8,8,1152]{2,1,0:T(8,128)} %stage_sums.1.refs_7_), calls=%async_computation.1 | async-start | bytes 589824 | tf_op jit(solution)/shard_map/all_to_all | solution.py:599
  44.9 0.8 copy-start.16
  45.7 15.8 %copy-start.11 = (f32[128,128]{1,0:T(8,128)S(1)}, f32[128,128]{1,0:T(8,128)}, u32[]{:S(2)}) copy-start(f32[128,128]{1,0:T(8,128)} %mix_hbm.1) | copy-start | bytes 196612
  62.7 24.6 %all-to-all-start.2 = ((bf16[32,8,1152]{2,1,0:T(8,128)(2,1)}), bf16[32,8,1152]{2,1,0:T(8,128)(2,1)S(1)}, u32[]{:S(2)}, u32[]{:S(2)}) async-start(bf16[32,8,1152]{2,1,0:T(8,128)(2,1)} %filter_rows.1.refs_7_), calls=%async_computation.2 | async-start | bytes 1179648 | tf_op jit(solution)/shard_map/all_to_all | solution.py:599
  71.5 15.8 %copy-start.5 = (f32[512,128]{1,0:T(8,128)S(1)}, f32[512,128]{1,0:T(8,128)}, u32[]{:S(2)}) copy-start(f32[512,128]{1,0:T(8,128)} %edge_part_0.1.refs_0_) | copy-start | bytes 786436
  71.5 15.8 %copy-start.10 = (f32[3,1024]{1,0:T(4,128)S(1)}, f32[3,1024]{1,0:T(4,128)}, u32[]{:S(2)}) copy-start(f32[3,1024]{1,0:T(4,128)} %pos_hbm.3) | copy-start | bytes 36868
  87.4 1.0 %copy-start.6 = (f32[512,128]{1,0:T(8,128)S(1)}, f32[512,128]{1,0:T(8,128)}, u32[]{:S(2)}) copy-start(f32[512,128]{1,0:T(8,128)} %edge_part_1.1.refs_1_) | copy-start | bytes 786436
  (3 other events, 2.1 us)

commit v6 on v5

--- a/solution.py
+++ b/solution.py
@@ -19,8 +19,8 @@
 HALF_TOP = TOP // 2
 PARTS = (512, 512)
 PLANE = 4
-UNROLL = 16
-BUFFERS = 4
+UNROLL = 32
+BUFFERS = 2
 COS_TERMS = (
     0.999999989059022, -19.7392044994538, 64.93911745989, -85.4501395308031,
     60.1676309503793, -25.9675992464965, 6.52865815867317,
@@ -361,8 +361,8 @@
 
     def radial_block(step, carry):
         turned = []
-        for at in range(2):
-            values = basis_ref[:, pl.ds(pl.multiple_of((step * 2 + at) * span, span), span)]
+        for at in range(4):
+            values = basis_ref[:, pl.ds(pl.multiple_of((step * 4 + at) * span, span), span)]
             values = values.astype(jnp.float32)
             stack = jnp.concatenate(
                 [values[:, g * 128 : (g + 1) * 128] for g in range(groups)], axis=0
@@ -375,14 +375,14 @@
                 wide_ref[:, g * channels : (g + 2) * channels],
                 preferred_element_type=jnp.float32,
             )
-            for at in range(2):
-                base = pl.multiple_of((step * 2 + at) * span, span) + g * 128
+            for at in range(4):
+                base = pl.multiple_of((step * 4 + at) * span, span) + g * 128
                 half = both[at * 128 : (at + 1) * 128]
                 radial_ref[pl.ds(base, 128), :] = half[:, :channels]
                 radial_ref[pl.ds(base + 128, 128), :] = half[:, channels:]
         return carry
 
-    lax.fori_loop(0, atoms * degree // span // 2, radial_block, 0)
+    lax.fori_loop(0, atoms * degree // span // 4, radial_block, 0)
     rows = blocks[0].shape[0]
     at = 0
     for copy, block in zip(landing, held):

time: 92.1 us -> 90.5 us (0.983)
  Pallas kernels: 41.6 us -> 40 us
    pallas_call x2, Pallas kernels: 31.6 us -> 30 us  [edge_call(): pl.pallas_call(functools.partial(edge_kernel, degree, first), in_specs=[h...]
  transfers between devices with their start and end apart: 10 -> 10, of which waited for: 2 -> 2; matrix products, arithmetic and copies ran while one was open for 1% -> 1% of each run, Pallas kernels for 40% -> 39%
where the time goes in v6:
time: 90.5 us; the launch traced here: 89.9 us
  Pallas kernels  40 us (44%)
  starting transfers between devices  37.8 us (42%)
  waiting for transfers between devices  6.04 us (7%)
  local copies, waits for them, and re-layouts  4.2 us (5%)
  between operations  1.23 us (1%)
    pallas_call x2, Pallas kernels, edge_call(): pl.pallas_call(functools.partial(edge_kernel, degree, first), in_specs=[h...  30 us
    all_to_all x3, starting transfers between devices, exchanged(): lax.all_to_all(array, ('slab', 'sub'), 0, 0, axis_index_groups=groups, ti...  24.1 us
    ppermute x7, starting transfers between devices, moved(): return lax.ppermute(array, ('slab', 'sub'), pairs)  13.7 us
    ppermute x7, waiting for transfers between devices, moved(): return lax.ppermute(array, ('slab', 'sub'), pairs)  6.03 us
    pallas_call x1, Pallas kernels, factor_call(): pl.pallas_call(factor_kernel, in_specs=[hbm(), anywhere, anywhere], out_s...  4.5 us
    unnamed x34, local copies, waits for them, and re-layouts  4.05 us
    pallas_call x1, Pallas kernels, final_call(): pl.pallas_call(functools.partial(final_kernel, scale), in_specs=[pl.Block...  3.11 us
  transfers between devices with their start and end apart: 10, of which 2 were waited for; matrix products, arithmetic and copies ran while one was open for 1% of the time, Pallas kernels for 39%

profile of v6, /device:TPU:1, one launch (start us, length us, event | category | flops | bytes accessed | tf_op | source)
XLA Modules:
  0.0 89.9 jit_solution(14132742172461877721)
XLA Ops:
  0.8 0.9 %copy-done.7 = bf16[1024,128]{1,0:T(8,128)(2,1)S(1)} copy-done((bf16[1024,128]{1,0:T(8,128)(2,1)S(1)}, bf16[1024,128]{1,0:T(8,128)(2,1)}, u32[]{:S(2)}) %copy-start.7) | copy-done | bytes 262168
  1.7 0.7 copy-done.9
  2.6 3.3 %collective-permute-start = (bf16[1216,128]{1,0:T(8,128)(2,1)S(1)}, bf16[1216,128]{1,0:T(8,128)(2,1)S(1)}, u32[]{:S(2)}, u32[]{:S(2)}) collective-permute-start(bf16[1216,128]{1,0:T(8,128)(2,1)S(1)} %prepare_rows.1.packed_any.packed_ref), channel_id=1, source_target_pairs={{0,8},{1,9},{2,10},{3,11},{4,12},{5,13},{6,14},{7,15},{8,0},{9,1},... | collective-permute-start | bytes 933896 | tf_op jit(solution)/shard_map/ppermute | solution.py:553
  6.0 1.2 %collective-permute-done.other_any.after_ref = bf16[1216,128]{1,0:T(8,128)(2,1)S(1)} collective-permute-done((bf16[1216,128]{1,0:T(8,128)(2,1)S(1)}, bf16[1216,128]{1,0:T(8,128)(2,1)S(1)}, u32[]{:S(2)}, u32[]{:S(2)}) %collective-permute-start) | collective-permute-done | bytes 311328 | tf_op jit(solution)/shard_map/ppermute | solution.py:553
  7.2 0.2 project_rows.1.own_ref.refs_0_
  7.4 1.3 %collective-permute-start.1 = (bf16[1024,128]{1,0:T(8,128)(2,1)S(1)}, bf16[1024,128]{1,0:T(8,128)(2,1)S(1)}, u32[]{:S(2)}, u32[]{:S(2)}) collective-permute-start(bf16[1024,128]{1,0:T(8,128)(2,1)S(1)} %project_rows.1.own_ref.refs_0_), channel_id=1, source_target_pairs={{0,1},{1,0},{2,3},{3,2},{4,5},{5,4},{6,7},{7,6},{8,9},{9,8},{10,11... | collective-permute-start | bytes 786440 | tf_op jit(solution)/shard_map/ppermute | solution.py:553
  8.7 2.3 %collective-permute-start.2 = (bf16[1024,128]{1,0:T(8,128)(2,1)S(1)}, bf16[1024,128]{1,0:T(8,128)(2,1)S(1)}, u32[]{:S(2)}, u32[]{:S(2)}) collective-permute-start(bf16[1024,128]{1,0:T(8,128)(2,1)S(1)} %project_rows.1.own_ref.refs_0_), channel_id=1, source_target_pairs={{0,7},{1,2},{2,1},{3,4},{4,3},{5,6},{6,5},{7,0},{8,15},{9,10},{10,... | collective-permute-start | bytes 786440 | tf_op jit(solution)/shard_map/ppermute | solution.py:553
  11.0 3.4 %collective-permute-start.3 = (bf16[1024,128]{1,0:T(8,128)(2,1)S(1)}, bf16[1024,128]{1,0:T(8,128)(2,1)S(1)}, u32[]{:S(2)}, u32[]{:S(2)}) collective-permute-start(bf16[1024,128]{1,0:T(8,128)(2,1)S(1)} %project_rows.1.own_ref.refs_0_), channel_id=1, source_target_pairs={{0,255},{1,250},{2,249},{3,252},{4,251},{5,254},{6,253},{7,248},{8... | collective-permute-start | bytes 786440 | tf_op jit(solution)/shard_map/ppermute | solution.py:553
  14.4 4.5 %factor_sums.1 = f32[128,1152]{1,0:T(8,128)} custom-call(f32[88,2]{1,0:T(8,128)S(1)} %copy-done.8, bf16[1216,128]{1,0:T(8,128)(2,1)S(1)} %prepare_rows.1.packed_any.packed_ref, bf16[1216,128]{1,0:T(8,128)(2,1)S(1)} %collective-permute-done.other_any.after_ref), custom_call_target="tpu_custom_call" | custom-call | tf_op jit(solution)/shard_map/factor_sums/pallas_call | solution.py:228
  18.9 4.9 %all-to-all-start = ((f32[16,8,1152]{2,1,0:T(8,128)}), f32[16,8,1152]{2,1,0:T(8,128)S(1)}, u32[]{:S(2)}, u32[]{:S(2)}) async-start(f32[16,8,1152]{2,1,0:T(8,128)} %bitcast), calls=%async_computation | async-start | bytes 1179648 | tf_op jit(solution)/shard_map/all_to_all | solution.py:599
  23.9 4.8 %collective-permute-done.3.after_ref.refs_6_ = bf16[1024,128]{1,0:T(8,128)(2,1)S(1)} collective-permute-done((bf16[1024,128]{1,0:T(8,128)(2,1)S(1)}, bf16[1024,128]{1,0:T(8,128)(2,1)S(1)}, u32[]{:S(2)}, u32[]{:S(2)}) %collective-permute-start.3) | collective-permute-done | bytes 262176 | tf_op jit(solution)/shard_map/ppermute | solution.py:553
  28.7 0.6 copy-done.4
  29.5 1.2 %collective-permute-start.5 = (bf16[1024,128]{1,0:T(8,128)(2,1)S(1)}, bf16[1024,128]{1,0:T(8,128)(2,1)S(1)}, u32[]{:S(2)}, u32[]{:S(2)}) collective-permute-start(bf16[1024,128]{1,0:T(8,128)(2,1)S(1)} %project_rows.1.own_ref.refs_0_), channel_id=1, source_target_pairs={{0,248},{1,249},{2,250},{3,251},{4,252},{5,253},{6,254},{7,255},{8... | collective-permute-start | bytes 786440 | tf_op jit(solution)/shard_map/ppermute | solution.py:553
  30.7 2.2 %collective-permute-start.6 = (bf16[1024,128]{1,0:T(8,128)(2,1)S(1)}, bf16[1024,128]{1,0:T(8,128)(2,1)S(1)}, u32[]{:S(2)}, u32[]{:S(2)}) collective-permute-start(bf16[1024,128]{1,0:T(8,128)(2,1)S(1)} %project_rows.1.own_ref.refs_0_), channel_id=1, source_target_pairs={{0,249},{1,248},{2,251},{3,250},{4,253},{5,252},{6,255},{7,254},{8... | collective-permute-start | bytes 786440 | tf_op jit(solution)/shard_map/ppermute | solution.py:553
  33.0 0.6 fusion.weight_ref
  33.6 0.8 stage_sums.1.refs_7_
  34.4 10.5 %all-to-all-start.1 = ((f32[8,8,1152]{2,1,0:T(8,128)}), f32[8,8,1152]{2,1,0:T(8,128)S(1)}, u32[]{:S(2)}, u32[]{:S(2)}) async-start(f32[8,8,1152]{2,1,0:T(8,128)} %stage_sums.1.refs_7_), calls=%async_computation.1 | async-start | bytes 589824 | tf_op jit(solution)/shard_map/all_to_all | solution.py:599
  44.9 0.7 copy-done.15
  45.7 15.0 %edge_part_0.1.refs_0_ = f32[512,128]{1,0:T(8,128)} custom-call(s32[256,128]{1,0:T(8,128)} %bitcast.9, bf16[8,32768]{1,0:T(8,128)(2,1)} %basis_hbm.3, bf16[1024,128]{1,0:T(8,128)(2,1)} %features_hbm.5, bf16[128,128]{1,0:T(8,128)(2,1)} %recv_hbm.3, bf16[8,128]{1,0:T(8,128)(2,1)} %wb_hbm.3, bf16[128,128]{1,0:T(8,128)(2,1)} %wo_hbm.3, ...), custom_call_target="tpu_custom_call" | custom-call | flops 8000000000 | bytes 4000000 | tf_op jit(solution)/shard_map/edge_part_0/pallas_call | solution.py:445
  60.7 1.2 %filter_rows.1.refs_7_ = bf16[32,8,1152]{2,1,0:T(8,128)(2,1)} custom-call(f32[8,8,1152]{2,1,0:T(8,128)S(1)} %all-to-all-done.1.sums_ref, f32[72,128]{1,0:T(8,128)S(1)} %fusion.weight_ref, f32[128,128]{1,0:T(8,128)S(1)} %copy-done.11), custom_call_target="tpu_custom_call" | custom-call | tf_op jit(solution)/shard_map/filter_rows/pallas_call | solution.py:289
  61.9 8.7 %all-to-all-start.2 = ((bf16[32,8,1152]{2,1,0:T(8,128)(2,1)}), bf16[32,8,1152]{2,1,0:T(8,128)(2,1)S(1)}, u32[]{:S(2)}, u32[]{:S(2)}) async-start(bf16[32,8,1152]{2,1,0:T(8,128)(2,1)} %filter_rows.1.refs_7_), calls=%async_computation.2 | async-start | bytes 1179648 | tf_op jit(solution)/shard_map/all_to_all | solution.py:599
  70.7 15.0 %edge_part_1.1.refs_1_ = f32[512,128]{1,0:T(8,128)} custom-call(s32[256,128]{1,0:T(8,128)} %bitcast.10, bf16[8,32768]{1,0:T(8,128)(2,1)} %basis_hbm.3, bf16[1024,128]{1,0:T(8,128)(2,1)} %features_hbm.5, bf16[128,128]{1,0:T(8,128)(2,1)} %recv_hbm.3, bf16[8,128]{1,0:T(8,128)(2,1)} %wb_hbm.3, bf16[128,128]{1,0:T(8,128)(2,1)} %wo_hbm.3, ...), custom_call_target="tpu_custom_call" | custom-call | flops 8000000000 | bytes 4000000 | tf_op jit(solution)/shard_map/edge_part_1/pallas_call | solution.py:445
  85.7 0.9 %copy-done.6 = f32[512,128]{1,0:T(8,128)S(1)} copy-done((f32[512,128]{1,0:T(8,128)S(1)}, f32[512,128]{1,0:T(8,128)}, u32[]{:S(2)}) %copy-start.6) | copy-done | bytes 262168
  86.7 3.1 %updated_rows.1 = f32[1024,128]{1,0:T(8,128)} custom-call(s32[1]{0:T(128)S(6)} %copy.15.count_ref, f32[88,2]{1,0:T(8,128)S(1)} %copy-done.8, f32[3,1024]{1,0:T(4,128)S(1)} %copy-done.10, bf16[256,1152]{1,0:T(8,128)(2,1)S(1)} %bitcast.7, f32[512,128]{1,0:T(8,128)S(1)} %copy-done.5, f32[512,128]{1,0:T(8,128)S(1)} %copy-done.6), custom_call_target="tpu_custom_call" | custom-call | tf_op jit(solution)/shard_map/updated_rows/pallas_call | solution.py:511
  (43 shorter events, 0.6 us)
Async XLA Ops:
  0.0 33.0 %copy-start = (f32[2048,128]{1,0:T(8,128)S(1)}, f32[2048,128]{1,0:T(8,128)}, u32[]{:S(2)}) copy-start(f32[2048,128]{1,0:T(8,128)} %param.18) | copy-start | bytes 3145732
  0.7 1.0 %copy-start.7 = (bf16[1024,128]{1,0:T(8,128)(2,1)S(1)}, bf16[1024,128]{1,0:T(8,128)(2,1)}, u32[]{:S(2)}) copy-start(bf16[1024,128]{1,0:T(8,128)(2,1)} %features_hbm.5) | copy-start | bytes 786436
  2.4 4.8 %copy-start.12 = (bf16[128,128]{1,0:T(8,128)(2,1)S(1)}, bf16[128,128]{1,0:T(8,128)(2,1)}, u32[]{:S(2)}) copy-start(bf16[128,128]{1,0:T(8,128)(2,1)} %send_ref.1) | copy-start | bytes 98308
  2.6 11.8 %copy-start.8 = (f32[88,2]{1,0:T(8,128)S(1)}, f32[88,2]{1,0:T(8,128)}, u32[]{:S(2)}) copy-start(f32[88,2]{1,0:T(8,128)} %constant.61.clone.xy_hbm) | copy-start | bytes 2116
  2.6 4.6 %collective-permute-start = (bf16[1216,128]{1,0:T(8,128)(2,1)S(1)}, bf16[1216,128]{1,0:T(8,128)(2,1)S(1)}, u32[]{:S(2)}, u32[]{:S(2)}) collective-permute-start(bf16[1216,128]{1,0:T(8,128)(2,1)S(1)} %prepare_rows.1.packed_any.packed_ref), channel_id=1, source_target_pairs={{0,8},{1,9},{2,10},{3,11},{4,12},{5,13},{6,14},{7,15},{8,0},{9,1},... | collective-permute-start | bytes 933896 | tf_op jit(solution)/shard_map/ppermute | solution.py:553
  7.4 23.3 %copy-start.1 = (bf16[1024,128]{1,0:T(8,128)(2,1)}, bf16[1024,128]{1,0:T(8,128)(2,1)S(1)}, u32[]{:S(2)}) copy-start(bf16[1024,128]{1,0:T(8,128)(2,1)S(1)} %project_rows.1.own_ref.refs_0_) | copy-start | bytes 786436
  7.4 16.4 %collective-permute-start.1 = (bf16[1024,128]{1,0:T(8,128)(2,1)S(1)}, bf16[1024,128]{1,0:T(8,128)(2,1)S(1)}, u32[]{:S(2)}, u32[]{:S(2)}) collective-permute-start(bf16[1024,128]{1,0:T(8,128)(2,1)S(1)} %project_rows.1.own_ref.refs_0_), channel_id=1, source_target_pairs={{0,1},{1,0},{2,3},{3,2},{4,5},{5,4},{6,7},{7,6},{8,9},{9,8},{10,11... | collective-permute-start | bytes 786440 | tf_op jit(solution)/shard_map/ppermute | solution.py:553
  8.7 15.2 %collective-permute-start.2 = (bf16[1024,128]{1,0:T(8,128)(2,1)S(1)}, bf16[1024,128]{1,0:T(8,128)(2,1)S(1)}, u32[]{:S(2)}, u32[]{:S(2)}) collective-permute-start(bf16[1024,128]{1,0:T(8,128)(2,1)S(1)} %project_rows.1.own_ref.refs_0_), channel_id=1, source_target_pairs={{0,7},{1,2},{2,1},{3,4},{4,3},{5,6},{6,5},{7,0},{8,15},{9,10},{10,... | collective-permute-start | bytes 786440 | tf_op jit(solution)/shard_map/ppermute | solution.py:553
  11.0 17.7 %collective-permute-start.3 = (bf16[1024,128]{1,0:T(8,128)(2,1)S(1)}, bf16[1024,128]{1,0:T(8,128)(2,1)S(1)}, u32[]{:S(2)}, u32[]{:S(2)}) collective-permute-start(bf16[1024,128]{1,0:T(8,128)(2,1)S(1)} %project_rows.1.own_ref.refs_0_), channel_id=1, source_target_pairs={{0,255},{1,250},{2,249},{3,252},{4,251},{5,254},{6,253},{7,248},{8... | collective-permute-start | bytes 786440 | tf_op jit(solution)/shard_map/ppermute | solution.py:553
  18.9 14.7 %all-to-all-start = ((f32[16,8,1152]{2,1,0:T(8,128)}), f32[16,8,1152]{2,1,0:T(8,128)S(1)}, u32[]{:S(2)}, u32[]{:S(2)}) async-start(f32[16,8,1152]{2,1,0:T(8,128)} %bitcast), calls=%async_computation | async-start | bytes 1179648 | tf_op jit(solution)/shard_map/all_to_all | solution.py:599
  23.8 5.6 %copy-start.13 = (s32[3,2048]{1,0:T(4,128)S(1)}, s32[3,2048]{1,0:T(4,128)}, u32[]{:S(2)}) copy-start(s32[3,2048]{1,0:T(4,128)} %param.17) | copy-start | bytes 73732
  23.8 4.9 %copy-start.2 = (bf16[1024,128]{1,0:T(8,128)(2,1)}, bf16[1024,128]{1,0:T(8,128)(2,1)S(1)}, u32[]{:S(2)}) copy-start(bf16[1024,128]{1,0:T(8,128)(2,1)S(1)} %collective-permute-done.1.near_ref.refs_1_) | copy-start | bytes 786436
  23.8 4.9 %copy-start.3 = (bf16[1024,128]{1,0:T(8,128)(2,1)}, bf16[1024,128]{1,0:T(8,128)(2,1)S(1)}, u32[]{:S(2)}) copy-start(bf16[1024,128]{1,0:T(8,128)(2,1)S(1)} %collective-permute-done.2.beyond_ref.refs_2_) | copy-start | bytes 786436
  29.4 15.5 %collective-permute-start.4 = (bf16[3072,128]{1,0:T(8,128)(2,1)S(1)}, bf16[3072,128]{1,0:T(8,128)(2,1)}, u32[]{:S(2)}, u32[]{:S(2)}) collective-permute-start(bf16[3072,128]{1,0:T(8,128)(2,1)S(1)} %column_rows.1), channel_id=1, source_target_pairs={{0,8},{1,9},{2,10},{3,11},{4,12},{5,13},{6,14},{7,15},{8,0},{9,1},... | collective-permute-start | bytes 2359304 | tf_op jit(solution)/shard_map/ppermute | solution.py:553
  29.4 3.4 %copy-start.14 = (s32[9,256]{1,0:T(8,128)S(1)}, s32[9,256]{1,0:T(8,128)}, u32[]{:S(2)}) copy-start(s32[9,256]{1,0:T(8,128)} %constant.62.clone) | copy-start | bytes 27652
  29.5 15.4 %collective-permute-start.5 = (bf16[1024,128]{1,0:T(8,128)(2,1)S(1)}, bf16[1024,128]{1,0:T(8,128)(2,1)S(1)}, u32[]{:S(2)}, u32[]{:S(2)}) collective-permute-start(bf16[1024,128]{1,0:T(8,128)(2,1)S(1)} %project_rows.1.own_ref.refs_0_), channel_id=1, source_target_pairs={{0,248},{1,249},{2,250},{3,251},{4,252},{5,253},{6,254},{7,255},{8... | collective-permute-start | bytes 786440 | tf_op jit(solution)/shard_map/ppermute | solution.py:553
  30.7 14.2 %collective-permute-start.6 = (bf16[1024,128]{1,0:T(8,128)(2,1)S(1)}, bf16[1024,128]{1,0:T(8,128)(2,1)S(1)}, u32[]{:S(2)}, u32[]{:S(2)}) collective-permute-start(bf16[1024,128]{1,0:T(8,128)(2,1)S(1)} %project_rows.1.own_ref.refs_0_), channel_id=1, source_target_pairs={{0,249},{1,248},{2,251},{3,250},{4,253},{5,252},{6,255},{7,254},{8... | collective-permute-start | bytes 786440 | tf_op jit(solution)/shard_map/ppermute | solution.py:553
  34.4 26.3 %all-to-all-start.1 = ((f32[8,8,1152]{2,1,0:T(8,128)}), f32[8,8,1152]{2,1,0:T(8,128)S(1)}, u32[]{:S(2)}, u32[]{:S(2)}) async-start(f32[8,8,1152]{2,1,0:T(8,128)} %stage_sums.1.refs_7_), calls=%async_computation.1 | async-start | bytes 589824 | tf_op jit(solution)/shard_map/all_to_all | solution.py:599
  44.9 0.8 copy-start.16
  45.7 15.0 %copy-start.11 = (f32[128,128]{1,0:T(8,128)S(1)}, f32[128,128]{1,0:T(8,128)}, u32[]{:S(2)}) copy-start(f32[128,128]{1,0:T(8,128)} %mix_hbm.1) | copy-start | bytes 196612
  61.9 23.8 %all-to-all-start.2 = ((bf16[32,8,1152]{2,1,0:T(8,128)(2,1)}), bf16[32,8,1152]{2,1,0:T(8,128)(2,1)S(1)}, u32[]{:S(2)}, u32[]{:S(2)}) async-start(bf16[32,8,1152]{2,1,0:T(8,128)(2,1)} %filter_rows.1.refs_7_), calls=%async_computation.2 | async-start | bytes 1179648 | tf_op jit(solution)/shard_map/all_to_all | solution.py:599
  70.7 15.0 %copy-start.5 = (f32[512,128]{1,0:T(8,128)S(1)}, f32[512,128]{1,0:T(8,128)}, u32[]{:S(2)}) copy-start(f32[512,128]{1,0:T(8,128)} %edge_part_0.1.refs_0_) | copy-start | bytes 786436
  70.7 15.0 %copy-start.10 = (f32[3,1024]{1,0:T(4,128)S(1)}, f32[3,1024]{1,0:T(4,128)}, u32[]{:S(2)}) copy-start(f32[3,1024]{1,0:T(4,128)} %pos_hbm.3) | copy-start | bytes 36868
  85.7 1.0 %copy-start.6 = (f32[512,128]{1,0:T(8,128)S(1)}, f32[512,128]{1,0:T(8,128)}, u32[]{:S(2)}) copy-start(f32[512,128]{1,0:T(8,128)} %edge_part_1.1.refs_1_) | copy-start | bytes 786436
  (3 other events, 2.1 us)

commit v7 on v6

--- a/solution.py
+++ b/solution.py
@@ -308,7 +308,7 @@
 
 
 def edge_kernel(
-    degree, first, ids_hbm, basis_hbm, features_hbm, recv_hbm, wb_hbm, wo_hbm, *refs
+    degree, first, count_ref, ids_hbm, basis_hbm, features_hbm, recv_hbm, wb_hbm, wo_hbm, *refs
 ):
     blocks, refs = refs[:7], refs[7:]
     (after_ref, out_ref, pool_ref, radial_ref, part_ref, own_ref, wide_ref), refs = refs[:7], refs[7:]
@@ -333,6 +333,7 @@
     edges = UNROLL * degree
     lines = edges // 128
     chunks = atoms // UNROLL
+    live = jnp.clip(count_ref[0] - first, 0, atoms)
 
     def fetch(chunk, at):
         source = ids_ref.at[pl.ds(chunk * lines, lines), :]
@@ -382,7 +383,8 @@
                 radial_ref[pl.ds(base + 128, 128), :] = half[:, channels:]
         return carry
 
-    lax.fori_loop(0, atoms * degree // span // 4, radial_block, 0)
+    step_atoms = 4 * span // degree
+    lax.fori_loop(0, lax.div(live + (step_atoms - 1), step_atoms), radial_block, 0)
     rows = blocks[0].shape[0]
     at = 0
     for copy, block in zip(landing, held):
@@ -423,7 +425,8 @@
             fetch(jnp.minimum(chunk + BUFFERS, chunks - 1), at).start()
         return carry
 
-    lax.fori_loop(0, chunks // BUFFERS, round_of_chunks, 0)
+    round_atoms = UNROLL * BUFFERS
+    lax.fori_loop(0, lax.div(live + (round_atoms - 1), round_atoms), round_of_chunks, 0)
     for at in range(BUFFERS):
         fetch(chunks - 1, at).wait()
     summed = part_ref[pl.ds(0, atoms, stride=8), :]
@@ -437,14 +440,16 @@
     out_ref[...] = message * (1.0 / math.sqrt(degree))
 
 
-def edge_call(part, after, senders, edge_basis, features, w_recv, w_basis, w_out, blocks):
+def edge_call(part, after, atom_count, senders, edge_basis, features, w_recv, w_basis, w_out, blocks):
     channels = features.shape[1]
     degree = senders.shape[0] // features.shape[0]
     atoms, first = PARTS[part], sum(PARTS[:part])
     rows = sum(block.shape[0] for block in blocks)
     return pl.pallas_call(
         functools.partial(edge_kernel, degree, first),
-        in_specs=[hbm()] * 6 + [pl.BlockSpec(memory_space=pl.ANY)] * (len(blocks) + 1),
+        in_specs=[pl.BlockSpec(memory_space=pltpu.SMEM)]
+        + [hbm()] * 6
+        + [pl.BlockSpec(memory_space=pl.ANY)] * (len(blocks) + 1),
         out_specs=vmem(),
         out_shape=jax.ShapeDtypeStruct((atoms, channels), jnp.float32),
         scratch_shapes=[
@@ -470,7 +475,7 @@
         ),
         name="edge_part_%d" % part,
     )(
-        senders.reshape(-1, 128), edge_basis, features, w_recv, w_basis, w_out, *blocks, after
+        atom_count, senders.reshape(-1, 128), edge_basis, features, w_recv, w_basis, w_out, *blocks, after
     )
 
 
@@ -634,7 +639,7 @@
 
     after = [stage_one, filtered]
     parts = [
-        edge_call(p, after[p], senders, edge_basis, features, w_recv, w_basis, w_out, blocks)
+        edge_call(p, after[p], atom_count, senders, edge_basis, features, w_recv, w_basis, w_out, blocks)
         for p in range(len(PARTS))
     ]
     return final_call(atom_count, positions, factors, parts, 4.0 / math.sqrt(total_k))

time: 90.5 us -> 89.8 us (level)
  the two profiles are of different devices: /device:TPU:1 before, /device:TPU:10 now
where the time goes in v7:
time: 89.8 us; the launch traced here: 88.9 us
  Pallas kernels  40 us (45%)
  starting transfers between devices  38 us (42%)
  waiting for transfers between devices  4.63 us (5%)
  local copies, waits for them, and re-layouts  4.36 us (5%)
  between operations  1.23 us (1%)
    all_to_all x3, starting transfers between devices, exchanged(): lax.all_to_all(array, ('slab', 'sub'), 0, 0, axis_index_groups=groups, ti...  30.2 us
    pallas_call x2, Pallas kernels, edge_call(): pl.pallas_call(functools.partial(edge_kernel, degree, first), in_specs=[p...  30 us
    ppermute x7, starting transfers between devices, moved(): return lax.ppermute(array, ('slab', 'sub'), pairs)  7.8 us
    pallas_call x1, Pallas kernels, factor_call(): pl.pallas_call(factor_kernel, in_specs=[hbm(), anywhere, anywhere], out_s...  4.5 us
    unnamed x34, local copies, waits for them, and re-layouts  4.2 us
    pallas_call x1, Pallas kernels, final_call(): pl.pallas_call(functools.partial(final_kernel, scale), in_specs=[pl.Block...  3.11 us
    all_to_all x3, waiting for transfers between devices, exchanged(): lax.all_to_all(array, ('slab', 'sub'), 0, 0, axis_index_groups=groups, ti...  3.02 us
  transfers between devices with their start and end apart: 10, of which 2 were waited for; matrix products, arithmetic and copies ran while one was open for 1% of the time, Pallas kernels for 40%

profile of v7, /device:TPU:10, one launch (start us, length us, event | category | flops | bytes accessed | tf_op | source)
XLA Modules:
  0.0 88.9 jit_solution(17806104262683894686)
XLA Ops:
  0.8 0.9 %copy-done.7 = bf16[1024,128]{1,0:T(8,128)(2,1)S(1)} copy-done((bf16[1024,128]{1,0:T(8,128)(2,1)S(1)}, bf16[1024,128]{1,0:T(8,128)(2,1)}, u32[]{:S(2)}) %copy-start.7) | copy-done | bytes 262168
  1.7 0.7 copy-done.9
  2.4 0.2 prepare_rows.1.packed_any.packed_ref
  2.7 1.6 %collective-permute-done.other_any.after_ref = bf16[1216,128]{1,0:T(8,128)(2,1)S(1)} collective-permute-done((bf16[1216,128]{1,0:T(8,128)(2,1)S(1)}, bf16[1216,128]{1,0:T(8,128)(2,1)S(1)}, u32[]{:S(2)}, u32[]{:S(2)}) %collective-permute-start) | collective-permute-done | bytes 311328 | tf_op jit(solution)/shard_map/ppermute | solution.py:558
  4.3 0.2 project_rows.1.own_ref.refs_0_
  4.6 2.4 %collective-permute-start.1 = (bf16[1024,128]{1,0:T(8,128)(2,1)S(1)}, bf16[1024,128]{1,0:T(8,128)(2,1)S(1)}, u32[]{:S(2)}, u32[]{:S(2)}) collective-permute-start(bf16[1024,128]{1,0:T(8,128)(2,1)S(1)} %project_rows.1.own_ref.refs_0_), channel_id=1, source_target_pairs={{0,1},{1,0},{2,3},{3,2},{4,5},{5,4},{6,7},{7,6},{8,9},{9,8},{10,11... | collective-permute-start | bytes 786440 | tf_op jit(solution)/shard_map/ppermute | solution.py:558
  6.9 1.2 %collective-permute-start.2 = (bf16[1024,128]{1,0:T(8,128)(2,1)S(1)}, bf16[1024,128]{1,0:T(8,128)(2,1)S(1)}, u32[]{:S(2)}, u32[]{:S(2)}) collective-permute-start(bf16[1024,128]{1,0:T(8,128)(2,1)S(1)} %project_rows.1.own_ref.refs_0_), channel_id=1, source_target_pairs={{0,7},{1,2},{2,1},{3,4},{4,3},{5,6},{6,5},{7,0},{8,15},{9,10},{10,... | collective-permute-start | bytes 786440 | tf_op jit(solution)/shard_map/ppermute | solution.py:558
  8.1 1.7 %collective-permute-start.3 = (bf16[1024,128]{1,0:T(8,128)(2,1)S(1)}, bf16[1024,128]{1,0:T(8,128)(2,1)S(1)}, u32[]{:S(2)}, u32[]{:S(2)}) collective-permute-start(bf16[1024,128]{1,0:T(8,128)(2,1)S(1)} %project_rows.1.own_ref.refs_0_), channel_id=1, source_target_pairs={{0,255},{1,250},{2,249},{3,252},{4,251},{5,254},{6,253},{7,248},{8... | collective-permute-start | bytes 786440 | tf_op jit(solution)/shard_map/ppermute | solution.py:558
  9.8 4.5 %factor_sums.1 = f32[128,1152]{1,0:T(8,128)} custom-call(f32[88,2]{1,0:T(8,128)S(1)} %copy-done.8, bf16[1216,128]{1,0:T(8,128)(2,1)S(1)} %prepare_rows.1.packed_any.packed_ref, bf16[1216,128]{1,0:T(8,128)(2,1)S(1)} %collective-permute-done.other_any.after_ref), custom_call_target="tpu_custom_call" | custom-call | tf_op jit(solution)/shard_map/factor_sums/pallas_call | solution.py:228
  14.3 12.5 %all-to-all-start = ((f32[16,8,1152]{2,1,0:T(8,128)}), f32[16,8,1152]{2,1,0:T(8,128)S(1)}, u32[]{:S(2)}, u32[]{:S(2)}) async-start(f32[16,8,1152]{2,1,0:T(8,128)} %bitcast), calls=%async_computation | async-start | bytes 1179648 | tf_op jit(solution)/shard_map/all_to_all | solution.py:604
  27.0 0.6 copy-done.2
  27.9 0.8 collective-permute-start.5
  28.6 1.7 %collective-permute-start.6 = (bf16[1024,128]{1,0:T(8,128)(2,1)S(1)}, bf16[1024,128]{1,0:T(8,128)(2,1)S(1)}, u32[]{:S(2)}, u32[]{:S(2)}) collective-permute-start(bf16[1024,128]{1,0:T(8,128)(2,1)S(1)} %project_rows.1.own_ref.refs_0_), channel_id=1, source_target_pairs={{0,249},{1,248},{2,251},{3,250},{4,253},{5,252},{6,255},{7,254},{8... | collective-permute-start | bytes 786440 | tf_op jit(solution)/shard_map/ppermute | solution.py:558
  30.5 0.6 fusion.weight_ref
  31.1 3.0 %all-to-all-done = f32[16,8,1152]{2,1,0:T(8,128)S(1)} async-done(((f32[16,8,1152]{2,1,0:T(8,128)}), f32[16,8,1152]{2,1,0:T(8,128)S(1)}, u32[]{:S(2)}, u32[]{:S(2)}) %all-to-all-start) | async-done | bytes 589856 | tf_op jit(solution)/shard_map/all_to_all | solution.py:604
  34.1 0.8 stage_sums.1.refs_7_
  34.8 9.2 %all-to-all-start.1 = ((f32[8,8,1152]{2,1,0:T(8,128)}), f32[8,8,1152]{2,1,0:T(8,128)S(1)}, u32[]{:S(2)}, u32[]{:S(2)}) async-start(f32[8,8,1152]{2,1,0:T(8,128)} %stage_sums.1.refs_7_), calls=%async_computation.1 | async-start | bytes 589824 | tf_op jit(solution)/shard_map/all_to_all | solution.py:604
  44.1 0.7 copy-done.15
  44.8 15.0 %edge_part_0.1.refs_0_ = f32[512,128]{1,0:T(8,128)} custom-call(s32[1]{0:T(128)S(6)} %copy.15.count_ref, s32[256,128]{1,0:T(8,128)} %bitcast.9, bf16[8,32768]{1,0:T(8,128)(2,1)} %basis_hbm.3, bf16[1024,128]{1,0:T(8,128)(2,1)} %features_hbm.5, bf16[128,128]{1,0:T(8,128)(2,1)} %recv_hbm.3, bf16[8,128]{1,0:T(8,128)(2,1)} %wb_hbm.3, bf16[128,128]{1,0:T(8,128)(2,1)} %wo_hbm.3, ...), custom_call_target="tpu_custom_call" | custom-call | flops 8000000000 | bytes 4000000 | tf_op jit(solution)/shard_map/edge_part_0/pallas_call | solution.py:448
  59.9 1.2 %filter_rows.1.refs_7_ = bf16[32,8,1152]{2,1,0:T(8,128)(2,1)} custom-call(f32[8,8,1152]{2,1,0:T(8,128)S(1)} %all-to-all-done.1.sums_ref, f32[72,128]{1,0:T(8,128)S(1)} %fusion.weight_ref, f32[128,128]{1,0:T(8,128)S(1)} %copy-done.11), custom_call_target="tpu_custom_call" | custom-call | tf_op jit(solution)/shard_map/filter_rows/pallas_call | solution.py:289
  61.1 8.5 %all-to-all-start.2 = ((bf16[32,8,1152]{2,1,0:T(8,128)(2,1)}), bf16[32,8,1152]{2,1,0:T(8,128)(2,1)S(1)}, u32[]{:S(2)}, u32[]{:S(2)}) async-start(bf16[32,8,1152]{2,1,0:T(8,128)(2,1)} %filter_rows.1.refs_7_), calls=%async_computation.2 | async-start | bytes 1179648 | tf_op jit(solution)/shard_map/all_to_all | solution.py:604
  69.6 15.0 %edge_part_1.1.refs_1_ = f32[512,128]{1,0:T(8,128)} custom-call(s32[1]{0:T(128)S(6)} %copy.15.count_ref, s32[256,128]{1,0:T(8,128)} %bitcast.10, bf16[8,32768]{1,0:T(8,128)(2,1)} %basis_hbm.3, bf16[1024,128]{1,0:T(8,128)(2,1)} %features_hbm.5, bf16[128,128]{1,0:T(8,128)(2,1)} %recv_hbm.3, bf16[8,128]{1,0:T(8,128)(2,1)} %wb_hbm.3, bf16[128,128]{1,0:T(8,128)(2,1)} %wo_hbm.3, ...), custom_call_target="tpu_custom_call" | custom-call | flops 8000000000 | bytes 4000000 | tf_op jit(solution)/shard_map/edge_part_1/pallas_call | solution.py:448
  84.7 0.9 %copy-done.6 = f32[512,128]{1,0:T(8,128)S(1)} copy-done((f32[512,128]{1,0:T(8,128)S(1)}, f32[512,128]{1,0:T(8,128)}, u32[]{:S(2)}) %copy-start.6) | copy-done | bytes 262168
  85.6 3.1 %updated_rows.1 = f32[1024,128]{1,0:T(8,128)} custom-call(s32[1]{0:T(128)S(6)} %copy.15.count_ref, f32[88,2]{1,0:T(8,128)S(1)} %copy-done.8, f32[3,1024]{1,0:T(4,128)S(1)} %copy-done.10, bf16[256,1152]{1,0:T(8,128)(2,1)S(1)} %bitcast.7, f32[512,128]{1,0:T(8,128)S(1)} %copy-done.5, f32[512,128]{1,0:T(8,128)S(1)} %copy-done.6), custom_call_target="tpu_custom_call" | custom-call | tf_op jit(solution)/shard_map/updated_rows/pallas_call | solution.py:516
  (43 shorter events, 0.7 us)
Async XLA Ops:
  0.0 30.5 %copy-start = (f32[2048,128]{1,0:T(8,128)S(1)}, f32[2048,128]{1,0:T(8,128)}, u32[]{:S(2)}) copy-start(f32[2048,128]{1,0:T(8,128)} %param.18) | copy-start | bytes 3145732
  0.7 1.0 %copy-start.7 = (bf16[1024,128]{1,0:T(8,128)(2,1)S(1)}, bf16[1024,128]{1,0:T(8,128)(2,1)}, u32[]{:S(2)}) copy-start(bf16[1024,128]{1,0:T(8,128)(2,1)} %features_hbm.5) | copy-start | bytes 786436
  2.4 1.9 %copy-start.12 = (bf16[128,128]{1,0:T(8,128)(2,1)S(1)}, bf16[128,128]{1,0:T(8,128)(2,1)}, u32[]{:S(2)}) copy-start(bf16[128,128]{1,0:T(8,128)(2,1)} %send_ref.1) | copy-start | bytes 98308
  2.6 7.2 %copy-start.8 = (f32[88,2]{1,0:T(8,128)S(1)}, f32[88,2]{1,0:T(8,128)}, u32[]{:S(2)}) copy-start(f32[88,2]{1,0:T(8,128)} %constant.61.clone.xy_hbm) | copy-start | bytes 2116
  2.6 1.7 %collective-permute-start = (bf16[1216,128]{1,0:T(8,128)(2,1)S(1)}, bf16[1216,128]{1,0:T(8,128)(2,1)S(1)}, u32[]{:S(2)}, u32[]{:S(2)}) collective-permute-start(bf16[1216,128]{1,0:T(8,128)(2,1)S(1)} %prepare_rows.1.packed_any.packed_ref), channel_id=1, source_target_pairs={{0,8},{1,9},{2,10},{3,11},{4,12},{5,13},{6,14},{7,15},{8,0},{9,1},... | collective-permute-start | bytes 933896 | tf_op jit(solution)/shard_map/ppermute | solution.py:558
  4.5 24.1 %copy-start.1 = (bf16[1024,128]{1,0:T(8,128)(2,1)}, bf16[1024,128]{1,0:T(8,128)(2,1)S(1)}, u32[]{:S(2)}) copy-start(bf16[1024,128]{1,0:T(8,128)(2,1)S(1)} %project_rows.1.own_ref.refs_0_) | copy-start | bytes 786436
  4.6 22.3 %collective-permute-start.1 = (bf16[1024,128]{1,0:T(8,128)(2,1)S(1)}, bf16[1024,128]{1,0:T(8,128)(2,1)S(1)}, u32[]{:S(2)}, u32[]{:S(2)}) collective-permute-start(bf16[1024,128]{1,0:T(8,128)(2,1)S(1)} %project_rows.1.own_ref.refs_0_), channel_id=1, source_target_pairs={{0,1},{1,0},{2,3},{3,2},{4,5},{5,4},{6,7},{7,6},{8,9},{9,8},{10,11... | collective-permute-start | bytes 786440 | tf_op jit(solution)/shard_map/ppermute | solution.py:558
  6.9 19.9 %collective-permute-start.2 = (bf16[1024,128]{1,0:T(8,128)(2,1)S(1)}, bf16[1024,128]{1,0:T(8,128)(2,1)S(1)}, u32[]{:S(2)}, u32[]{:S(2)}) collective-permute-start(bf16[1024,128]{1,0:T(8,128)(2,1)S(1)} %project_rows.1.own_ref.refs_0_), channel_id=1, source_target_pairs={{0,7},{1,2},{2,1},{3,4},{4,3},{5,6},{6,5},{7,0},{8,15},{9,10},{10,... | collective-permute-start | bytes 786440 | tf_op jit(solution)/shard_map/ppermute | solution.py:558
  8.1 18.7 %collective-permute-start.3 = (bf16[1024,128]{1,0:T(8,128)(2,1)S(1)}, bf16[1024,128]{1,0:T(8,128)(2,1)S(1)}, u32[]{:S(2)}, u32[]{:S(2)}) collective-permute-start(bf16[1024,128]{1,0:T(8,128)(2,1)S(1)} %project_rows.1.own_ref.refs_0_), channel_id=1, source_target_pairs={{0,255},{1,250},{2,249},{3,252},{4,251},{5,254},{6,253},{7,248},{8... | collective-permute-start | bytes 786440 | tf_op jit(solution)/shard_map/ppermute | solution.py:558
  14.3 19.7 %all-to-all-start = ((f32[16,8,1152]{2,1,0:T(8,128)}), f32[16,8,1152]{2,1,0:T(8,128)S(1)}, u32[]{:S(2)}, u32[]{:S(2)}) async-start(f32[16,8,1152]{2,1,0:T(8,128)} %bitcast), calls=%async_computation | async-start | bytes 1179648 | tf_op jit(solution)/shard_map/all_to_all | solution.py:604
  26.8 0.9 %copy-start.13 = (s32[3,2048]{1,0:T(4,128)S(1)}, s32[3,2048]{1,0:T(4,128)}, u32[]{:S(2)}) copy-start(s32[3,2048]{1,0:T(4,128)} %param.17) | copy-start | bytes 73732
  26.9 0.8 copy-start.3
  26.9 0.9 copy-start.4
  27.7 16.3 %collective-permute-start.4 = (bf16[3072,128]{1,0:T(8,128)(2,1)S(1)}, bf16[3072,128]{1,0:T(8,128)(2,1)}, u32[]{:S(2)}, u32[]{:S(2)}) collective-permute-start(bf16[3072,128]{1,0:T(8,128)(2,1)S(1)} %column_rows.1), channel_id=1, source_target_pairs={{0,8},{1,9},{2,10},{3,11},{4,12},{5,13},{6,14},{7,15},{8,0},{9,1},... | collective-permute-start | bytes 2359304 | tf_op jit(solution)/shard_map/ppermute | solution.py:558
  27.8 2.5 %copy-start.14 = (s32[9,256]{1,0:T(8,128)S(1)}, s32[9,256]{1,0:T(8,128)}, u32[]{:S(2)}) copy-start(s32[9,256]{1,0:T(8,128)} %constant.62.clone) | copy-start | bytes 27652
  27.9 16.2 %collective-permute-start.5 = (bf16[1024,128]{1,0:T(8,128)(2,1)S(1)}, bf16[1024,128]{1,0:T(8,128)(2,1)S(1)}, u32[]{:S(2)}, u32[]{:S(2)}) collective-permute-start(bf16[1024,128]{1,0:T(8,128)(2,1)S(1)} %project_rows.1.own_ref.refs_0_), channel_id=1, source_target_pairs={{0,248},{1,249},{2,250},{3,251},{4,252},{5,253},{6,254},{7,255},{8... | collective-permute-start | bytes 786440 | tf_op jit(solution)/shard_map/ppermute | solution.py:558
  28.6 15.4 %collective-permute-start.6 = (bf16[1024,128]{1,0:T(8,128)(2,1)S(1)}, bf16[1024,128]{1,0:T(8,128)(2,1)S(1)}, u32[]{:S(2)}, u32[]{:S(2)}) collective-permute-start(bf16[1024,128]{1,0:T(8,128)(2,1)S(1)} %project_rows.1.own_ref.refs_0_), channel_id=1, source_target_pairs={{0,249},{1,248},{2,251},{3,250},{4,253},{5,252},{6,255},{7,254},{8... | collective-permute-start | bytes 786440 | tf_op jit(solution)/shard_map/ppermute | solution.py:558
  34.8 25.0 %all-to-all-start.1 = ((f32[8,8,1152]{2,1,0:T(8,128)}), f32[8,8,1152]{2,1,0:T(8,128)S(1)}, u32[]{:S(2)}, u32[]{:S(2)}) async-start(f32[8,8,1152]{2,1,0:T(8,128)} %stage_sums.1.refs_7_), calls=%async_computation.1 | async-start | bytes 589824 | tf_op jit(solution)/shard_map/all_to_all | solution.py:604
  44.1 0.8 copy-start.16
  44.8 15.0 %copy-start.11 = (f32[128,128]{1,0:T(8,128)S(1)}, f32[128,128]{1,0:T(8,128)}, u32[]{:S(2)}) copy-start(f32[128,128]{1,0:T(8,128)} %mix_hbm.1) | copy-start | bytes 196612
  61.1 23.5 %all-to-all-start.2 = ((bf16[32,8,1152]{2,1,0:T(8,128)(2,1)}), bf16[32,8,1152]{2,1,0:T(8,128)(2,1)S(1)}, u32[]{:S(2)}, u32[]{:S(2)}) async-start(bf16[32,8,1152]{2,1,0:T(8,128)(2,1)} %filter_rows.1.refs_7_), calls=%async_computation.2 | async-start | bytes 1179648 | tf_op jit(solution)/shard_map/all_to_all | solution.py:604
  69.6 15.1 %copy-start.5 = (f32[512,128]{1,0:T(8,128)S(1)}, f32[512,128]{1,0:T(8,128)}, u32[]{:S(2)}) copy-start(f32[512,128]{1,0:T(8,128)} %edge_part_0.1.refs_0_) | copy-start | bytes 786436
  69.6 15.1 %copy-start.10 = (f32[3,1024]{1,0:T(4,128)S(1)}, f32[3,1024]{1,0:T(4,128)}, u32[]{:S(2)}) copy-start(f32[3,1024]{1,0:T(4,128)} %pos_hbm.3) | copy-start | bytes 36868
  84.6 1.0 %copy-start.6 = (f32[512,128]{1,0:T(8,128)S(1)}, f32[512,128]{1,0:T(8,128)}, u32[]{:S(2)}) copy-start(f32[512,128]{1,0:T(8,128)} %edge_part_1.1.refs_1_) | copy-start | bytes 786436
  (3 other events, 2.2 us)
